TPU v7x, 512 devices: a whole 4x4x16 slice. The times are simulated.
512 devices in a mesh: dp: 4 (over y), row: 8 (over x, core), col: 16 (over z).
Axes of the slice: x: 4, y: 4, z: 16, core: 2. Of those that a mesh axis runs over, the one named last changes fastest.
Arguments:
- tokens: bfloat16 [512, 8192], P(('dp', 'col'), 'row'), may hold values from -6 to 6
- grad_out: bfloat16 [512, 8192], P(('dp', 'col'), 'row'), may hold values from -6 to 6
- gate_blocks: bfloat16 [8, 16, 44, 4096], P('row', 'col'), may hold values from -0.21875 to 0.21875
- up_blocks: bfloat16 [8, 16, 44, 4096], P('row', 'col'), may hold values from -0.21875 to 0.21875
- down_blocks: bfloat16 [8, 16, 44, 4096], P('row', 'col'), may hold values from -0.109375 to 0.109375
- block_index: int32 [3, 8, 16, 2, 44], P(None, 'row', 'col'), may hold values from 0 to 27, as said below
- block_count: int32 [3, 8, 16], P(None, 'row', 'col'), may hold values from 11 to 44, as said below
Outputs:
- mixed: bfloat16 [512, 8192], P(('dp', 'col'), 'row')
- tokens_grad: bfloat16 [512, 8192], P(('dp', 'col'), 'row')
- gate_grad: bfloat16 [8, 16, 44, 4096], P('row', 'col')
- up_grad: bfloat16 [8, 16, 44, 4096], P('row', 'col')
- down_grad: bfloat16 [8, 16, 44, 4096], P('row', 'col')
Inputs may be any that keep to these rules, and one draw needn't show every extreme that they name: block_index[m, r, c, 0, s] is a block row of the tile, below 16, and block_index[m, r, c, 1, s] a block column, below 28; the 44 slots of one list name distinct blocks. Slots s >= block_count[m, r, c] are not part of the matrix. Every draw has a list with exactly 44 live slots.
All inputs are finite; a program needn't handle non-finite values.
Results may differ from a plain program's by a relative error of at most 0.03.
Values may be sent and summed in bfloat16 or wider, within the bound.
No kernel may reach another device: no remote copies, remote signals or barrier semaphores. Data moves between devices by JAX's collectives and lax.ppermute only.
A program may use at most 64 MiB of HBM per device.

v0:
```python
import jax
import jax.numpy as jnp
from jax import lax
from jax.sharding import PartitionSpec as P

FF = 28672
BS = 64


def slot_view(band_rows, pick_ids, block_width):
    shaped = band_rows.reshape(band_rows.shape[0] // block_width, block_width, band_rows.shape[1])
    return jnp.take(shaped, pick_ids, axis=0)


def collect(products, places, count_out):
    summed = (
        jnp.zeros((count_out, products.shape[1], products.shape[2]), jnp.float32)
        .at[places]
        .add(products)
    )
    return summed.reshape(count_out * products.shape[1], products.shape[2])


def spread(blocks, source, pick_ids, places, count_out):
    slot_data = slot_view(source, pick_ids, blocks.shape[1])
    products = jnp.einsum("sdf,sdt->sft", blocks, slot_data, preferred_element_type=jnp.float32)
    return collect(products, places, count_out)


def fold_back(blocks, source, pick_ids, places, count_out):
    slot_data = slot_view(source, pick_ids, blocks.shape[1])
    products = jnp.einsum("sdf,sft->sdt", blocks, slot_data, preferred_element_type=jnp.float32)
    return collect(products, places, count_out)


def block_grad(left_band, left_ids, right_band, right_ids, live_mask, block_width):
    left_slot_list = slot_view(left_band, left_ids, block_width)
    right_slot_list = slot_view(right_band, right_ids, block_width)
    products = jnp.einsum(
        "sdt,sft->sdf", left_slot_list, right_slot_list, preferred_element_type=jnp.float32
    )
    return products * live_mask[:, None, None]


def per_device(tokens, grad_out, gate_blocks, up_blocks, down_blocks, block_index, block_count):
    slot_count = gate_blocks.shape[2]
    block_width = BS
    pick_ids = block_index.reshape(3, 2, slot_count)
    live_mask = (
        jnp.arange(slot_count, dtype=jnp.int32)[None, :] < block_count.reshape(3, 1)
    ).astype(jnp.float32)
    live_weight = live_mask.astype(jnp.bfloat16)
    gate_tile = (
        gate_blocks.reshape(slot_count, block_width, block_width) * live_weight[0][:, None, None]
    )
    up_tile = (
        up_blocks.reshape(slot_count, block_width, block_width) * live_weight[1][:, None, None]
    )
    down_tile = (
        down_blocks.reshape(slot_count, block_width, block_width) * live_weight[2][:, None, None]
    )
    tok_cols, grad_cols = (
        lax.all_gather(tokens.T, "col", axis=1, tiled=True),
        lax.all_gather(grad_out.T, "col", axis=1, tiled=True),
    )
    band_height = tok_cols.shape[0]
    tile_brows = band_height // block_width
    tile_bcols = FF // (block_width * lax.axis_size("col"))
    share_rows = tile_bcols * block_width // lax.axis_size("row")
    first_row = lax.axis_index("row") * share_rows
    gate_portion = spread(gate_tile, tok_cols, pick_ids[0, 0], pick_ids[0, 1], tile_bcols)
    up_part = spread(up_tile, tok_cols, pick_ids[1, 0], pick_ids[1, 1], tile_bcols)
    gate_full, up_full = (
        lax.psum(gate_portion.astype(jnp.bfloat16), "row").astype(jnp.float32),
        lax.psum(up_part.astype(jnp.bfloat16), "row").astype(jnp.float32),
    )
    hidden = (jax.nn.silu(gate_full) * up_full).astype(jnp.bfloat16)
    gate_own = lax.dynamic_slice_in_dim(gate_full, first_row, share_rows, 0)
    up_own = lax.dynamic_slice_in_dim(up_full, first_row, share_rows, 0)
    out_part = fold_back(down_tile, hidden, pick_ids[2, 1], pick_ids[2, 0], tile_brows)
    hgrad_part = spread(down_tile, grad_cols, pick_ids[2, 0], pick_ids[2, 1], tile_bcols)
    hgrad_own = lax.psum_scatter(
        hgrad_part.astype(jnp.bfloat16), "row", scatter_dimension=0, tiled=True
    ).astype(jnp.float32)
    gate_sigmoid = jax.nn.sigmoid(gate_own)
    up_grad_h = (hgrad_own * gate_own * gate_sigmoid).astype(jnp.bfloat16)
    gate_grad_h = (
        hgrad_own * up_own * gate_sigmoid * (1.0 + gate_own * (1.0 - gate_sigmoid))
    ).astype(jnp.bfloat16)
    gate_grad_all, up_grad_all = (
        lax.all_gather(gate_grad_h, "row", axis=0, tiled=True),
        lax.all_gather(up_grad_h, "row", axis=0, tiled=True),
    )
    in_part = fold_back(gate_tile, gate_grad_all, pick_ids[0, 1], pick_ids[0, 0], tile_brows)
    in_part = in_part + fold_back(up_tile, up_grad_all, pick_ids[1, 1], pick_ids[1, 0], tile_brows)
    grad_terms = (
        block_grad(
            tok_cols, pick_ids[0, 0], gate_grad_all, pick_ids[0, 1], live_mask[0], block_width
        ),
        block_grad(
            tok_cols, pick_ids[1, 0], up_grad_all, pick_ids[1, 1], live_mask[1], block_width
        ),
        block_grad(grad_cols, pick_ids[2, 0], hidden, pick_ids[2, 1], live_mask[2], block_width),
    )
    grad_sums = (
        lax.psum(grad_terms[0].astype(jnp.bfloat16), "dp").astype(jnp.float32),
        lax.psum(grad_terms[1].astype(jnp.bfloat16), "dp").astype(jnp.float32),
        lax.psum(grad_terms[2].astype(jnp.bfloat16), "dp").astype(jnp.float32),
    )
    out_rows, in_rows = (
        lax.psum_scatter(
            out_part.astype(jnp.bfloat16), "col", scatter_dimension=1, tiled=True
        ).astype(jnp.float32),
        lax.psum_scatter(
            in_part.astype(jnp.bfloat16), "col", scatter_dimension=1, tiled=True
        ).astype(jnp.float32),
    )
    mixed = out_rows.T.astype(jnp.bfloat16)
    tokens_grad = in_rows.T.astype(jnp.bfloat16)
    shape_out = (1, 1, slot_count, block_width * block_width)
    gate_grad = grad_sums[0].astype(jnp.bfloat16).reshape(shape_out)
    up_grad = grad_sums[1].astype(jnp.bfloat16).reshape(shape_out)
    down_grad = grad_sums[2].astype(jnp.bfloat16).reshape(shape_out)
    return (mixed, tokens_grad, gate_grad, up_grad, down_grad)


def solution(mesh):
    placed = (
        P(("dp", "col"), "row"),
        P(("dp", "col"), "row"),
        P("row", "col", None, None),
        P("row", "col", None, None),
        P("row", "col", None, None),
        P(None, "row", "col", None, None),
        P(None, "row", "col"),
    )
    return jax.shard_map(
        per_device,
        mesh=mesh,
        in_specs=placed,
        out_specs=(
            P(("dp", "col"), "row"),
            P(("dp", "col"), "row"),
            P("row", "col", None, None),
            P("row", "col", None, None),
            P("row", "col", None, None),
        ),
        check_vma=False,
    )
```

profile of v0, /device:TPU:1, one launch (start us, length us, event | category | flops | bytes accessed | tf_op | source)
XLA Modules:
  0.0 397.3 jit_solution(10989333229346332986)
XLA Ops:
  7.2 1.3 fusion.32
  8.5 1.4 compare_and_fusion
  9.9 0.7 fusion.26
  10.6 1.7 reshape.255
  12.4 30.7 %all_gather.12 = bf16[1024,128]{0,1:T(8,128)(2,1)S(1)} all-gather(bf16[1024,8]{0,1:T(8,128)(2,1)} %bitcast.91), channel_id=1, replica_groups=mesh['dp'=4,'row'=8,'col'=16] {'col'}, dimensions={1}, use_global_device_ids=true | all-gather | bytes 278528 | tf_op jit(solution)/shard_map/all_gather | solution.py:63
  43.0 0.2 copy.25
  43.2 0.7 gather_fusion.1
  43.9 1.6 fusion.5
  45.6 0.1 broadcast.113.clone
  45.7 5.4 %scatter_fusion.1 = f32[28,64,128]{2,1,0:T(8,128)S(1)} fusion(f32[28,64,128]{2,1,0:T(8,128)S(1)} %broadcast.113.clone, s32[44]{0:T(128)S(1)} %get-tuple-element.49, f32[44,64,128]{2,1,0:T(8,128)} %fusion.5), kind=kCustom, calls=%fused_computation.7 | custom fusion | flops 360448 | bytes 4325552 | tf_op jit(solution)/shard_map/scatter-add | solution.py:19
  51.1 0.9 convert_element_type.84
  51.9 0.2 copy-done.12
  52.1 0.8 reshape.253
  52.9 0.7 gather_fusion
  53.6 1.6 fusion.9
  55.2 0.1 broadcast.113.clone.1
  55.3 5.4 %scatter_fusion = f32[28,64,128]{2,1,0:T(8,128)S(1)} fusion(f32[28,64,128]{2,1,0:T(8,128)S(1)} %broadcast.113.clone.1, s32[44]{0:T(128)S(1)} %get-tuple-element.50, f32[44,64,128]{2,1,0:T(8,128)} %fusion.9), kind=kCustom, calls=%fused_computation.6 | custom fusion | flops 360448 | bytes 4325552 | tf_op jit(solution)/shard_map/scatter-add | solution.py:19
  60.7 0.8 convert_element_type.81
  61.6 0.0 reduce-scatter.8.cloned.1.call-start
  61.7 20.6 %all_gather.13 = bf16[1024,128]{0,1:T(8,128)(2,1)S(1)} all-gather(bf16[1024,8]{0,1:T(8,128)(2,1)S(1)} %bitcast.92), channel_id=1, replica_groups=mesh['dp'=4,'row'=8,'col'=16] {'col'}, dimensions={1}, use_global_device_ids=true | all-gather | bytes 278528 | tf_op jit(solution)/shard_map/all_gather | solution.py:64
  82.3 0.8 reshape.252
  83.1 0.3 copy.24
  83.5 0.2 copy.29
  83.6 0.1 copy-done.22
  83.8 0.7 gather_fusion.3
  84.5 1.5 fusion.11
  86.0 0.1 broadcast.113.clone.2
  86.1 5.4 %scatter_fusion.3 = f32[28,64,128]{2,1,0:T(8,128)S(1)} fusion(f32[28,64,128]{2,1,0:T(8,128)S(1)} %broadcast.113.clone.2, s32[44]{0:T(128)S(1)} %copy-done.19, f32[44,64,128]{2,1,0:T(8,128)} %fusion.11), kind=kCustom, calls=%fused_computation.9 | custom fusion | flops 360448 | bytes 4325552 | tf_op jit(solution)/shard_map/scatter-add | solution.py:19
  91.5 0.8 convert_element_type.91
  92.5 48.5 %all-reduce.5.cloned.1.call-done = (bf16[1792,128]{1,0:T(8,128)(2,1)}, bf16[1792,128]{1,0:T(8,128)(2,1)}) async-done(((bf16[1792,128]{1,0:T(8,128)(2,1)}, bf16[1792,128]{1,0:T(8,128)(2,1)}), (bf16[1792,128]{1,0:T(8,128)(2,1)}, bf16[1792,128]{1,0:T(8,128)(2,1)})) %all-reduce.5.cloned.1.call-update) | async-done | bytes 917520 | tf_op jit(solution)/shard_map/psum | solution.py:75
  141.1 2.1 convert_element_type.83
  143.2 1.0 convert_element_type.86
  144.2 0.3 multiply_convert_fusion
  144.5 0.7 gather_fusion.2
  145.2 1.6 fusion.13
  146.9 5.4 %scatter_fusion.2 = f32[16,64,128]{2,1,0:T(8,128)S(1)} fusion(f32[16,64,128]{2,1,0:T(8,128)S(1)} %broadcast.110.clone, s32[44]{0:T(128)S(1)} %copy-done.18, f32[44,64,128]{2,1,0:T(8,128)} %fusion.13), kind=kCustom, calls=%fused_computation.8 | custom fusion | flops 360448 | bytes 4325552 | tf_op jit(solution)/shard_map/scatter-add | solution.py:19
  152.3 0.7 convert_element_type.88
  153.0 1.8 copy.35
  154.8 1.5 fusion.2
  156.3 2.5 reshape.262
  158.9 23.1 %reduce-scatter.8.cloned.1.call-done = bf16[224,128]{1,0:T(8,128)(2,1)} async-done(((bf16[1792,128]{1,0:T(8,128)(2,1)}), bf16[224,128]{1,0:T(8,128)(2,1)}) %reduce-scatter.8.cloned.1.call-update) | async-done | bytes 57360 | tf_op jit(solution)/shard_map/reduce_scatter | solution.py:82
  182.0 1.1 fusion.25
  183.0 15.1 %all_gather.14 = bf16[1792,128]{1,0:T(8,128)(2,1)S(1)} all-gather(bf16[224,128]{1,0:T(8,128)(2,1)S(1)} %get-tuple-element.35), channel_id=1, replica_groups=mesh['dp'=4,'row'=8,'col'=16] {'row'}, dimensions={0}, use_global_device_ids=true | all-gather | bytes 516096 | tf_op jit(solution)/shard_map/all_gather | solution.py:91
  198.2 13.2 %all_gather.15 = bf16[1792,128]{1,0:T(8,128)(2,1)S(1)} all-gather(bf16[224,128]{1,0:T(8,128)(2,1)S(1)} %get-tuple-element.34), channel_id=1, replica_groups=mesh['dp'=4,'row'=8,'col'=16] {'row'}, dimensions={0}, use_global_device_ids=true | all-gather | bytes 516096 | tf_op jit(solution)/shard_map/all_gather | solution.py:92
  211.4 0.7 gather_fusion.4
  212.1 0.8 copy-done.8
  212.9 1.5 fusion.7
  214.5 1.5 gather_fusion.5
  216.1 3.1 scatter_fusion.4
  219.2 0.4 fusion.3
  219.7 0.2 copy-done.16
  219.8 3.1 scatter_fusion.5
  223.0 0.8 add_convert_fusion
  223.7 1.8 copy.37
  225.6 1.5 fusion
  227.1 2.5 reshape.260
  229.6 0.6 fusion.1
  230.2 1.3 reshape.261
  231.5 12.1 %reduce-scatter.10.cloned.1.call-done = bf16[8,1024]{1,0:T(8,128)(2,1)} async-done(((bf16[128,1024]{1,0:T(8,128)(2,1)}), bf16[8,1024]{1,0:T(8,128)(2,1)}) %reduce-scatter.10.cloned.1.call-update) | async-done | bytes 16400 | tf_op jit(solution)/shard_map/convert_element_type | solution.py:118
  243.6 69.5 %reduce-scatter.12.cloned.1.call-done = bf16[8,1024]{1,0:T(8,128)(2,1)} async-done(((bf16[128,1024]{1,0:T(8,128)(2,1)}), bf16[8,1024]{1,0:T(8,128)(2,1)}) %reduce-scatter.12.cloned.1.call-update) | async-done | bytes 16400 | tf_op jit(solution)/shard_map/convert_element_type | solution.py:119
  313.1 73.3 %all-reduce.7.cloned.1.call-done = (bf16[1,1,44,4096]{3,2,1,0:T(8,128)(2,1)}, bf16[1,1,44,4096]{3,2,1,0:T(8,128)(2,1)}, bf16[1,1,44,4096]{3,2,1,0:T(8,128)(2,1)}) async-done(((bf16[1,1,44,4096]{3,2,1,0:T(8,128)(2,1)}, bf16[1,1,44,4096]{3,2,1,0:T(8,128)(2,1)}, bf16[1,1,44,4096]{3,2,1,0:T(8,128)(2,1)}), (bf16[1,1,44,4096]{3,2,1,0:T(8,128)(2,1)}, bf16[1,1,44,4096]{3,2,1,0:T(8,128)(2,1)}, ...) | async-done | bytes 1081360 | tf_op jit(solution)/shard_map/psum | solution.py:106
  386.4 1.8 copy.52
  388.2 1.8 copy.53
  390.0 0.7 copy.54
  (78 shorter events, 0.5 us)
Async XLA Ops:
  7.2 133.9 %all-reduce.5.cloned.1.call-start = ((), (), s32[]{:S(2)}) async-start(), calls=%async_computation.6 | async-start | bytes 1835008 | tf_op jit(solution)/shard_map/psum | solution.py:75
  9.9 34.1 %copy-start.25 = (pred[44]{0:T(512)(128)(4,1)}, pred[44]{0:T(512)(128)(4,1)S(1)}, u32[]{:S(2)}) copy-start(pred[44]{0:T(512)(128)(4,1)S(1)} %get-tuple-element.42) | copy-start | bytes 136
  9.9 43.7 %copy-start.28 = (pred[44]{0:T(512)(128)(4,1)}, pred[44]{0:T(512)(128)(4,1)S(1)}, u32[]{:S(2)}) copy-start(pred[44]{0:T(512)(128)(4,1)S(1)} %get-tuple-element.44) | copy-start | bytes 136
  43.9 1.7 copy-start.1
  51.1 1.0 copy-start.12
  53.6 1.7 copy-start.3
  60.7 0.9 copy-start.15
  60.7 21.6 %copy-start.13 = (bf16[1,1,44,4096]{3,2,1,0:T(8,128)(2,1)S(1)}, bf16[1,1,44,4096]{3,2,1,0:T(8,128)(2,1)}, u32[]{:S(2)}) copy-start(bf16[1,1,44,4096]{3,2,1,0:T(8,128)(2,1)} %param.15) | copy-start | bytes 1081348
  61.6 120.4 %reduce-scatter.8.cloned.1.call-start = ((), (), s32[]{:S(2)}) async-start(), calls=%async_computation.3 | async-start | bytes 516096 | tf_op jit(solution)/shard_map/reduce_scatter | solution.py:82
  83.1 0.7 copy-start.22
  83.1 0.7 copy-start.23
  83.1 1.4 copy-start.30
  84.5 1.6 copy-start.5
  84.5 1.7 copy-start.19
  91.5 1.0 copy-start.21
  91.5 1.0 copy-start.20
  92.4 151.2 %reduce-scatter.10.cloned.1.call-start = ((), (), s32[]{:S(2)}) async-start(), calls=%async_computation.4 | async-start | bytes 278528 | tf_op jit(solution)/shard_map/convert_element_type | solution.py:118
  141.1 2.1 copy-start.10
  141.1 3.1 copy-start.11
  144.2 1.0 copy-start.31
  145.2 1.7 copy-start.18
  146.9 7.9 %copy-start.6 = (bf16[44,64,128]{2,1,0:T(8,128)(2,1)S(1)}, bf16[44,64,128]{2,1,0:T(8,128)(2,1)}, u32[]{:S(2)}) copy-start(bf16[44,64,128]{2,1,0:T(8,128)(2,1)} %copy-done.5) | copy-start | bytes 2162692
  158.8 54.1 %copy-start.27 = (pred[44]{0:T(512)(128)(4,1)S(1)}, pred[44]{0:T(512)(128)(4,1)}, u32[]{:S(2)}) copy-start(pred[44]{0:T(512)(128)(4,1)} %get-tuple-element.38) | copy-start | bytes 136
  158.8 154.3 %reduce-scatter.12.cloned.1.call-start = ((), (), s32[]{:S(2)}) async-start(), calls=%async_computation.5 | async-start | bytes 278528 | tf_op jit(solution)/shard_map/convert_element_type | solution.py:119
  212.1 0.9 copy-start.8
  214.4 1.6 copy-start
  214.4 1.6 copy-start.17
  216.1 3.1 copy-start.7
  216.1 3.1 copy-start.24
  219.2 0.7 copy-start.16
  222.9 2.7 copy-start.4
  222.9 2.7 copy-start.9
  222.9 2.7 copy-start.29
  225.5 160.9 %all-reduce.7.cloned.1.call-start = ((), (), s32[]{:S(2)}) async-start(), calls=%async_computation.7 | async-start | bytes 2359296 | tf_op jit(solution)/shard_map/psum | solution.py:106
  225.6 4.0 %copy-start.2 = (bf16[44,64,128]{2,1,0:T(8,128)(2,1)S(1)}, bf16[44,64,128]{2,1,0:T(8,128)(2,1)}, u32[]{:S(2)}) copy-start(bf16[44,64,128]{2,1,0:T(8,128)(2,1)} %copy-done.1) | copy-start | bytes 2162692
  225.6 4.0 %copy-start.26 = (pred[44]{0:T(512)(128)(4,1)S(1)}, pred[44]{0:T(512)(128)(4,1)}, u32[]{:S(2)}) copy-start(pred[44]{0:T(512)(128)(4,1)} %copy-done.25) | copy-start | bytes 136
  386.4 3.6 copy-start.14
Sparse Core Ops, SparseCore 0:
  61.7 79.3 all-reduce.4
  144.1 37.8 reduce-scatter.7
  185.4 58.2 reduce-scatter.9
  247.1 66.0 reduce-scatter.11
  316.1 70.2 all-reduce.6
where the time goes:
time: 399 us; the launch traced here: 397 us
  waiting for transfers between devices  227 us (57%)
  blocking collectives  79.7 us (20%)
  other arithmetic  39.5 us (10%)
  local copies, waits for them, and re-layouts  25 us (6%)
  between operations  14.4 us (4%)
  matrix products  11.9 us (3%)
    psum x1, waiting for transfers between devices, per_device(): lax.psum(grad_terms[0].astype(jnp.bfloat16), 'dp').astype(jnp.float32)  73.3 us
    convert_element_type x1, waiting for transfers between devices, per_device(): tokens_grad = in_rows.T.astype(jnp.bfloat16)  69.5 us
    psum x1, waiting for transfers between devices, per_device(): lax.psum(up_part.astype(jnp.bfloat16), 'row').astype(jnp.float32)  48.5 us
    all_gather x1, blocking collectives, per_device(): lax.all_gather(tokens.T, 'col', axis=1, tiled=True)  30.7 us
    scatter-add x6, other arithmetic, collect(): summed = jnp.zeros((count_out, products.shape[1], products.shape[2]), jnp...  27.6 us
    reduce_scatter x1, waiting for transfers between devices, per_device(): lax.psum_scatter(hgrad_part.astype(jnp.bfloat16), 'row', scatter_dimensio...  23.1 us
    all_gather x1, blocking collectives, per_device(): lax.all_gather(grad_out.T, 'col', axis=1, tiled=True)  20.6 us
    all_gather x1, blocking collectives, per_device(): lax.all_gather(gate_grad_h, 'row', axis=0, tiled=True)  15.1 us
  transfers between devices with their start and end apart: 5, of which 5 were waited for; matrix products, arithmetic and copies ran while one was open for 12% of the time, Pallas kernels for 0%

commit v1 on v0

v1 whole, which is shorter than its diff:
```python
import functools

import jax
import jax.numpy as jnp
from jax import lax
from jax.experimental import pallas as pl
from jax.experimental.pallas import tpu as pltpu
from jax.sharding import PartitionSpec as P

BS = 64
UNROLL = 4
VMEM = pl.BlockSpec(memory_space=pltpu.VMEM)
SMEM = pl.BlockSpec(memory_space=pltpu.SMEM)
PARAMS = pltpu.CompilerParams(vmem_limit_bytes=40 * 1024 * 1024)
F32 = jnp.float32
BF16 = jnp.bfloat16


def for_slots(count, step):
    def group(g, carry):
        for u in range(UNROLL):
            s = g * UNROLL + u
            step(s, s < count)
        return carry

    lax.fori_loop(0, (count + UNROLL - 1) // UNROLL, group, 0)


def rows_of(block):
    return pl.ds(pl.multiple_of(block * BS, BS), BS)


def spread_kernel(index, count, wide, gate, up, down, cols, parts, total):
    n_col, pair, width = wide.shape
    half = pair // 2
    toks = n_col * half
    for j in range(0, width, 128):
        piece = wide[:, :, j : j + 128].astype(F32).reshape(n_col, 2, half, 128)
        for side in range(2):
            cols[side, j : j + 128, :] = piece[:, side].reshape(toks, 128).T.astype(BF16)
    total[...] = jnp.zeros_like(total)
    for m, weights in enumerate((gate, up, down)):
        side = m // 2

        def step(s, live):
            block = jnp.where(live, weights[s], jnp.zeros_like(weights[s]))
            source = cols[side, rows_of(index[m, 0, s]), :]
            place = rows_of(index[m, 1, s])
            total[m, place, :] += lax.dot_general(
                block, source, (((0,), (0,)), ((), ())), preferred_element_type=F32
            )

        for_slots(count[m], step)
    share = parts.shape[2]
    for j in range(parts.shape[0]):
        for m in range(3):
            parts[j, m] = total[m, j * share : (j + 1) * share, :].astype(BF16)


def hidden_kernel(terms, out):
    sums = [terms[0, m].astype(F32) for m in range(3)]
    for j in range(1, terms.shape[0]):
        sums = [sums[m] + terms[j, m].astype(F32) for m in range(3)]
    gate, up, hgrad = sums
    sig = jax.nn.sigmoid(gate)
    out[0] = (hgrad * up * sig * (1.0 + gate * (1.0 - sig))).astype(BF16)
    out[1] = (hgrad * gate * sig).astype(BF16)
    out[2] = (gate * sig * up).astype(BF16)


def back_kernel(index, count, units, cols, gate, up, down, rows, grads, hidden, out_total, in_total):
    n_row, _, share, toks = units.shape
    for j in range(n_row):
        for m in range(3):
            hidden[m, j * share : (j + 1) * share, :] = units[j, m]
    out_total[...] = jnp.zeros_like(out_total)
    in_total[...] = jnp.zeros_like(in_total)
    grads[...] = jnp.zeros_like(grads)
    per = grads.shape[2]
    for m, weights in enumerate((gate, up, down)):
        side = m // 2
        total = out_total if m == 2 else in_total

        def step(s, live):
            block = jnp.where(live, weights[s], jnp.zeros_like(weights[s]))
            unit = hidden[m, rows_of(index[m, 1, s]), :]
            place = rows_of(index[m, 0, s])
            total[place, :] += jnp.dot(block, unit, preferred_element_type=F32)
            grad = lax.dot_general(
                cols[side, place, :], unit, (((1,), (1,)), ((), ())), preferred_element_type=F32
            )
            grad = jnp.where(live, grad, 0.0)
            packed = jnp.concatenate([grad[: BS // 2], grad[BS // 2 :]], axis=1)
            grads[s // per, m, s % per] = packed.astype(BF16)

        for_slots(count[m], step)
    n_col, pair, width = rows.shape
    half = pair // 2
    for j in range(0, width, 128):
        out_piece = out_total[j : j + 128, :].T.reshape(n_col, half, 128)
        in_piece = in_total[j : j + 128, :].T.reshape(n_col, half, 128)
        rows[:, :, j : j + 128] = jnp.concatenate([out_piece, in_piece], axis=1).astype(BF16)


def unpack_kernel(packed, gate, up, down, flat):
    n_dp, _, per, depth, lanes = packed.shape
    slots = n_dp * per
    low = lax.broadcasted_iota(jnp.int32, (slots, lanes), 1) < BS
    for m, out in enumerate((gate, up, down)):
        for g in range(n_dp):
            flat[g * per * depth : (g + 1) * per * depth, :] = (
                packed[g, m].astype(F32).reshape(per * depth, lanes)
            )
        for k in range(0, depth, 2):
            even = flat[pl.ds(k, slots, stride=depth), :]
            odd = flat[pl.ds(k + 1, slots, stride=depth), :]
            out[:, k * BS : k * BS + lanes] = jnp.where(low, even, pltpu.roll(odd, BS, 1)).astype(BF16)
            start = (depth + k) * BS
            out[:, start : start + lanes] = jnp.where(low, pltpu.roll(even, BS, 1), odd).astype(BF16)


def per_device(tokens, grad_out, gate_blocks, up_blocks, down_blocks, block_index, block_count):
    n_dp, n_row, n_col = (lax.axis_size(a) for a in ("dp", "row", "col"))
    slots = gate_blocks.shape[2]
    half, width = tokens.shape
    toks = half * n_col
    units = 28 * BS
    share = units // n_row
    index = block_index.reshape(3, 2, slots)
    count = block_count.reshape(3)
    weights = [w.reshape(slots, BS, BS) for w in (gate_blocks, up_blocks, down_blocks)]

    both = jnp.concatenate([tokens, grad_out], axis=0)
    wide = lax.all_gather(both, "col", axis=0)
    cols, parts = pl.pallas_call(
        spread_kernel,
        out_shape=(
            jax.ShapeDtypeStruct((2, width, toks), BF16),
            jax.ShapeDtypeStruct((n_row, 3, share, toks), BF16),
        ),
        in_specs=[SMEM, SMEM, VMEM, VMEM, VMEM, VMEM],
        out_specs=(VMEM, VMEM),
        scratch_shapes=[pltpu.VMEM((3, units, toks), F32)],
        compiler_params=PARAMS,
        name="spread",
    )(index, count, wide, *weights)
    terms = lax.all_to_all(parts, "row", 0, 0)
    own = pl.pallas_call(
        hidden_kernel,
        out_shape=jax.ShapeDtypeStruct((3, share, toks), BF16),
        in_specs=[VMEM],
        out_specs=VMEM,
        compiler_params=PARAMS,
        name="hidden",
    )(terms)
    all_units = lax.all_gather(own, "row", axis=0)
    rows, grads = pl.pallas_call(
        back_kernel,
        out_shape=(
            jax.ShapeDtypeStruct((n_col, 2 * half, width), BF16),
            jax.ShapeDtypeStruct((n_dp, 3, slots // n_dp, BS // 2, 2 * BS), BF16),
        ),
        in_specs=[SMEM, SMEM, VMEM, VMEM, VMEM, VMEM, VMEM],
        out_specs=(VMEM, VMEM),
        scratch_shapes=[
            pltpu.VMEM((3, units, toks), BF16),
            pltpu.VMEM((width, toks), F32),
            pltpu.VMEM((width, toks), F32),
        ],
        compiler_params=PARAMS,
        name="back",
    )(index, count, all_units, cols, *weights)
    row_terms = lax.all_to_all(rows, "col", 0, 0)
    grad_terms = lax.all_to_all(grads, "dp", 0, 0)
    grad_own = jnp.sum(grad_terms.astype(F32), axis=0).astype(BF16)
    grad_all = lax.all_gather(grad_own, "dp", axis=0)
    flat = jax.ShapeDtypeStruct((slots, BS * BS), BF16)
    block_grads = pl.pallas_call(
        unpack_kernel,
        out_shape=(flat, flat, flat),
        in_specs=[VMEM],
        out_specs=(VMEM, VMEM, VMEM),
        scratch_shapes=[pltpu.VMEM((slots * BS // 2, 2 * BS), F32)],
        compiler_params=PARAMS,
        name="unpack",
    )(grad_all)
    row_sum = jnp.sum(row_terms.astype(F32), axis=0).astype(BF16)
    return (row_sum[:half], row_sum[half:], *(b[None, None] for b in block_grads))


def solution(mesh):
    placed = (
        P(("dp", "col"), "row"),
        P(("dp", "col"), "row"),
        P("row", "col", None, None),
        P("row", "col", None, None),
        P("row", "col", None, None),
        P(None, "row", "col", None, None),
        P(None, "row", "col"),
    )
    return jax.shard_map(
        per_device,
        mesh=mesh,
        in_specs=placed,
        out_specs=(
            P(("dp", "col"), "row"),
            P(("dp", "col"), "row"),
            P("row", "col", None, None),
            P("row", "col", None, None),
            P("row", "col", None, None),
        ),
        check_vma=False,
    )
```

time: 399 us -> 190 us (0.48)
  waiting for transfers between devices: 227 us -> 58.8 us
  other arithmetic: 39.5 us -> 1.77 us
  local copies, waits for them, and re-layouts: 25 us -> 6.45 us
  Pallas kernels: 0 us -> 15.7 us
  matrix products: 11.9 us -> 0 us
  starting transfers between devices: 0.21 us -> 9.96 us
    psum x2 -> x0, waiting for transfers between devices: 122 us -> none  [the longest x1 73.3 us: per_device(): lax.psum(grad_terms[0].astype(jnp.bfloat16), 'dp').astype(jnp.float32)]
    convert_element_type x2 -> x0, waiting for transfers between devices: 81.6 us -> none  [the longest x1 69.5 us: per_device(): tokens_grad = in_rows.T.astype(jnp.bfloat16)]
    all_to_all x0 -> x2, blocking collectives: none -> 50.4 us  [the longest x1 30.6 us: per_device(): terms = lax.all_to_all(parts, 'row', 0, 0)]
    all_gather x4 -> x1, blocking collectives: 79.7 us -> 31.9 us  [per_device(): wide = lax.all_gather(both, 'col', axis=0)]
    all_gather x0 -> x2, waiting for transfers between devices: none -> 36.9 us  [the longest x1 26.5 us: per_device(): all_units = lax.all_gather(own, 'row', axis=0)]
    scatter-add x6 -> x0, other arithmetic: 27.6 us -> none  [collect(): summed = jnp.zeros((count_out, products.shape[1], products.shape[2]), jnp...]
    reduce_scatter x1 -> x0, waiting for transfers between devices: 23.1 us -> none  [per_device(): lax.psum_scatter(hgrad_part.astype(jnp.bfloat16), 'row', scatter_dimensio...]
    all_to_all x0 -> x1, waiting for transfers between devices: none -> 21.8 us  [per_device(): row_terms = lax.all_to_all(rows, 'col', 0, 0)]
  transfers between devices with their start and end apart: 5 -> 3, of which waited for: 5 -> 3; matrix products, arithmetic and copies ran while one was open for 12% -> 1% of each run, Pallas kernels for 0% -> 0%
where the time goes in v1:
time: 190 us; the launch traced here: 189 us
  blocking collectives  82.3 us (43%)
  waiting for transfers between devices  58.8 us (31%)
  Pallas kernels  15.7 us (8%)
  between operations  14.1 us (7%)
  starting transfers between devices  9.96 us (5%)
  local copies, waits for them, and re-layouts  6.45 us (3%)
    all_gather x1, blocking collectives, per_device(): wide = lax.all_gather(both, 'col', axis=0)  31.9 us
    all_to_all x1, blocking collectives, per_device(): terms = lax.all_to_all(parts, 'row', 0, 0)  30.6 us
    all_gather x1, waiting for transfers between devices, per_device(): all_units = lax.all_gather(own, 'row', axis=0)  26.5 us
    all_to_all x1, waiting for transfers between devices, per_device(): row_terms = lax.all_to_all(rows, 'col', 0, 0)  21.8 us
    all_to_all x1, blocking collectives, per_device(): grad_terms = lax.all_to_all(grads, 'dp', 0, 0)  19.8 us
    all_gather x1, waiting for transfers between devices, per_device(): grad_all = lax.all_gather(grad_own, 'dp', axis=0)  10.4 us
    all_to_all x1, starting transfers between devices, per_device(): row_terms = lax.all_to_all(rows, 'col', 0, 0)  9.88 us
    pallas_call x1, Pallas kernels, per_device(): pl.pallas_call(back_kernel, out_shape=(jax.ShapeDtypeStruct((n_col, 2 * h...  7.15 us
  transfers between devices with their start and end apart: 3, of which 3 were waited for; matrix products, arithmetic and copies ran while one was open for 1% of the time, Pallas kernels for 0%

profile of v1, /device:TPU:1, one launch (start us, length us, event | category | flops | bytes accessed | tf_op | source)
XLA Modules:
  0.0 189.1 jit_solution(4970363529416719773)
XLA Ops:
  7.2 0.0 copy-start.4
  7.2 0.0 all-gather.6.cloned.1.call-start
  7.2 0.8 pad_maximum_fusion
  8.0 0.0 copy-start.5
  8.0 31.9 %all-gather = bf16[256,1024]{1,0:T(8,128)(2,1)S(1)} all-gather(bf16[16,1024]{1,0:T(8,128)(2,1)S(1)} %pad_maximum_fusion), channel_id=2, replica_groups=mesh['dp'=4,'row'=8,'col'=16] {'col'}, dimensions={0}, use_global_device_ids=true | all-gather | bytes 557056 | tf_op jit(solution)/shard_map/all_gather | solution.py:134
  39.9 1.7 reshape.27.gate
  41.6 0.0 copy-done.4
  41.7 0.0 copy-start.2
  41.7 0.0 copy-start.3
  41.7 0.8 reshape.28.up
  42.4 0.0 copy-done.5
  42.5 0.8 reshape.29.down
  43.2 0.0 copy-done.2
  43.2 0.0 copy-done.3
  43.2 5.0 %spread.1 = (bf16[2,1024,128]{2,1,0:T(8,128)(2,1)S(1)}, bf16[8,3,224,128]{3,2,1,0:T(8,128)(2,1)S(1)}) custom-call(s32[3,2,44]{2,1,0:T(2,128)S(1)} %bitcast.11, s32[3]{0:T(128)S(1)} %bitcast.13, bf16[16,16,1024]{2,1,0:T(8,128)(2,1)S(1)} %bitcast.8, bf16[44,64,64]{2,1,0:T(8,128)(2,1)S(1)} %reshape.27.gate, bf16[44,64,64]{2,1,0:T(8,128)(2,1)S(1)} %reshape.28.up, ...), custom_call_target="tpu_custom_call" | custom-call | tf_op jit(solution)/shard_map/spread/pallas_call | solution.py:135
  48.3 30.6 %all_to_all.15.terms = bf16[8,3,224,128]{3,2,1,0:T(8,128)(2,1)S(1)} all-to-all(bf16[8,3,224,128]{3,2,1,0:T(8,128)(2,1)S(1)} %get-tuple-element.12), channel_id=1, replica_groups=mesh['dp'=4,'row'=8,'col'=16] {'row'}, dimensions={0} | all-to-all | bytes 2752512 | tf_op jit(solution)/shard_map/all_to_all | solution.py:147
  78.9 0.9 hidden.1
  79.8 0.0 all-gather.6.cloned.1.call-update
  79.8 26.5 %all-gather.6.cloned.1.call-done = bf16[24,224,128]{2,1,0:T(8,128)(2,1)} async-done(((bf16[3,224,128]{2,1,0:T(8,128)(2,1)}), bf16[24,224,128]{2,1,0:T(8,128)(2,1)}) %all-gather.6.cloned.1.call-update) | async-done | bytes 1376272 | tf_op jit(solution)/shard_map/all_gather | solution.py:156
  106.3 0.0 copy-start
  106.3 1.3 copy-done
  107.6 7.2 %back.1 = (bf16[16,16,1024]{2,1,0:T(8,128)(2,1)}, bf16[4,3,11,32,128]{4,3,2,1,0:T(8,128)(2,1)S(1)}) custom-call(s32[3,2,44]{2,1,0:T(2,128)S(1)} %bitcast.12, s32[3]{0:T(128)S(1)} %bitcast.14, bf16[8,3,224,128]{3,2,1,0:T(8,128)(2,1)S(1)} %bitcast.9, bf16[2,1024,128]{2,1,0:T(8,128)(2,1)S(1)} %get-tuple-element.13.cols, bf16[44,64,64]{2,1,0:T(8,128)(2,1)S(1)} %reshape.27.gate, ...), custom_call_target="tpu_custom_call" | custom-call | tf_op jit(solution)/shard_map/back/pallas_call | solution.py:157
  114.8 19.8 %all_to_all.16 = bf16[4,3,11,32,128]{4,3,2,1,0:T(8,128)(2,1)S(1)} all-to-all(bf16[4,3,11,32,128]{4,3,2,1,0:T(8,128)(2,1)S(1)} %get-tuple-element.15), channel_id=1, replica_groups=mesh['dp'=4,'row'=8,'col'=16] {'dp'}, dimensions={0} | all-to-all | bytes 2162688 | tf_op jit(solution)/shard_map/all_to_all | solution.py:174
  134.6 9.9 %all-to-all-start.1 = ((bf16[16,16,1024]{2,1,0:T(8,128)(2,1)}), bf16[16,16,1024]{2,1,0:T(8,128)(2,1)S(1)}, u32[]{:S(2)}, u32[]{:S(2)}) async-start(bf16[16,16,1024]{2,1,0:T(8,128)(2,1)} %get-tuple-element.14), calls=%async_computation.1 | async-start | bytes 1048576 | tf_op jit(solution)/shard_map/all_to_all | solution.py:173
  144.5 0.0 all-gather.8.cloned.1.call-start
  144.5 0.9 reduce_sum.25
  145.4 0.0 all-gather.8.cloned.1.call-update
  145.4 21.8 %all-to-all-done.1 = bf16[16,16,1024]{2,1,0:T(8,128)(2,1)S(1)} async-done(((bf16[16,16,1024]{2,1,0:T(8,128)(2,1)}), bf16[16,16,1024]{2,1,0:T(8,128)(2,1)S(1)}, u32[]{:S(2)}, u32[]{:S(2)}) %all-to-all-start.1) | async-done | bytes 524320 | tf_op jit(solution)/shard_map/all_to_all | solution.py:173
  167.3 0.1 reduce_sum.24
  167.3 0.6 fusion
  168.0 10.4 %all-gather.8.cloned.1.call-done = bf16[12,11,32,128]{3,2,1,0:T(8,128)(2,1)} async-done(((bf16[3,11,32,128]{3,2,1,0:T(8,128)(2,1)}), bf16[12,11,32,128]{3,2,1,0:T(8,128)(2,1)}) %all-gather.8.cloned.1.call-update) | async-done | bytes 1081360 | tf_op jit(solution)/shard_map/all_gather | solution.py:176
  178.4 0.0 copy-start.1
  178.4 1.2 copy-done.1
  179.6 2.6 %unpack.1 = (bf16[44,4096]{1,0:T(8,128)(2,1)}, bf16[44,4096]{1,0:T(8,128)(2,1)}, bf16[44,4096]{1,0:T(8,128)(2,1)}) custom-call(bf16[4,3,11,32,128]{4,3,2,1,0:T(8,128)(2,1)S(1)} %bitcast.10), custom_call_target="tpu_custom_call" | custom-call | tf_op jit(solution)/shard_map/unpack/pallas_call | solution.py:178
Async XLA Ops:
  7.2 34.5 %copy-start.4 = (bf16[1,1,44,4096]{3,2,1,0:T(8,128)(2,1)S(1)}, bf16[1,1,44,4096]{3,2,1,0:T(8,128)(2,1)}, u32[]{:S(2)}) copy-start(bf16[1,1,44,4096]{3,2,1,0:T(8,128)(2,1)} %param.10) | copy-start | bytes 1081348
  7.2 99.1 %all-gather.6.cloned.1.call-start = ((), (), s32[]{:S(2)}) async-start(), calls=%async_computation.3 | async-start | bytes 1548288 | tf_op jit(solution)/shard_map/all_gather | solution.py:156
  8.0 34.5 %copy-start.5 = (bf16[1,1,44,4096]{3,2,1,0:T(8,128)(2,1)S(1)}, bf16[1,1,44,4096]{3,2,1,0:T(8,128)(2,1)}, u32[]{:S(2)}) copy-start(bf16[1,1,44,4096]{3,2,1,0:T(8,128)(2,1)} %param.11) | copy-start | bytes 1081348
  41.7 1.6 copy-start.2
  41.7 1.6 copy-start.3
  106.3 1.3 copy-start
  134.6 32.7 %all-to-all-start.1 = ((bf16[16,16,1024]{2,1,0:T(8,128)(2,1)}), bf16[16,16,1024]{2,1,0:T(8,128)(2,1)S(1)}, u32[]{:S(2)}, u32[]{:S(2)}) async-start(bf16[16,16,1024]{2,1,0:T(8,128)(2,1)} %get-tuple-element.14), calls=%async_computation.1 | async-start | bytes 1048576 | tf_op jit(solution)/shard_map/all_to_all | solution.py:173
  144.5 33.9 %all-gather.8.cloned.1.call-start = ((), (), s32[]{:S(2)}) async-start(), calls=%async_computation.4 | async-start | bytes 1351680 | tf_op jit(solution)/shard_map/all_gather | solution.py:176
  178.4 1.2 copy-start.1
Sparse Core Ops, SparseCore 0:
  79.9 26.3 all-gather.5
  148.0 30.3 all-gather.7

commit v2 on v1

v2 whole, which is shorter than its diff:
```python
import jax
import jax.numpy as jnp
from jax import lax
from jax.experimental import pallas as pl
from jax.experimental.pallas import tpu as pltpu
from jax.sharding import PartitionSpec as P

BS = 64
UNROLL = 4
VMEM = pl.BlockSpec(memory_space=pltpu.VMEM)
SMEM = pl.BlockSpec(memory_space=pltpu.SMEM)
PARAMS = pltpu.CompilerParams(vmem_limit_bytes=40 * 1024 * 1024)
F32 = jnp.float32
BF16 = jnp.bfloat16


def for_slots(count, step):
    def group(g, carry):
        for u in range(UNROLL):
            s = g * UNROLL + u
            step(s, s < count)
        return carry

    lax.fori_loop(0, (count + UNROLL - 1) // UNROLL, group, 0)


def rows_of(block):
    return pl.ds(pl.multiple_of(block * BS, BS), BS)


def feature_major(wide, cols):
    n_col, pair, width = wide.shape
    half = pair // 2
    toks = n_col * half
    for j in range(0, width, 128):
        piece = wide[:, :, j : j + 128].astype(F32).reshape(n_col, 2, half, 128)
        for side in range(2):
            cols[side, j : j + 128, :] = piece[:, side].reshape(toks, 128).T.astype(BF16)


def spread_terms(index, count, cols, weights, total, mats):
    total[...] = jnp.zeros_like(total)
    for i, m in enumerate(mats):

        def step(s, live):
            block = jnp.where(live, weights[i][s], jnp.zeros_like(weights[i][s]))
            source = cols[m // 2, rows_of(index[m, 0, s]), :]
            place = rows_of(index[m, 1, s])
            total[i, place, :] += lax.dot_general(
                block, source, (((0,), (0,)), ((), ())), preferred_element_type=F32
            )

        for_slots(count[m], step)


def split_shares(total, mine, theirs):
    core = lax.axis_index("row") % 2
    share = mine.shape[2]
    for x in range(mine.shape[0]):
        for i in range(mine.shape[1]):
            for out, side in ((mine, core), (theirs, 1 - core)):
                first = pl.multiple_of((2 * x + side) * share, 32)
                out[x, i] = total[i, pl.ds(first, share), :].astype(BF16)


def gate_up_kernel(index, count, wide, gate, up, cols, mine, theirs, total):
    feature_major(wide, cols)
    spread_terms(index, count, cols, (gate, up), total, (0, 1))
    split_shares(total, mine, theirs)


def hgrad_kernel(index, count, cols, down, mine, theirs, total):
    spread_terms(index, count, cols, (down,), total, (2,))
    split_shares(total, mine, theirs)


def pair_sum_kernel(mine_ab, mine_c, other_ab, other_c, out):
    out[:, :2] = (mine_ab[...].astype(F32) + other_ab[...].astype(F32)).astype(BF16)
    out[:, 2:] = (mine_c[...].astype(F32) + other_c[...].astype(F32)).astype(BF16)


def hidden_kernel(terms, out):
    sums = [terms[0, m].astype(F32) for m in range(3)]
    for j in range(1, terms.shape[0]):
        sums = [sums[m] + terms[j, m].astype(F32) for m in range(3)]
    gate, up, hgrad = sums
    sig = jax.nn.sigmoid(gate)
    units = (
        (hgrad * up * sig * (1.0 + gate * (1.0 - sig))).astype(BF16),
        (hgrad * gate * sig).astype(BF16),
        (gate * sig * up).astype(BF16),
    )
    for j in range(out.shape[0]):
        for m in range(3):
            out[j, m] = units[m]


def back_kernel(index, count, mine, theirs, gate, up, down, rows, units, out_total, in_total):
    core = lax.axis_index("row") % 2
    share = mine.shape[2]
    for x in range(mine.shape[0]):
        for m in range(3):
            for half, side in ((mine, core), (theirs, 1 - core)):
                first = pl.multiple_of((2 * x + side) * share, 32)
                units[m, pl.ds(first, share), :] = half[x, m]
    out_total[...] = jnp.zeros_like(out_total)
    in_total[...] = jnp.zeros_like(in_total)
    for m, weights in enumerate((gate, up, down)):
        total = out_total if m == 2 else in_total

        def step(s, live):
            block = jnp.where(live, weights[s], jnp.zeros_like(weights[s]))
            unit = units[m, rows_of(index[m, 1, s]), :]
            place = rows_of(index[m, 0, s])
            total[place, :] += jnp.dot(block, unit, preferred_element_type=F32)

        for_slots(count[m], step)
    n_col, pair, width = rows.shape
    half = pair // 2
    for j in range(0, width, 128):
        out_piece = out_total[j : j + 128, :].T.reshape(n_col, half, 128)
        in_piece = in_total[j : j + 128, :].T.reshape(n_col, half, 128)
        rows[:, :, j : j + 128] = jnp.concatenate([out_piece, in_piece], axis=1).astype(BF16)


def grads_kernel(index, count, units, cols, *outs):
    n_dp = len(outs)
    per = outs[0].shape[1]
    here = lax.axis_index("dp")

    def step(p, carry):
        for away, out in enumerate(outs):
            s = ((here + away) % n_dp) * per + p
            for m in range(3):
                unit = units[m, rows_of(index[m, 1, s]), :]
                source = cols[m // 2, rows_of(index[m, 0, s]), :]
                grad = lax.dot_general(
                    source, unit, (((1,), (1,)), ((), ())), preferred_element_type=F32
                )
                grad = jnp.where(s < count[m], grad, 0.0)
                packed = jnp.concatenate([grad[: BS // 2], grad[BS // 2 :]], axis=1)
                out[m, p] = packed.astype(BF16)
        return carry

    lax.fori_loop(0, per, step, 0)


def dp_sum_kernel(a, b, c, d, out):
    out[...] = (
        (a[...].astype(F32) + b[...].astype(F32)) + (c[...].astype(F32) + d[...].astype(F32))
    ).astype(BF16)


def unpack_kernel(*refs):
    *pieces, gate, up, down, flat = refs
    n_dp = len(pieces)
    _, per, depth, lanes = pieces[0].shape
    slots = n_dp * per
    here = lax.axis_index("dp")
    low = lax.broadcasted_iota(jnp.int32, (slots, lanes), 1) < BS
    for m, out in enumerate((gate, up, down)):
        for away, piece in enumerate(pieces):
            owner = (here + n_dp - away) % n_dp
            first = pl.multiple_of(owner * per * depth, 32)
            flat[pl.ds(first, per * depth), :] = piece[m].astype(F32).reshape(per * depth, lanes)
        for k in range(0, depth, 2):
            even = flat[pl.ds(k, slots, stride=depth), :]
            odd = flat[pl.ds(k + 1, slots, stride=depth), :]
            out[:, k * BS : k * BS + lanes] = jnp.where(low, even, pltpu.roll(odd, BS, 1)).astype(BF16)
            start = (depth + k) * BS
            out[:, start : start + lanes] = jnp.where(low, pltpu.roll(even, BS, 1), odd).astype(BF16)


def call(body, name, out_shape, n_scalars, n_arrays, scratch=()):
    many = isinstance(out_shape, (tuple, list))
    return pl.pallas_call(
        body,
        out_shape=out_shape,
        in_specs=[SMEM] * n_scalars + [VMEM] * n_arrays,
        out_specs=tuple(VMEM for _ in out_shape) if many else VMEM,
        scratch_shapes=list(scratch),
        compiler_params=PARAMS,
        name=name,
    )


def per_device(tokens, grad_out, gate_blocks, up_blocks, down_blocks, block_index, block_count):
    n_dp, n_row, n_col = (lax.axis_size(a) for a in ("dp", "row", "col"))
    slots = gate_blocks.shape[2]
    half, width = tokens.shape
    toks = half * n_col
    units = 28 * BS
    share = units // n_row
    chips = n_row // 2
    index = block_index.reshape(3, 2, slots)
    count = block_count.reshape(3)
    gate, up, down = (w.reshape(slots, BS, BS) for w in (gate_blocks, up_blocks, down_blocks))
    pair = [(i, i ^ 1) for i in range(n_row)]
    same_core = [[2 * x + k for x in range(chips)] for k in range(2)]

    def arr(*shape):
        return jax.ShapeDtypeStruct(shape, BF16)

    both = jnp.concatenate([tokens, grad_out], axis=0)
    wide = lax.all_to_all(jnp.broadcast_to(both[None], (n_col, 2 * half, width)), "col", 0, 0)
    cols, mine_ab, theirs_ab = call(
        gate_up_kernel,
        "gate_up",
        (arr(2, width, toks), arr(chips, 2, share, toks), arr(chips, 2, share, toks)),
        2,
        3,
        [pltpu.VMEM((2, units, toks), F32)],
    )(index, count, wide, gate, up)
    other_ab = lax.ppermute(theirs_ab, "row", pair)
    mine_c, theirs_c = call(
        hgrad_kernel,
        "hgrad",
        (arr(chips, 1, share, toks), arr(chips, 1, share, toks)),
        2,
        2,
        [pltpu.VMEM((1, units, toks), F32)],
    )(index, count, cols, down)
    other_c = lax.ppermute(theirs_c, "row", pair)
    terms = call(pair_sum_kernel, "pair_sum", arr(chips, 3, share, toks), 0, 4)(
        mine_ab, mine_c, other_ab, other_c
    )
    terms = lax.all_to_all(terms, "row", 0, 0, axis_index_groups=same_core)
    own = call(hidden_kernel, "hidden", arr(chips, 3, share, toks), 0, 1)(terms)
    mine = lax.all_to_all(own, "row", 0, 0, axis_index_groups=same_core)
    theirs = lax.ppermute(mine, "row", pair)
    rows, band = call(
        back_kernel,
        "back",
        (arr(n_col, 2 * half, width), arr(3, units, toks)),
        2,
        5,
        [pltpu.VMEM((width, toks), F32), pltpu.VMEM((width, toks), F32)],
    )(index, count, mine, theirs, gate, up, down)
    row_terms = lax.all_to_all(rows, "col", 0, 0)
    packed = arr(3, slots // n_dp, BS // 2, 2 * BS)
    grads = call(grads_kernel, "grads", (packed,) * n_dp, 2, 2)(index, count, band, cols)
    moves = [[(i, (i + away) % n_dp) for i in range(n_dp)] for away in range(n_dp)]
    arrived = [lax.ppermute(grads[away], "dp", moves[away]) for away in range(1, n_dp)]
    summed = call(dp_sum_kernel, "dp_sum", packed, 0, n_dp)(grads[0], *arrived)
    pieces = [summed] + [lax.ppermute(summed, "dp", moves[away]) for away in range(1, n_dp)]
    flat = arr(slots, BS * BS)
    block_grads = call(
        unpack_kernel,
        "unpack",
        (flat, flat, flat),
        0,
        n_dp,
        [pltpu.VMEM((slots * BS // 2, 2 * BS), F32)],
    )(*pieces)
    row_sum = jnp.sum(row_terms.astype(F32), axis=0).astype(BF16)
    return (row_sum[:half], row_sum[half:], *(b[None, None] for b in block_grads))


def solution(mesh):
    placed = (
        P(("dp", "col"), "row"),
        P(("dp", "col"), "row"),
        P("row", "col", None, None),
        P("row", "col", None, None),
        P("row", "col", None, None),
        P(None, "row", "col", None, None),
        P(None, "row", "col"),
    )
    return jax.shard_map(
        per_device,
        mesh=mesh,
        in_specs=placed,
        out_specs=(
            P(("dp", "col"), "row"),
            P(("dp", "col"), "row"),
            P("row", "col", None, None),
            P("row", "col", None, None),
            P("row", "col", None, None),
        ),
        check_vma=False,
    )
```

time: 190 us -> 159 us (0.84)
  blocking collectives: 82.3 us -> 26.4 us
  starting transfers between devices: 9.96 us -> 58.8 us
  waiting for transfers between devices: 58.8 us -> 44.9 us
  between operations: 14.1 us -> 0.83 us
  Pallas kernels: 15.7 us -> 20.1 us
    all_gather x2 -> x0, waiting for transfers between devices: 36.9 us -> none  [the longest x1 26.5 us: per_device(): all_units = lax.all_gather(own, 'row', axis=0)]
    ppermute x0 -> x9, starting transfers between devices: none -> 36.7 us  [the longest x3 10.7 us: per_device(): lax.ppermute(grads[away], 'dp', moves[away])]
    all_gather x1 -> x0, blocking collectives: 31.9 us -> none  [per_device(): wide = lax.all_gather(both, 'col', axis=0)]
    all_to_all x2, blocking collectives: 50.4 us -> 26.4 us  [the longest x1 14.5 us: per_device(): terms = lax.all_to_all(terms, 'row', 0, 0, axis_index_groups=same_core)]
    ppermute x0 -> x9, waiting for transfers between devices: none -> 23.7 us  [the longest x3 12.1 us: per_device(): lax.ppermute(summed, 'dp', moves[away])]
    all_to_all x1, waiting for transfers between devices: 21.8 us -> 0.01 us  [per_device(): row_terms = lax.all_to_all(rows, 'col', 0, 0)]
    all_to_all x0 -> x1, waiting for transfers between devices: none -> 21.2 us  [per_device(): lax.all_to_all(jnp.broadcast_to(both[None], (n_col, 2 * half, width)), 'c...]
    all_to_all x0 -> x1, starting transfers between devices: none -> 15.7 us  [per_device(): lax.all_to_all(jnp.broadcast_to(both[None], (n_col, 2 * half, width)), 'c...]
  transfers between devices with their start and end apart: 3 -> 11, of which waited for: 3 -> 9; matrix products, arithmetic and copies ran while one was open for 1% -> 1% of each run, Pallas kernels for 0% -> 6%
where the time goes in v2:
time: 159 us; the launch traced here: 158 us
  starting transfers between devices  58.8 us (37%)
  waiting for transfers between devices  44.9 us (28%)
  blocking collectives  26.4 us (17%)
  Pallas kernels  20.1 us (13%)
  local copies, waits for them, and re-layouts  6.22 us (4%)
    all_to_all x1, waiting for transfers between devices, per_device(): lax.all_to_all(jnp.broadcast_to(both[None], (n_col, 2 * half, width)), 'c...  21.2 us
    all_to_all x1, starting transfers between devices, per_device(): lax.all_to_all(jnp.broadcast_to(both[None], (n_col, 2 * half, width)), 'c...  15.7 us
    all_to_all x1, blocking collectives, per_device(): terms = lax.all_to_all(terms, 'row', 0, 0, axis_index_groups=same_core)  14.5 us
    ppermute x3, waiting for transfers between devices, per_device(): lax.ppermute(summed, 'dp', moves[away])  12.1 us
    all_to_all x1, blocking collectives, per_device(): mine = lax.all_to_all(own, 'row', 0, 0, axis_index_groups=same_core)  11.8 us
    ppermute x3, starting transfers between devices, per_device(): lax.ppermute(grads[away], 'dp', moves[away])  10.7 us
    ppermute x3, starting transfers between devices, per_device(): lax.ppermute(summed, 'dp', moves[away])  10.5 us
    ppermute x1, starting transfers between devices, per_device(): other_ab = lax.ppermute(theirs_ab, 'row', pair)  8.91 us
  transfers between devices with their start and end apart: 11, of which 9 were waited for; matrix products, arithmetic and copies ran while one was open for 1% of the time, Pallas kernels for 6%

profile of v2, /device:TPU:1, one launch (start us, length us, event | category | flops | bytes accessed | tf_op | source)
XLA Modules:
  0.0 158.1 jit_solution(2241854797900398233)
XLA Ops:
  0.6 0.0 copy-start.4
  0.6 0.8 pad_maximum_fusion
  1.4 0.0 copy-start.5
  1.4 0.9 broadcast_in_dim.15
  2.3 15.7 %all-to-all-start = ((bf16[16,16,1024]{2,1,0:T(8,128)(2,1)}), bf16[16,16,1024]{2,1,0:T(8,128)(2,1)S(1)}, u32[]{:S(2)}, u32[]{:S(2)}) async-start(bf16[16,16,1024]{2,1,0:T(8,128)(2,1)} %broadcast_in_dim.15), calls=%async_computation | async-start | bytes 1048576 | tf_op jit(solution)/shard_map/all_to_all | solution.py:205
  18.0 0.0 copy-done.4
  18.1 0.0 copy-start.2
  18.1 0.0 copy-start.3
  18.1 0.8 reshape.28.gate
  18.9 0.0 copy-done.5
  18.9 0.0 copy-start.6
  18.9 0.8 reshape.29.up
  19.6 21.2 %all-to-all-done.wide = bf16[16,16,1024]{2,1,0:T(8,128)(2,1)S(1)} async-done(((bf16[16,16,1024]{2,1,0:T(8,128)(2,1)}), bf16[16,16,1024]{2,1,0:T(8,128)(2,1)S(1)}, u32[]{:S(2)}, u32[]{:S(2)}) %all-to-all-start) | async-done | bytes 524320 | tf_op jit(solution)/shard_map/all_to_all | solution.py:205
  40.9 0.0 copy-done.2
  40.9 0.0 copy-done.3
  40.9 4.7 %gate_up.1 = (bf16[2,1024,128]{2,1,0:T(8,128)(2,1)S(1)}, bf16[4,2,224,128]{3,2,1,0:T(8,128)(2,1)S(1)}, bf16[4,2,224,128]{3,2,1,0:T(8,128)(2,1)}) custom-call(s32[3,2,44]{2,1,0:T(2,128)S(1)} %bitcast.5, s32[3]{0:T(128)S(1)} %bitcast.9, bf16[16,16,1024]{2,1,0:T(8,128)(2,1)S(1)} %all-to-all-done.wide, bf16[44,64,64]{2,1,0:T(8,128)(2,1)S(1)} %reshape.28.gate, ...), custom_call_target="tpu_custom_call" | custom-call | tf_op jit(solution)/shard_map/gate_up/pallas_call | solution.py:206
  45.5 8.9 %collective-permute-start = (bf16[4,2,224,128]{3,2,1,0:T(8,128)(2,1)}, bf16[4,2,224,128]{3,2,1,0:T(8,128)(2,1)}, u32[]{:S(2)}, u32[]{:S(2)}) collective-permute-start(bf16[4,2,224,128]{3,2,1,0:T(8,128)(2,1)} %get-tuple-element.22), channel_id=1, source_target_pairs={{0,16},{16,0},{32,48},{48,32},{64,80},{80,64},{96,112},{112,96},{1... | collective-permute-start | bytes 1376264 | tf_op jit(solution)/shard_map/ppermute | solution.py:214
  54.5 0.0 copy-done.6
  54.5 0.8 reshape.30.down
  55.2 2.2 %hgrad.1 = (bf16[4,1,224,128]{3,2,1,0:T(8,128)(2,1)S(1)}, bf16[4,1,224,128]{3,2,1,0:T(8,128)(2,1)S(1)}) custom-call(s32[3,2,44]{2,1,0:T(2,128)S(1)} %bitcast.6, s32[3]{0:T(128)S(1)} %bitcast.10, bf16[2,1024,128]{2,1,0:T(8,128)(2,1)S(1)} %get-tuple-element.20.cols, bf16[44,64,64]{2,1,0:T(8,128)(2,1)S(1)} %reshape.30.down), custom_call_target="tpu_custom_call" | custom-call | tf_op jit(solution)/shard_map/hgrad/pallas_call | solution.py:215
  57.4 1.9 %collective-permute-start.1 = (bf16[4,1,224,128]{3,2,1,0:T(8,128)(2,1)S(1)}, bf16[4,1,224,128]{3,2,1,0:T(8,128)(2,1)S(1)}, u32[]{:S(2)}, u32[]{:S(2)}) collective-permute-start(bf16[4,1,224,128]{3,2,1,0:T(8,128)(2,1)S(1)} %get-tuple-element.23), channel_id=1, source_target_pairs={{0,16},{16,0},{32,48},{48,32},{64,80},{80,64},{96,112},{112,96},{1... | collective-permute-start | bytes 688136 | tf_op jit(solution)/shard_map/ppermute | solution.py:223
  59.3 1.5 collective-permute-done.1.other_c
  60.8 0.0 collective-permute-done.other_ab
  60.8 1.2 pair_sum.1
  62.0 14.5 %all_to_all.20.terms = bf16[4,3,224,128]{3,2,1,0:T(8,128)(2,1)S(1)} all-to-all(bf16[4,3,224,128]{3,2,1,0:T(8,128)(2,1)S(1)} %pair_sum.1), channel_id=1, replica_groups={{0,32,64,96},{16,48,80,112},{1,33,65,97},{17,49,81,113},{2,34,66,98},{1..., dimensions={0} | all-to-all | bytes 1376256 | tf_op jit(solution)/shard_map/all_to_all | solution.py:227
  76.5 0.1 hidden.1
  76.7 11.8 %all_to_all.21.mine = bf16[4,3,224,128]{3,2,1,0:T(8,128)(2,1)S(1)} all-to-all(bf16[4,3,224,128]{3,2,1,0:T(8,128)(2,1)S(1)} %hidden.1), channel_id=1, replica_groups={{0,32,64,96},{16,48,80,112},{1,33,65,97},{17,49,81,113},{2,34,66,98},{1..., dimensions={0} | all-to-all | bytes 1376256 | tf_op jit(solution)/shard_map/all_to_all | solution.py:229
  88.5 4.6 %collective-permute-start.2 = (bf16[4,3,224,128]{3,2,1,0:T(8,128)(2,1)S(1)}, bf16[4,3,224,128]{3,2,1,0:T(8,128)(2,1)S(1)}, u32[]{:S(2)}, u32[]{:S(2)}) collective-permute-start(bf16[4,3,224,128]{3,2,1,0:T(8,128)(2,1)S(1)} %all_to_all.21.mine), channel_id=1, source_target_pairs={{0,16},{16,0},{32,48},{48,32},{64,80},{80,64},{96,112},{112,96},{1... | collective-permute-start | bytes 2064392 | tf_op jit(solution)/shard_map/ppermute | solution.py:230
  93.1 1.7 %collective-permute-done.2.theirs = bf16[4,3,224,128]{3,2,1,0:T(8,128)(2,1)S(1)} collective-permute-done((bf16[4,3,224,128]{3,2,1,0:T(8,128)(2,1)S(1)}, bf16[4,3,224,128]{3,2,1,0:T(8,128)(2,1)S(1)}, u32[]{:S(2)}, u32[]{:S(2)}) %collective-permute-start.2) | collective-permute-done | bytes 688160 | tf_op jit(solution)/shard_map/ppermute | solution.py:230
  94.9 5.1 %back.1 = (bf16[16,16,1024]{2,1,0:T(8,128)(2,1)}, bf16[3,1792,128]{2,1,0:T(8,128)(2,1)S(1)}) custom-call(s32[3,2,44]{2,1,0:T(2,128)S(1)} %bitcast.7, s32[3]{0:T(128)S(1)} %bitcast.11, bf16[4,3,224,128]{3,2,1,0:T(8,128)(2,1)S(1)} %all_to_all.21.mine, bf16[4,3,224,128]{3,2,1,0:T(8,128)(2,1)S(1)} %collective-permute-done.2.theirs, ...), custom_call_target="tpu_custom_call" | custom-call | tf_op jit(solution)/shard_map/back/pallas_call | solution.py:231
  100.0 0.0 copy-start
  100.0 1.1 copy-done
  101.1 6.4 %all-to-all-start.3 = ((bf16[16,16,1024]{2,1,0:T(8,128)(2,1)}), bf16[16,16,1024]{2,1,0:T(8,128)(2,1)S(1)}, u32[]{:S(2)}, u32[]{:S(2)}) async-start(bf16[16,16,1024]{2,1,0:T(8,128)(2,1)} %get-tuple-element.24), calls=%async_computation.3 | async-start | bytes 1048576 | tf_op jit(solution)/shard_map/all_to_all | solution.py:239
  107.5 0.0 copy-start.1
  107.5 1.3 copy-done.1
  108.8 4.1 %grads.1 = (bf16[3,11,32,128]{3,2,1,0:T(8,128)(2,1)S(1)}, bf16[3,11,32,128]{3,2,1,0:T(8,128)(2,1)S(1)}, bf16[3,11,32,128]{3,2,1,0:T(8,128)(2,1)S(1)}, bf16[3,11,32,128]{3,2,1,0:T(8,128)(2,1)S(1)}) custom-call(s32[3,2,44]{2,1,0:T(2,128)S(1)} %bitcast.8, s32[3]{0:T(128)S(1)} %bitcast.12, bf16[3,1792,128]{2,1,0:T(8,128)(2,1)S(1)} %copy-done.1, ...), custom_call_target="tpu_custom_call" | custom-call | tf_op jit(solution)/shard_map/grads/pallas_call | solution.py:241
  112.9 3.2 %collective-permute-start.3 = (bf16[3,11,32,128]{3,2,1,0:T(8,128)(2,1)S(1)}, bf16[3,11,32,128]{3,2,1,0:T(8,128)(2,1)S(1)}, u32[]{:S(2)}, u32[]{:S(2)}) collective-permute-start(bf16[3,11,32,128]{3,2,1,0:T(8,128)(2,1)S(1)} %get-tuple-element.27), channel_id=1, source_target_pairs={{0,128},{128,256},{256,384},{384,0},{1,129},{129,257},{257,385},{3... | collective-permute-start | bytes 811016 | tf_op jit(solution)/shard_map/ppermute | solution.py:243
  116.1 4.5 %collective-permute-start.4 = (bf16[3,11,32,128]{3,2,1,0:T(8,128)(2,1)S(1)}, bf16[3,11,32,128]{3,2,1,0:T(8,128)(2,1)S(1)}, u32[]{:S(2)}, u32[]{:S(2)}) collective-permute-start(bf16[3,11,32,128]{3,2,1,0:T(8,128)(2,1)S(1)} %get-tuple-element.28), channel_id=1, source_target_pairs={{0,256},{128,384},{256,0},{384,128},{1,257},{129,385},{257,1},{385... | collective-permute-start | bytes 811016 | tf_op jit(solution)/shard_map/ppermute | solution.py:243
  120.7 3.0 %collective-permute-start.5 = (bf16[3,11,32,128]{3,2,1,0:T(8,128)(2,1)S(1)}, bf16[3,11,32,128]{3,2,1,0:T(8,128)(2,1)S(1)}, u32[]{:S(2)}, u32[]{:S(2)}) collective-permute-start(bf16[3,11,32,128]{3,2,1,0:T(8,128)(2,1)S(1)} %get-tuple-element.29), channel_id=1, source_target_pairs={{0,384},{128,0},{256,128},{384,256},{1,385},{129,1},{257,129},{385... | collective-permute-start | bytes 811016 | tf_op jit(solution)/shard_map/ppermute | solution.py:243
  123.6 0.4 collective-permute-done.3.b
  124.1 6.9 %collective-permute-done.4.c = bf16[3,11,32,128]{3,2,1,0:T(8,128)(2,1)S(1)} collective-permute-done((bf16[3,11,32,128]{3,2,1,0:T(8,128)(2,1)S(1)}, bf16[3,11,32,128]{3,2,1,0:T(8,128)(2,1)S(1)}, u32[]{:S(2)}, u32[]{:S(2)}) %collective-permute-start.4) | collective-permute-done | bytes 270368 | tf_op jit(solution)/shard_map/ppermute | solution.py:243
  131.0 1.1 collective-permute-done.5.d
  132.0 0.1 dp_sum.1.refs_0_
  132.2 5.0 %collective-permute-start.8 = (bf16[3,11,32,128]{3,2,1,0:T(8,128)(2,1)S(1)}, bf16[3,11,32,128]{3,2,1,0:T(8,128)(2,1)S(1)}, u32[]{:S(2)}, u32[]{:S(2)}) collective-permute-start(bf16[3,11,32,128]{3,2,1,0:T(8,128)(2,1)S(1)} %dp_sum.1.refs_0_), channel_id=1, source_target_pairs={{0,384},{128,0},{256,128},{384,256},{1,385},{129,1},{257,129},{385... | collective-permute-start | bytes 811016 | tf_op jit(solution)/shard_map/ppermute | solution.py:245
  137.2 3.5 %collective-permute-start.7 = (bf16[3,11,32,128]{3,2,1,0:T(8,128)(2,1)S(1)}, bf16[3,11,32,128]{3,2,1,0:T(8,128)(2,1)S(1)}, u32[]{:S(2)}, u32[]{:S(2)}) collective-permute-start(bf16[3,11,32,128]{3,2,1,0:T(8,128)(2,1)S(1)} %dp_sum.1.refs_0_), channel_id=1, source_target_pairs={{0,256},{128,384},{256,0},{384,128},{1,257},{129,385},{257,1},{385... | collective-permute-start | bytes 811016 | tf_op jit(solution)/shard_map/ppermute | solution.py:245
  140.8 1.9 %collective-permute-start.6 = (bf16[3,11,32,128]{3,2,1,0:T(8,128)(2,1)S(1)}, bf16[3,11,32,128]{3,2,1,0:T(8,128)(2,1)S(1)}, u32[]{:S(2)}, u32[]{:S(2)}) collective-permute-start(bf16[3,11,32,128]{3,2,1,0:T(8,128)(2,1)S(1)} %dp_sum.1.refs_0_), channel_id=1, source_target_pairs={{0,128},{128,256},{256,384},{384,0},{1,129},{129,257},{257,385},{3... | collective-permute-start | bytes 811016 | tf_op jit(solution)/shard_map/ppermute | solution.py:245
  142.7 0.8 collective-permute-done.8.refs_3_
  143.5 4.4 %collective-permute-done.7.refs_2_ = bf16[3,11,32,128]{3,2,1,0:T(8,128)(2,1)S(1)} collective-permute-done((bf16[3,11,32,128]{3,2,1,0:T(8,128)(2,1)S(1)}, bf16[3,11,32,128]{3,2,1,0:T(8,128)(2,1)S(1)}, u32[]{:S(2)}, u32[]{:S(2)}) %collective-permute-start.7) | collective-permute-done | bytes 270368 | tf_op jit(solution)/shard_map/ppermute | solution.py:245
  147.9 6.9 %collective-permute-done.6.refs_1_ = bf16[3,11,32,128]{3,2,1,0:T(8,128)(2,1)S(1)} collective-permute-done((bf16[3,11,32,128]{3,2,1,0:T(8,128)(2,1)S(1)}, bf16[3,11,32,128]{3,2,1,0:T(8,128)(2,1)S(1)}, u32[]{:S(2)}, u32[]{:S(2)}) %collective-permute-start.6) | collective-permute-done | bytes 270368 | tf_op jit(solution)/shard_map/ppermute | solution.py:245
  154.8 2.6 %unpack.1 = (bf16[44,4096]{1,0:T(8,128)(2,1)}, bf16[44,4096]{1,0:T(8,128)(2,1)}, bf16[44,4096]{1,0:T(8,128)(2,1)}) custom-call(bf16[3,11,32,128]{3,2,1,0:T(8,128)(2,1)S(1)} %dp_sum.1.refs_0_, bf16[3,11,32,128]{3,2,1,0:T(8,128)(2,1)S(1)} %collective-permute-done.6.refs_1_, bf16[3,11,32,128]{3,2,1,0:T(8,128)(2,1)S(1)} %collective-permute-done.7.refs_2_, ...), custom_call_target="tpu_custom_call" | custom-call | tf_op jit(solution)/shard_map/unpack/pallas_call | solution.py:247
  157.4 0.0 all-to-all-done.3
  157.4 0.1 reduce_sum.12
  157.5 0.6 fusion
Async XLA Ops:
  0.6 17.4 %copy-start.4 = (bf16[1,1,44,4096]{3,2,1,0:T(8,128)(2,1)S(1)}, bf16[1,1,44,4096]{3,2,1,0:T(8,128)(2,1)}, u32[]{:S(2)}) copy-start(bf16[1,1,44,4096]{3,2,1,0:T(8,128)(2,1)} %param.9) | copy-start | bytes 1081348
  1.4 17.4 %copy-start.5 = (bf16[1,1,44,4096]{3,2,1,0:T(8,128)(2,1)S(1)}, bf16[1,1,44,4096]{3,2,1,0:T(8,128)(2,1)}, u32[]{:S(2)}) copy-start(bf16[1,1,44,4096]{3,2,1,0:T(8,128)(2,1)} %param.10) | copy-start | bytes 1081348
  2.3 38.6 %all-to-all-start = ((bf16[16,16,1024]{2,1,0:T(8,128)(2,1)}), bf16[16,16,1024]{2,1,0:T(8,128)(2,1)S(1)}, u32[]{:S(2)}, u32[]{:S(2)}) async-start(bf16[16,16,1024]{2,1,0:T(8,128)(2,1)} %broadcast_in_dim.15), calls=%async_computation | async-start | bytes 1048576 | tf_op jit(solution)/shard_map/all_to_all | solution.py:205
  18.1 22.8 %copy-start.2 = (s32[3,1,1,2,44]{4,3,2,1,0:T(2,128)S(1)}, s32[3,1,1,2,44]{4,3,2,1,0:T(2,128)}, u32[]{:S(2)}) copy-start(s32[3,1,1,2,44]{4,3,2,1,0:T(2,128)} %param.12) | copy-start | bytes 3172
  18.1 22.8 %copy-start.3 = (s32[3,1,1]{0,2,1:T(1,128)S(1)}, s32[3,1,1]{0,2,1:T(1,128)}, u32[]{:S(2)}) copy-start(s32[3,1,1]{0,2,1:T(1,128)} %param.13) | copy-start | bytes 40
  18.9 35.6 %copy-start.6 = (bf16[1,1,44,4096]{3,2,1,0:T(8,128)(2,1)S(1)}, bf16[1,1,44,4096]{3,2,1,0:T(8,128)(2,1)}, u32[]{:S(2)}) copy-start(bf16[1,1,44,4096]{3,2,1,0:T(8,128)(2,1)} %param.11) | copy-start | bytes 1081348
  45.5 15.3 %collective-permute-start = (bf16[4,2,224,128]{3,2,1,0:T(8,128)(2,1)}, bf16[4,2,224,128]{3,2,1,0:T(8,128)(2,1)}, u32[]{:S(2)}, u32[]{:S(2)}) collective-permute-start(bf16[4,2,224,128]{3,2,1,0:T(8,128)(2,1)} %get-tuple-element.22), channel_id=1, source_target_pairs={{0,16},{16,0},{32,48},{48,32},{64,80},{80,64},{96,112},{112,96},{1... | collective-permute-start | bytes 1376264 | tf_op jit(solution)/shard_map/ppermute | solution.py:214
  57.4 3.4 %collective-permute-start.1 = (bf16[4,1,224,128]{3,2,1,0:T(8,128)(2,1)S(1)}, bf16[4,1,224,128]{3,2,1,0:T(8,128)(2,1)S(1)}, u32[]{:S(2)}, u32[]{:S(2)}) collective-permute-start(bf16[4,1,224,128]{3,2,1,0:T(8,128)(2,1)S(1)} %get-tuple-element.23), channel_id=1, source_target_pairs={{0,16},{16,0},{32,48},{48,32},{64,80},{80,64},{96,112},{112,96},{1... | collective-permute-start | bytes 688136 | tf_op jit(solution)/shard_map/ppermute | solution.py:223
  88.5 6.4 %collective-permute-start.2 = (bf16[4,3,224,128]{3,2,1,0:T(8,128)(2,1)S(1)}, bf16[4,3,224,128]{3,2,1,0:T(8,128)(2,1)S(1)}, u32[]{:S(2)}, u32[]{:S(2)}) collective-permute-start(bf16[4,3,224,128]{3,2,1,0:T(8,128)(2,1)S(1)} %all_to_all.21.mine), channel_id=1, source_target_pairs={{0,16},{16,0},{32,48},{48,32},{64,80},{80,64},{96,112},{112,96},{1... | collective-permute-start | bytes 2064392 | tf_op jit(solution)/shard_map/ppermute | solution.py:230
  100.0 1.1 copy-start
  101.1 56.3 %all-to-all-start.3 = ((bf16[16,16,1024]{2,1,0:T(8,128)(2,1)}), bf16[16,16,1024]{2,1,0:T(8,128)(2,1)S(1)}, u32[]{:S(2)}, u32[]{:S(2)}) async-start(bf16[16,16,1024]{2,1,0:T(8,128)(2,1)} %get-tuple-element.24), calls=%async_computation.3 | async-start | bytes 1048576 | tf_op jit(solution)/shard_map/all_to_all | solution.py:239
  107.5 1.3 copy-start.1
  112.9 11.2 %collective-permute-start.3 = (bf16[3,11,32,128]{3,2,1,0:T(8,128)(2,1)S(1)}, bf16[3,11,32,128]{3,2,1,0:T(8,128)(2,1)S(1)}, u32[]{:S(2)}, u32[]{:S(2)}) collective-permute-start(bf16[3,11,32,128]{3,2,1,0:T(8,128)(2,1)S(1)} %get-tuple-element.27), channel_id=1, source_target_pairs={{0,128},{128,256},{256,384},{384,0},{1,129},{129,257},{257,385},{3... | collective-permute-start | bytes 811016 | tf_op jit(solution)/shard_map/ppermute | solution.py:243
  116.1 14.8 %collective-permute-start.4 = (bf16[3,11,32,128]{3,2,1,0:T(8,128)(2,1)S(1)}, bf16[3,11,32,128]{3,2,1,0:T(8,128)(2,1)S(1)}, u32[]{:S(2)}, u32[]{:S(2)}) collective-permute-start(bf16[3,11,32,128]{3,2,1,0:T(8,128)(2,1)S(1)} %get-tuple-element.28), channel_id=1, source_target_pairs={{0,256},{128,384},{256,0},{384,128},{1,257},{129,385},{257,1},{385... | collective-permute-start | bytes 811016 | tf_op jit(solution)/shard_map/ppermute | solution.py:243
  120.7 11.4 %collective-permute-start.5 = (bf16[3,11,32,128]{3,2,1,0:T(8,128)(2,1)S(1)}, bf16[3,11,32,128]{3,2,1,0:T(8,128)(2,1)S(1)}, u32[]{:S(2)}, u32[]{:S(2)}) collective-permute-start(bf16[3,11,32,128]{3,2,1,0:T(8,128)(2,1)S(1)} %get-tuple-element.29), channel_id=1, source_target_pairs={{0,384},{128,0},{256,128},{384,256},{1,385},{129,1},{257,129},{385... | collective-permute-start | bytes 811016 | tf_op jit(solution)/shard_map/ppermute | solution.py:243
  132.2 11.3 %collective-permute-start.8 = (bf16[3,11,32,128]{3,2,1,0:T(8,128)(2,1)S(1)}, bf16[3,11,32,128]{3,2,1,0:T(8,128)(2,1)S(1)}, u32[]{:S(2)}, u32[]{:S(2)}) collective-permute-start(bf16[3,11,32,128]{3,2,1,0:T(8,128)(2,1)S(1)} %dp_sum.1.refs_0_), channel_id=1, source_target_pairs={{0,384},{128,0},{256,128},{384,256},{1,385},{129,1},{257,129},{385... | collective-permute-start | bytes 811016 | tf_op jit(solution)/shard_map/ppermute | solution.py:245
  137.2 10.6 %collective-permute-start.7 = (bf16[3,11,32,128]{3,2,1,0:T(8,128)(2,1)S(1)}, bf16[3,11,32,128]{3,2,1,0:T(8,128)(2,1)S(1)}, u32[]{:S(2)}, u32[]{:S(2)}) collective-permute-start(bf16[3,11,32,128]{3,2,1,0:T(8,128)(2,1)S(1)} %dp_sum.1.refs_0_), channel_id=1, source_target_pairs={{0,256},{128,384},{256,0},{384,128},{1,257},{129,385},{257,1},{385... | collective-permute-start | bytes 811016 | tf_op jit(solution)/shard_map/ppermute | solution.py:245
  140.8 14.0 %collective-permute-start.6 = (bf16[3,11,32,128]{3,2,1,0:T(8,128)(2,1)S(1)}, bf16[3,11,32,128]{3,2,1,0:T(8,128)(2,1)S(1)}, u32[]{:S(2)}, u32[]{:S(2)}) collective-permute-start(bf16[3,11,32,128]{3,2,1,0:T(8,128)(2,1)S(1)} %dp_sum.1.refs_0_), channel_id=1, source_target_pairs={{0,128},{128,256},{256,384},{384,0},{1,129},{129,257},{257,385},{3... | collective-permute-start | bytes 811016 | tf_op jit(solution)/shard_map/ppermute | solution.py:245

commit v3 on v2

v3 whole, which is shorter than its diff:
```python
import jax
import jax.numpy as jnp
from jax import lax
from jax.experimental import pallas as pl
from jax.experimental.pallas import tpu as pltpu
from jax.sharding import PartitionSpec as P

BS = 64
UNROLL = 4
VMEM = pl.BlockSpec(memory_space=pltpu.VMEM)
SMEM = pl.BlockSpec(memory_space=pltpu.SMEM)
PARAMS = pltpu.CompilerParams(vmem_limit_bytes=40 * 1024 * 1024)
F32 = jnp.float32
BF16 = jnp.bfloat16


def for_slots(count, step):
    def group(g, carry):
        for u in range(UNROLL):
            s = g * UNROLL + u
            step(s, s < count)
        return carry

    lax.fori_loop(0, (count + UNROLL - 1) // UNROLL, group, 0)


def rows_of(block):
    return pl.ds(pl.multiple_of(block * BS, BS), BS)


def feature_major(wide, cols):
    n_col, pair, width = wide.shape
    half = pair // 2
    toks = n_col * half
    for j in range(0, width, 128):
        piece = wide[:, :, j : j + 128].astype(F32).reshape(n_col, 2, half, 128)
        for side in range(2):
            cols[side, j : j + 128, :] = piece[:, side].reshape(toks, 128).T.astype(BF16)


def spread_kernel(index, count, wide, gate, up, down, cols, mine, theirs, total):
    feature_major(wide, cols)
    total[...] = jnp.zeros_like(total)
    for m, weights in enumerate((gate, up, down)):

        def step(s, live):
            block = jnp.where(live, weights[s], jnp.zeros_like(weights[s]))
            source = cols[m // 2, rows_of(index[m, 0, s]), :]
            place = rows_of(index[m, 1, s])
            total[m, place, :] += lax.dot_general(
                block, source, (((0,), (0,)), ((), ())), preferred_element_type=F32
            )

        for_slots(count[m], step)
    core = lax.axis_index("row") % 2
    share = mine.shape[2]
    for x in range(mine.shape[0]):
        for m in range(3):
            for out, side in ((theirs, 1 - core), (mine, core)):
                first = pl.multiple_of((2 * x + side) * share, 32)
                out[x, m] = total[m, pl.ds(first, share), :].astype(BF16)


def pair_sum_kernel(mine, other, out):
    out[...] = (mine[...].astype(F32) + other[...].astype(F32)).astype(BF16)


def hidden_kernel(terms, out):
    sums = [terms[0, m].astype(F32) for m in range(3)]
    for j in range(1, terms.shape[0]):
        sums = [sums[m] + terms[j, m].astype(F32) for m in range(3)]
    gate, up, hgrad = sums
    sig = jax.nn.sigmoid(gate)
    units = (
        (hgrad * up * sig * (1.0 + gate * (1.0 - sig))).astype(BF16),
        (hgrad * gate * sig).astype(BF16),
        (gate * sig * up).astype(BF16),
    )
    for j in range(out.shape[0]):
        for m in range(3):
            out[j, m] = units[m]


def grads_kernel(index, count, mine, theirs, cols, band, own, ahead, across, behind):
    core = lax.axis_index("row") % 2
    share = mine.shape[2]
    for x in range(mine.shape[0]):
        for m in range(3):
            for half, side in ((mine, core), (theirs, 1 - core)):
                first = pl.multiple_of((2 * x + side) * share, 32)
                band[m, pl.ds(first, share), :] = half[x, m]
    outs = (own, ahead, across, behind)
    n_dp = len(outs)
    per = own.shape[1]
    here = lax.axis_index("dp")

    def step(p, carry):
        for away, out in enumerate(outs):
            s = ((here + away) % n_dp) * per + p
            for m in range(3):
                unit = band[m, rows_of(index[m, 1, s]), :]
                source = cols[m // 2, rows_of(index[m, 0, s]), :]
                grad = lax.dot_general(
                    source, unit, (((1,), (1,)), ((), ())), preferred_element_type=F32
                )
                grad = jnp.where(s < count[m], grad, 0.0)
                packed = jnp.concatenate([grad[: BS // 2], grad[BS // 2 :]], axis=1)
                out[m, p] = packed.astype(BF16)
        return carry

    lax.fori_loop(0, per, step, 0)


def back_kernel(index, count, band, gate, up, down, rows, out_total, in_total):
    out_total[...] = jnp.zeros_like(out_total)
    in_total[...] = jnp.zeros_like(in_total)
    for m, weights in enumerate((gate, up, down)):
        total = out_total if m == 2 else in_total

        def step(s, live):
            block = jnp.where(live, weights[s], jnp.zeros_like(weights[s]))
            unit = band[m, rows_of(index[m, 1, s]), :]
            place = rows_of(index[m, 0, s])
            total[place, :] += jnp.dot(block, unit, preferred_element_type=F32)

        for_slots(count[m], step)
    n_col, pair, width = rows.shape
    half = pair // 2
    for j in range(0, width, 128):
        out_piece = out_total[j : j + 128, :].T.reshape(n_col, half, 128)
        in_piece = in_total[j : j + 128, :].T.reshape(n_col, half, 128)
        rows[:, :, j : j + 128] = jnp.concatenate([out_piece, in_piece], axis=1).astype(BF16)


def dp_sum_kernel(a, b, c, d, out):
    out[...] = (
        (a[...].astype(F32) + b[...].astype(F32)) + (c[...].astype(F32) + d[...].astype(F32))
    ).astype(BF16)


def unpack_kernel(own, prev, next_, far_low, far_high, gate, up, down, flat):
    n_dp = 4
    _, per, depth, lanes = own.shape
    slots = n_dp * per
    here = lax.axis_index("dp")
    low = lax.broadcasted_iota(jnp.int32, (slots, lanes), 1) < BS
    for m, out in enumerate((gate, up, down)):
        for away, piece in ((0, own[m]), (3, prev[m]), (1, next_[m]), (2, None)):
            if piece is None:
                piece = jnp.concatenate([far_low[m], far_high[m]], axis=1)
            first = pl.multiple_of(((here + away) % n_dp) * per * depth, 32)
            flat[pl.ds(first, per * depth), :] = piece.astype(F32).reshape(per * depth, lanes)
        for k in range(0, depth, 2):
            even = flat[pl.ds(k, slots, stride=depth), :]
            odd = flat[pl.ds(k + 1, slots, stride=depth), :]
            out[:, k * BS : k * BS + lanes] = jnp.where(low, even, pltpu.roll(odd, BS, 1)).astype(BF16)
            start = (depth + k) * BS
            out[:, start : start + lanes] = jnp.where(low, pltpu.roll(even, BS, 1), odd).astype(BF16)


def call(body, name, out_shape, ins, outs, scratch=()):
    return pl.pallas_call(
        body,
        out_shape=out_shape,
        in_specs=ins,
        out_specs=outs,
        scratch_shapes=list(scratch),
        compiler_params=PARAMS,
        name=name,
    )


def per_device(tokens, grad_out, gate_blocks, up_blocks, down_blocks, block_index, block_count):
    n_dp, n_row, n_col = (lax.axis_size(a) for a in ("dp", "row", "col"))
    slots = gate_blocks.shape[2]
    half, width = tokens.shape
    toks = half * n_col
    units = 28 * BS
    share = units // n_row
    chips = n_row // 2
    index = block_index.reshape(3, 2, slots)
    count = block_count.reshape(3)
    gate, up, down = (w.reshape(slots, BS, BS) for w in (gate_blocks, up_blocks, down_blocks))
    pair = [(i, i ^ 1) for i in range(n_row)]
    same_core = [[2 * x + k for x in range(chips)] for k in range(2)]
    ahead, behind, across = ([(i, (i + d) % n_dp) for i in range(n_dp)] for d in (1, 3, 2))

    def arr(*shape):
        return jax.ShapeDtypeStruct(shape, BF16)

    both = jnp.concatenate([tokens, grad_out], axis=0)
    wide = lax.all_gather(both, "col", axis=0)
    terms = arr(chips, 3, share, toks)
    cols, mine, theirs = call(
        spread_kernel,
        "spread",
        (arr(2, width, toks), terms, terms),
        [SMEM] * 2 + [VMEM] * 4,
        (VMEM,) * 3,
        [pltpu.VMEM((3, units, toks), F32)],
    )(index, count, wide, gate, up, down)
    other = lax.ppermute(theirs, "row", pair)
    paired = call(pair_sum_kernel, "pair_sum", terms, [VMEM] * 2, VMEM)(mine, other)
    summed = lax.all_to_all(paired, "row", 0, 0, axis_index_groups=same_core)
    own = call(hidden_kernel, "hidden", terms, [VMEM], VMEM)(summed)
    mine = lax.all_to_all(own, "row", 0, 0, axis_index_groups=same_core)
    theirs = lax.ppermute(mine, "row", pair)
    packed = arr(3, slots // n_dp, BS // 2, 2 * BS)
    band, own, to_next, to_far, to_prev = call(
        grads_kernel,
        "grads",
        (arr(3, units, toks),) + (packed,) * n_dp,
        [SMEM] * 2 + [VMEM] * 3,
        (VMEM,) * (1 + n_dp),
    )(index, count, mine, theirs, cols)
    rows = call(
        back_kernel,
        "back",
        arr(n_col, 2 * half, width),
        [SMEM] * 2 + [VMEM] * 4,
        VMEM,
        [pltpu.VMEM((width, toks), F32), pltpu.VMEM((width, toks), F32)],
    )(index, count, band, gate, up, down)
    row_terms = lax.all_to_all(rows, "col", 0, 0)
    from_far = lax.ppermute(to_far, "dp", across)
    from_prev = lax.ppermute(to_next, "dp", ahead)
    from_next = lax.ppermute(to_prev, "dp", behind)
    own = call(dp_sum_kernel, "dp_sum", packed, [VMEM] * 4, VMEM)(own, from_far, from_prev, from_next)
    prev = lax.ppermute(own, "dp", ahead)
    next_ = lax.ppermute(own, "dp", behind)
    cut = BS // 4
    far_low = lax.ppermute(prev[:, :, :cut], "dp", ahead)
    far_high = lax.ppermute(next_[:, :, cut:], "dp", behind)
    flat = arr(slots, BS * BS)
    block_grads = call(
        unpack_kernel,
        "unpack",
        (flat, flat, flat),
        [VMEM] * 5,
        (VMEM,) * 3,
        [pltpu.VMEM((slots * BS // 2, 2 * BS), F32)],
    )(own, prev, next_, far_low, far_high)
    row_sum = jnp.sum(row_terms.astype(F32), axis=0).astype(BF16)
    return (row_sum[:half], row_sum[half:], *(b[None, None] for b in block_grads))


def solution(mesh):
    placed = (
        P(("dp", "col"), "row"),
        P(("dp", "col"), "row"),
        P("row", "col", None, None),
        P("row", "col", None, None),
        P("row", "col", None, None),
        P(None, "row", "col", None, None),
        P(None, "row", "col"),
    )
    return jax.shard_map(
        per_device,
        mesh=mesh,
        in_specs=placed,
        out_specs=(
            P(("dp", "col"), "row"),
            P(("dp", "col"), "row"),
            P("row", "col", None, None),
            P("row", "col", None, None),
            P("row", "col", None, None),
        ),
        check_vma=False,
    )
```

time: 159 us -> 147 us (0.925)
  the two profiles are of different devices: /device:TPU:1 before, /device:TPU:2 now
where the time goes in v3:
time: 147 us
  blocking collectives  67.8 us (46%)
  starting transfers between devices  38.3 us (26%)
  waiting for transfers between devices  20.7 us (14%)
  Pallas kernels  14.4 us (10%)
  local copies, waits for them, and re-layouts  3.9 us (3%)
    all_gather x1, blocking collectives, per_device(): wide = lax.all_gather(both, 'col', axis=0)  38.6 us
    all_to_all x1, blocking collectives, per_device(): summed = lax.all_to_all(paired, 'row', 0, 0, axis_index_groups=same_core)  16.1 us
    all_to_all x1, blocking collectives, per_device(): mine = lax.all_to_all(own, 'row', 0, 0, axis_index_groups=same_core)  13 us
    all_to_all x1, starting transfers between devices, per_device(): row_terms = lax.all_to_all(rows, 'col', 0, 0)  7.67 us
    ppermute x1, waiting for transfers between devices, per_device(): from_prev = lax.ppermute(to_next, 'dp', ahead)  5.7 us
    ppermute x1, waiting for transfers between devices, per_device(): far_low = lax.ppermute(prev[:, :, :cut], 'dp', ahead)  5.61 us
    ppermute x1, starting transfers between devices, per_device(): far_high = lax.ppermute(next_[:, :, cut:], 'dp', behind)  5.6 us
    ppermute x1, starting transfers between devices, per_device(): next_ = lax.ppermute(own, 'dp', behind)  5.2 us
  transfers between devices with their start and end apart: 10, of which 8 were waited for; matrix products, arithmetic and copies ran while one was open for 0% of the time, Pallas kernels for 2%

profile of v3, /device:TPU:2, one launch (start us, length us, event | category | flops | bytes accessed | tf_op | source)
XLA Modules:
  0.0 146.8 jit_solution(11113041767914566327)
XLA Ops:
  0.6 0.0 copy-start.2
  0.6 0.8 pad_maximum_fusion
  1.4 0.0 copy-start.3
  1.4 38.6 %all-gather = bf16[256,1024]{1,0:T(8,128)(2,1)S(1)} all-gather(bf16[16,1024]{1,0:T(8,128)(2,1)S(1)} %pad_maximum_fusion), channel_id=2, replica_groups=mesh['dp'=4,'row'=8,'col'=16] {'col'}, dimensions={0}, use_global_device_ids=true | all-gather | bytes 557056 | tf_op jit(solution)/shard_map/all_gather | solution.py:192
  40.1 1.7 %reshape.27.gate = bf16[44,64,64]{2,1,0:T(8,128)(2,1)S(1)} reshape(bf16[1,1,44,4096]{3,2,1,0:T(8,128)(2,1)} %param.9) | data formatting | bytes 720896 | tf_op jit(solution)/shard_map/reshape | solution.py:183
  41.8 0.0 copy-done.2
  41.8 0.0 copy-start
  41.8 0.0 copy-start.1
  41.8 0.8 reshape.28.up
  42.6 0.0 copy-done.3
  42.6 0.8 reshape.29.down
  43.4 0.0 copy-done
  43.4 0.0 copy-done.1
  43.4 3.6 %spread.1 = (bf16[2,1024,128]{2,1,0:T(8,128)(2,1)S(1)}, bf16[4,3,224,128]{3,2,1,0:T(8,128)(2,1)S(1)}, bf16[4,3,224,128]{3,2,1,0:T(8,128)(2,1)S(1)}) custom-call(s32[3,2,44]{2,1,0:T(2,128)S(1)} %bitcast.7, s32[3]{0:T(128)S(1)} %bitcast.10, bf16[16,16,1024]{2,1,0:T(8,128)(2,1)S(1)} %bitcast.6, bf16[44,64,64]{2,1,0:T(8,128)(2,1)S(1)} %reshape.27.gate, ...), custom_call_target="tpu_custom_call" | custom-call | tf_op jit(solution)/shard_map/spread/pallas_call | solution.py:194
  47.0 1.9 %collective-permute-start = (bf16[4,3,224,128]{3,2,1,0:T(8,128)(2,1)S(1)}, bf16[4,3,224,128]{3,2,1,0:T(8,128)(2,1)S(1)}, u32[]{:S(2)}, u32[]{:S(2)}) collective-permute-start(bf16[4,3,224,128]{3,2,1,0:T(8,128)(2,1)S(1)} %get-tuple-element.17), channel_id=1, source_target_pairs={{0,16},{16,0},{32,48},{48,32},{64,80},{80,64},{96,112},{112,96},{1... | collective-permute-start | bytes 2064392 | tf_op jit(solution)/shard_map/ppermute | solution.py:202
  48.9 2.1 %collective-permute-done.other = bf16[4,3,224,128]{3,2,1,0:T(8,128)(2,1)S(1)} collective-permute-done((bf16[4,3,224,128]{3,2,1,0:T(8,128)(2,1)S(1)}, bf16[4,3,224,128]{3,2,1,0:T(8,128)(2,1)S(1)}, u32[]{:S(2)}, u32[]{:S(2)}) %collective-permute-start) | collective-permute-done | bytes 688160 | tf_op jit(solution)/shard_map/ppermute | solution.py:202
  51.0 0.2 pair_sum.1
  51.2 16.1 %all_to_all.15.terms = bf16[4,3,224,128]{3,2,1,0:T(8,128)(2,1)S(1)} all-to-all(bf16[4,3,224,128]{3,2,1,0:T(8,128)(2,1)S(1)} %pair_sum.1), channel_id=1, replica_groups={{0,32,64,96},{16,48,80,112},{1,33,65,97},{17,49,81,113},{2,34,66,98},{1..., dimensions={0} | all-to-all | bytes 1376256 | tf_op jit(solution)/shard_map/all_to_all | solution.py:204
  67.3 0.1 hidden.1
  67.4 13.0 %all_to_all.16.mine = bf16[4,3,224,128]{3,2,1,0:T(8,128)(2,1)S(1)} all-to-all(bf16[4,3,224,128]{3,2,1,0:T(8,128)(2,1)S(1)} %hidden.1), channel_id=1, replica_groups={{0,32,64,96},{16,48,80,112},{1,33,65,97},{17,49,81,113},{2,34,66,98},{1..., dimensions={0} | all-to-all | bytes 1376256 | tf_op jit(solution)/shard_map/all_to_all | solution.py:206
  80.5 1.9 %collective-permute-start.1 = (bf16[4,3,224,128]{3,2,1,0:T(8,128)(2,1)S(1)}, bf16[4,3,224,128]{3,2,1,0:T(8,128)(2,1)S(1)}, u32[]{:S(2)}, u32[]{:S(2)}) collective-permute-start(bf16[4,3,224,128]{3,2,1,0:T(8,128)(2,1)S(1)} %all_to_all.16.mine), channel_id=1, source_target_pairs={{0,16},{16,0},{32,48},{48,32},{64,80},{80,64},{96,112},{112,96},{1... | collective-permute-start | bytes 2064392 | tf_op jit(solution)/shard_map/ppermute | solution.py:207
  82.4 2.1 %collective-permute-done.1.theirs = bf16[4,3,224,128]{3,2,1,0:T(8,128)(2,1)S(1)} collective-permute-done((bf16[4,3,224,128]{3,2,1,0:T(8,128)(2,1)S(1)}, bf16[4,3,224,128]{3,2,1,0:T(8,128)(2,1)S(1)}, u32[]{:S(2)}, u32[]{:S(2)}) %collective-permute-start.1) | collective-permute-done | bytes 688160 | tf_op jit(solution)/shard_map/ppermute | solution.py:207
  84.5 4.2 %grads.1 = (bf16[3,1792,128]{2,1,0:T(8,128)(2,1)S(1)}, bf16[3,11,32,128]{3,2,1,0:T(8,128)(2,1)S(1)}, bf16[3,11,32,128]{3,2,1,0:T(8,128)(2,1)S(1)}, bf16[3,11,32,...) custom-call(s32[3,2,44]{2,1,0:T(2,128)S(1)} %bitcast.8, s32[3]{0:T(128)S(1)} %bitcast.11, ...), custom_call_target="tpu_custom_call" | custom-call | tf_op jit(solution)/shard_map/grads/pallas_call | solution.py:209
  88.7 3.6 %back.1 = bf16[16,16,1024]{2,1,0:T(8,128)(2,1)} custom-call(s32[3,2,44]{2,1,0:T(2,128)S(1)} %bitcast.9, s32[3]{0:T(128)S(1)} %bitcast.12, bf16[3,1792,128]{2,1,0:T(8,128)(2,1)S(1)} %get-tuple-element.19.band, bf16[44,64,64]{2,1,0:T(8,128)(2,1)S(1)} %reshape.27.gate, bf16[44,64,64]{2,1,0:T(8,128)(2,1)S(1)} %reshape.28.up, bf16[44,64,64]{2,1,0:T(8,128)(2,1)S(1)} %reshape.29.down), custom_call_target="tpu_custom_call" | custom-call | tf_op jit(solution)/shard_map/back/pallas_call | solution.py:216
  92.3 7.7 %all-to-all-start.2 = ((bf16[16,16,1024]{2,1,0:T(8,128)(2,1)}), bf16[16,16,1024]{2,1,0:T(8,128)(2,1)S(1)}, u32[]{:S(2)}, u32[]{:S(2)}) async-start(bf16[16,16,1024]{2,1,0:T(8,128)(2,1)} %back.1), calls=%async_computation.2 | async-start | bytes 1048576 | tf_op jit(solution)/shard_map/all_to_all | solution.py:224
  100.0 5.1 %collective-permute-start.2 = (bf16[3,11,32,128]{3,2,1,0:T(8,128)(2,1)S(1)}, bf16[3,11,32,128]{3,2,1,0:T(8,128)(2,1)S(1)}, u32[]{:S(2)}, u32[]{:S(2)}) collective-permute-start(bf16[3,11,32,128]{3,2,1,0:T(8,128)(2,1)S(1)} %get-tuple-element.21), channel_id=1, source_target_pairs={{0,256},{128,384},{256,0},{384,128},{1,257},{129,385},{257,1},{385... | collective-permute-start | bytes 811016 | tf_op jit(solution)/shard_map/ppermute | solution.py:225
  105.1 2.6 %collective-permute-start.3 = (bf16[3,11,32,128]{3,2,1,0:T(8,128)(2,1)S(1)}, bf16[3,11,32,128]{3,2,1,0:T(8,128)(2,1)S(1)}, u32[]{:S(2)}, u32[]{:S(2)}) collective-permute-start(bf16[3,11,32,128]{3,2,1,0:T(8,128)(2,1)S(1)} %get-tuple-element.22), channel_id=1, source_target_pairs={{0,128},{128,256},{256,384},{384,0},{1,129},{129,257},{257,385},{3... | collective-permute-start | bytes 811016 | tf_op jit(solution)/shard_map/ppermute | solution.py:226
  107.7 4.5 %collective-permute-start.4 = (bf16[3,11,32,128]{3,2,1,0:T(8,128)(2,1)S(1)}, bf16[3,11,32,128]{3,2,1,0:T(8,128)(2,1)S(1)}, u32[]{:S(2)}, u32[]{:S(2)}) collective-permute-start(bf16[3,11,32,128]{3,2,1,0:T(8,128)(2,1)S(1)} %get-tuple-element.23), channel_id=1, source_target_pairs={{0,384},{128,0},{256,128},{384,256},{1,385},{129,1},{257,129},{385... | collective-permute-start | bytes 811016 | tf_op jit(solution)/shard_map/ppermute | solution.py:227
  112.2 0.7 collective-permute-done.2.b
  112.8 5.7 %collective-permute-done.3.c = bf16[3,11,32,128]{3,2,1,0:T(8,128)(2,1)S(1)} collective-permute-done((bf16[3,11,32,128]{3,2,1,0:T(8,128)(2,1)S(1)}, bf16[3,11,32,128]{3,2,1,0:T(8,128)(2,1)S(1)}, u32[]{:S(2)}, u32[]{:S(2)}) %collective-permute-start.3) | collective-permute-done | bytes 270368 | tf_op jit(solution)/shard_map/ppermute | solution.py:226
  118.5 0.3 collective-permute-done.4.d
  118.9 0.1 dp_sum.1.own
  119.0 5.2 %collective-permute-start.6 = (bf16[3,11,32,128]{3,2,1,0:T(8,128)(2,1)S(1)}, bf16[3,11,32,128]{3,2,1,0:T(8,128)(2,1)S(1)}, u32[]{:S(2)}, u32[]{:S(2)}) collective-permute-start(bf16[3,11,32,128]{3,2,1,0:T(8,128)(2,1)S(1)} %dp_sum.1.own), channel_id=1, source_target_pairs={{0,384},{128,0},{256,128},{384,256},{1,385},{129,1},{257,129},{385... | collective-permute-start | bytes 811016 | tf_op jit(solution)/shard_map/ppermute | solution.py:230
  124.2 1.9 %collective-permute-start.5 = (bf16[3,11,32,128]{3,2,1,0:T(8,128)(2,1)S(1)}, bf16[3,11,32,128]{3,2,1,0:T(8,128)(2,1)S(1)}, u32[]{:S(2)}, u32[]{:S(2)}) collective-permute-start(bf16[3,11,32,128]{3,2,1,0:T(8,128)(2,1)S(1)} %dp_sum.1.own), channel_id=1, source_target_pairs={{0,128},{128,256},{256,384},{384,0},{1,129},{129,257},{257,385},{3... | collective-permute-start | bytes 811016 | tf_op jit(solution)/shard_map/ppermute | solution.py:229
  126.1 3.6 %collective-permute-done.6.next_ = bf16[3,11,32,128]{3,2,1,0:T(8,128)(2,1)S(1)} collective-permute-done((bf16[3,11,32,128]{3,2,1,0:T(8,128)(2,1)S(1)}, bf16[3,11,32,128]{3,2,1,0:T(8,128)(2,1)S(1)}, u32[]{:S(2)}, u32[]{:S(2)}) %collective-permute-start.6) | collective-permute-done | bytes 270368 | tf_op jit(solution)/shard_map/ppermute | solution.py:230
  129.8 5.6 %collective-permute-start.8 = (bf16[3,11,16,128]{3,2,1,0:T(8,128)(2,1)S(1)}, bf16[3,11,16,128]{3,2,1,0:T(8,128)(2,1)S(1)}, u32[]{:S(2)}, u32[]{:S(2)}) collective-permute-start(bf16[3,11,16,128]{3,2,1,0:T(8,128)(2,1)S(1)} %slice.19), channel_id=1, source_target_pairs={{0,384},{128,0},{256,128},{384,256},{1,385},{129,1},{257,129},{385... | collective-permute-start | bytes 405512 | tf_op jit(solution)/shard_map/ppermute | solution.py:233
  135.4 0.0 collective-permute-done.5.prev
  135.4 1.9 %collective-permute-start.7 = (bf16[3,11,16,128]{3,2,1,0:T(8,128)(2,1)S(1)}, bf16[3,11,16,128]{3,2,1,0:T(8,128)(2,1)S(1)}, u32[]{:S(2)}, u32[]{:S(2)}) collective-permute-start(bf16[3,11,16,128]{3,2,1,0:T(8,128)(2,1)S(1)} %slice.18), channel_id=1, source_target_pairs={{0,128},{128,256},{256,384},{384,0},{1,129},{129,257},{257,385},{3... | collective-permute-start | bytes 405512 | tf_op jit(solution)/shard_map/ppermute | solution.py:232
  137.3 0.6 collective-permute-done.8.far_high
  137.9 5.6 %collective-permute-done.7.far_low = bf16[3,11,16,128]{3,2,1,0:T(8,128)(2,1)S(1)} collective-permute-done((bf16[3,11,16,128]{3,2,1,0:T(8,128)(2,1)S(1)}, bf16[3,11,16,128]{3,2,1,0:T(8,128)(2,1)S(1)}, u32[]{:S(2)}, u32[]{:S(2)}) %collective-permute-start.7) | collective-permute-done | bytes 135200 | tf_op jit(solution)/shard_map/ppermute | solution.py:232
  143.5 2.6 %unpack.1 = (bf16[44,4096]{1,0:T(8,128)(2,1)}, bf16[44,4096]{1,0:T(8,128)(2,1)}, bf16[44,4096]{1,0:T(8,128)(2,1)}) custom-call(bf16[3,11,32,128]{3,2,1,0:T(8,128)(2,1)S(1)} %dp_sum.1.own, bf16[3,11,32,128]{3,2,1,0:T(8,128)(2,1)S(1)} %collective-permute-done.5.prev, bf16[3,11,32,128]{3,2,1,0:T(8,128)(2,1)S(1)} %collective-permute-done.6.next_, ...), custom_call_target="tpu_custom_call" | custom-call | tf_op jit(solution)/shard_map/unpack/pallas_call | solution.py:235
  146.1 0.0 all-to-all-done.2
  146.1 0.1 reduce_sum.12
  146.2 0.6 fusion
  (2 shorter events, 0.0 us)
Async XLA Ops:
  0.6 41.2 %copy-start.2 = (bf16[1,1,44,4096]{3,2,1,0:T(8,128)(2,1)S(1)}, bf16[1,1,44,4096]{3,2,1,0:T(8,128)(2,1)}, u32[]{:S(2)}) copy-start(bf16[1,1,44,4096]{3,2,1,0:T(8,128)(2,1)} %param.10) | copy-start | bytes 1081348
  1.4 41.2 %copy-start.3 = (bf16[1,1,44,4096]{3,2,1,0:T(8,128)(2,1)S(1)}, bf16[1,1,44,4096]{3,2,1,0:T(8,128)(2,1)}, u32[]{:S(2)}) copy-start(bf16[1,1,44,4096]{3,2,1,0:T(8,128)(2,1)} %param.11) | copy-start | bytes 1081348
  41.8 1.6 %copy-start = (s32[3,1,1,2,44]{4,3,2,1,0:T(2,128)S(1)}, s32[3,1,1,2,44]{4,3,2,1,0:T(2,128)}, u32[]{:S(2)}) copy-start(s32[3,1,1,2,44]{4,3,2,1,0:T(2,128)} %param.12) | copy-start | bytes 3172
  41.8 1.6 %copy-start.1 = (s32[3,1,1]{0,2,1:T(1,128)S(1)}, s32[3,1,1]{0,2,1:T(1,128)}, u32[]{:S(2)}) copy-start(s32[3,1,1]{0,2,1:T(1,128)} %param.13) | copy-start | bytes 40
  47.0 4.0 %collective-permute-start = (bf16[4,3,224,128]{3,2,1,0:T(8,128)(2,1)S(1)}, bf16[4,3,224,128]{3,2,1,0:T(8,128)(2,1)S(1)}, u32[]{:S(2)}, u32[]{:S(2)}) collective-permute-start(bf16[4,3,224,128]{3,2,1,0:T(8,128)(2,1)S(1)} %get-tuple-element.17), channel_id=1, source_target_pairs={{0,16},{16,0},{32,48},{48,32},{64,80},{80,64},{96,112},{112,96},{1... | collective-permute-start | bytes 2064392 | tf_op jit(solution)/shard_map/ppermute | solution.py:202
  80.5 4.0 %collective-permute-start.1 = (bf16[4,3,224,128]{3,2,1,0:T(8,128)(2,1)S(1)}, bf16[4,3,224,128]{3,2,1,0:T(8,128)(2,1)S(1)}, u32[]{:S(2)}, u32[]{:S(2)}) collective-permute-start(bf16[4,3,224,128]{3,2,1,0:T(8,128)(2,1)S(1)} %all_to_all.16.mine), channel_id=1, source_target_pairs={{0,16},{16,0},{32,48},{48,32},{64,80},{80,64},{96,112},{112,96},{1... | collective-permute-start | bytes 2064392 | tf_op jit(solution)/shard_map/ppermute | solution.py:207
  92.3 53.8 %all-to-all-start.2 = ((bf16[16,16,1024]{2,1,0:T(8,128)(2,1)}), bf16[16,16,1024]{2,1,0:T(8,128)(2,1)S(1)}, u32[]{:S(2)}, u32[]{:S(2)}) async-start(bf16[16,16,1024]{2,1,0:T(8,128)(2,1)} %back.1), calls=%async_computation.2 | async-start | bytes 1048576 | tf_op jit(solution)/shard_map/all_to_all | solution.py:224
  100.0 12.8 %collective-permute-start.2 = (bf16[3,11,32,128]{3,2,1,0:T(8,128)(2,1)S(1)}, bf16[3,11,32,128]{3,2,1,0:T(8,128)(2,1)S(1)}, u32[]{:S(2)}, u32[]{:S(2)}) collective-permute-start(bf16[3,11,32,128]{3,2,1,0:T(8,128)(2,1)S(1)} %get-tuple-element.21), channel_id=1, source_target_pairs={{0,256},{128,384},{256,0},{384,128},{1,257},{129,385},{257,1},{385... | collective-permute-start | bytes 811016 | tf_op jit(solution)/shard_map/ppermute | solution.py:225
  105.1 13.4 %collective-permute-start.3 = (bf16[3,11,32,128]{3,2,1,0:T(8,128)(2,1)S(1)}, bf16[3,11,32,128]{3,2,1,0:T(8,128)(2,1)S(1)}, u32[]{:S(2)}, u32[]{:S(2)}) collective-permute-start(bf16[3,11,32,128]{3,2,1,0:T(8,128)(2,1)S(1)} %get-tuple-element.22), channel_id=1, source_target_pairs={{0,128},{128,256},{256,384},{384,0},{1,129},{129,257},{257,385},{3... | collective-permute-start | bytes 811016 | tf_op jit(solution)/shard_map/ppermute | solution.py:226
  107.7 11.2 %collective-permute-start.4 = (bf16[3,11,32,128]{3,2,1,0:T(8,128)(2,1)S(1)}, bf16[3,11,32,128]{3,2,1,0:T(8,128)(2,1)S(1)}, u32[]{:S(2)}, u32[]{:S(2)}) collective-permute-start(bf16[3,11,32,128]{3,2,1,0:T(8,128)(2,1)S(1)} %get-tuple-element.23), channel_id=1, source_target_pairs={{0,384},{128,0},{256,128},{384,256},{1,385},{129,1},{257,129},{385... | collective-permute-start | bytes 811016 | tf_op jit(solution)/shard_map/ppermute | solution.py:227
  119.0 10.7 %collective-permute-start.6 = (bf16[3,11,32,128]{3,2,1,0:T(8,128)(2,1)S(1)}, bf16[3,11,32,128]{3,2,1,0:T(8,128)(2,1)S(1)}, u32[]{:S(2)}, u32[]{:S(2)}) collective-permute-start(bf16[3,11,32,128]{3,2,1,0:T(8,128)(2,1)S(1)} %dp_sum.1.own), channel_id=1, source_target_pairs={{0,384},{128,0},{256,128},{384,256},{1,385},{129,1},{257,129},{385... | collective-permute-start | bytes 811016 | tf_op jit(solution)/shard_map/ppermute | solution.py:230
  124.2 11.1 %collective-permute-start.5 = (bf16[3,11,32,128]{3,2,1,0:T(8,128)(2,1)S(1)}, bf16[3,11,32,128]{3,2,1,0:T(8,128)(2,1)S(1)}, u32[]{:S(2)}, u32[]{:S(2)}) collective-permute-start(bf16[3,11,32,128]{3,2,1,0:T(8,128)(2,1)S(1)} %dp_sum.1.own), channel_id=1, source_target_pairs={{0,128},{128,256},{256,384},{384,0},{1,129},{129,257},{257,385},{3... | collective-permute-start | bytes 811016 | tf_op jit(solution)/shard_map/ppermute | solution.py:229
  129.8 8.1 %collective-permute-start.8 = (bf16[3,11,16,128]{3,2,1,0:T(8,128)(2,1)S(1)}, bf16[3,11,16,128]{3,2,1,0:T(8,128)(2,1)S(1)}, u32[]{:S(2)}, u32[]{:S(2)}) collective-permute-start(bf16[3,11,16,128]{3,2,1,0:T(8,128)(2,1)S(1)} %slice.19), channel_id=1, source_target_pairs={{0,384},{128,0},{256,128},{384,256},{1,385},{129,1},{257,129},{385... | collective-permute-start | bytes 405512 | tf_op jit(solution)/shard_map/ppermute | solution.py:233
  135.4 8.1 %collective-permute-start.7 = (bf16[3,11,16,128]{3,2,1,0:T(8,128)(2,1)S(1)}, bf16[3,11,16,128]{3,2,1,0:T(8,128)(2,1)S(1)}, u32[]{:S(2)}, u32[]{:S(2)}) collective-permute-start(bf16[3,11,16,128]{3,2,1,0:T(8,128)(2,1)S(1)} %slice.18), channel_id=1, source_target_pairs={{0,128},{128,256},{256,384},{384,0},{1,129},{129,257},{257,385},{3... | collective-permute-start | bytes 405512 | tf_op jit(solution)/shard_map/ppermute | solution.py:232

commit v4 on v3

--- a/solution.py
+++ b/solution.py
@@ -81,7 +81,7 @@
             out[j, m] = units[m]
 
 
-def grads_kernel(index, count, mine, theirs, cols, band, own, ahead, across, behind):
+def grads_kernel(index, count, mine, theirs, cols, band, grads):
     core = lax.axis_index("row") % 2
     share = mine.shape[2]
     for x in range(mine.shape[0]):
@@ -89,14 +89,11 @@
             for half, side in ((mine, core), (theirs, 1 - core)):
                 first = pl.multiple_of((2 * x + side) * share, 32)
                 band[m, pl.ds(first, share), :] = half[x, m]
-    outs = (own, ahead, across, behind)
-    n_dp = len(outs)
-    per = own.shape[1]
-    here = lax.axis_index("dp")
+    n_dp, _, per = grads.shape[:3]
 
     def step(p, carry):
-        for away, out in enumerate(outs):
-            s = ((here + away) % n_dp) * per + p
+        for owner in range(n_dp):
+            s = owner * per + p
             for m in range(3):
                 unit = band[m, rows_of(index[m, 1, s]), :]
                 source = cols[m // 2, rows_of(index[m, 0, s]), :]
@@ -105,13 +102,13 @@
                 )
                 grad = jnp.where(s < count[m], grad, 0.0)
                 packed = jnp.concatenate([grad[: BS // 2], grad[BS // 2 :]], axis=1)
-                out[m, p] = packed.astype(BF16)
+                grads[owner, m, p] = packed.astype(BF16)
         return carry
 
     lax.fori_loop(0, per, step, 0)
 
 
-def back_kernel(index, count, band, gate, up, down, rows, out_total, in_total):
+def back_kernel(index, count, band, gate, up, down, keep, give, out_total, in_total):
     out_total[...] = jnp.zeros_like(out_total)
     in_total[...] = jnp.zeros_like(in_total)
     for m, weights in enumerate((gate, up, down)):
@@ -124,17 +121,21 @@
             total[place, :] += jnp.dot(block, unit, preferred_element_type=F32)
 
         for_slots(count[m], step)
-    n_col, pair, width = rows.shape
+    even_here = lax.axis_index("col") % 2 == 0
+    owners, pair, width = keep.shape
     half = pair // 2
     for j in range(0, width, 128):
-        out_piece = out_total[j : j + 128, :].T.reshape(n_col, half, 128)
-        in_piece = in_total[j : j + 128, :].T.reshape(n_col, half, 128)
-        rows[:, :, j : j + 128] = jnp.concatenate([out_piece, in_piece], axis=1).astype(BF16)
-
-
-def dp_sum_kernel(a, b, c, d, out):
+        out_piece = out_total[j : j + 128, :].T.reshape(owners, 2, half, 128)
+        in_piece = in_total[j : j + 128, :].T.reshape(owners, 2, half, 128)
+        piece = jnp.concatenate([out_piece, in_piece], axis=2)
+        even, odd = piece[:, 0], piece[:, 1]
+        keep[:, :, j : j + 128] = jnp.where(even_here, even, odd).astype(BF16)
+        give[:, :, j : j + 128] = jnp.where(even_here, odd, even).astype(BF16)
+
+
+def dp_sum_kernel(terms, out):
     out[...] = (
-        (a[...].astype(F32) + b[...].astype(F32)) + (c[...].astype(F32) + d[...].astype(F32))
+        (terms[0].astype(F32) + terms[1].astype(F32)) + (terms[2].astype(F32) + terms[3].astype(F32))
     ).astype(BF16)
 
 
@@ -206,26 +207,28 @@
     mine = lax.all_to_all(own, "row", 0, 0, axis_index_groups=same_core)
     theirs = lax.ppermute(mine, "row", pair)
     packed = arr(3, slots // n_dp, BS // 2, 2 * BS)
-    band, own, to_next, to_far, to_prev = call(
+    band, grads = call(
         grads_kernel,
         "grads",
-        (arr(3, units, toks),) + (packed,) * n_dp,
+        (arr(3, units, toks), arr(n_dp, *packed.shape)),
         [SMEM] * 2 + [VMEM] * 3,
-        (VMEM,) * (1 + n_dp),
+        (VMEM, VMEM),
     )(index, count, mine, theirs, cols)
-    rows = call(
+    grad_terms = lax.all_to_all(grads, "dp", 0, 0)
+    row_half = arr(n_col // 2, 2 * half, width)
+    keep, give = call(
         back_kernel,
         "back",
-        arr(n_col, 2 * half, width),
+        (row_half, row_half),
         [SMEM] * 2 + [VMEM] * 4,
-        VMEM,
+        (VMEM, VMEM),
         [pltpu.VMEM((width, toks), F32), pltpu.VMEM((width, toks), F32)],
     )(index, count, band, gate, up, down)
-    row_terms = lax.all_to_all(rows, "col", 0, 0)
-    from_far = lax.ppermute(to_far, "dp", across)
-    from_prev = lax.ppermute(to_next, "dp", ahead)
-    from_next = lax.ppermute(to_prev, "dp", behind)
-    own = call(dp_sum_kernel, "dp_sum", packed, [VMEM] * 4, VMEM)(own, from_far, from_prev, from_next)
+    given = lax.ppermute(give, "col", [(i, i ^ 1) for i in range(n_col)])
+    halved = call(pair_sum_kernel, "col_pair_sum", row_half, [VMEM] * 2, VMEM)(keep, given)
+    own = call(dp_sum_kernel, "dp_sum", packed, [VMEM], VMEM)(grad_terms)
+    same_parity = [list(range(p, n_col, 2)) for p in range(2)]
+    row_terms = lax.all_to_all(halved, "col", 0, 0, axis_index_groups=same_parity)
     prev = lax.ppermute(own, "dp", ahead)
     next_ = lax.ppermute(own, "dp", behind)
     cut = BS // 4

time: 147 us -> 146 us (level)
  the two profiles are of different devices: /device:TPU:2 before, /device:TPU:1 now
where the time goes in v4:
time: 146 us; the launch traced here: 144 us
  blocking collectives  58.3 us (40%)
  starting transfers between devices  41.7 us (29%)
  waiting for transfers between devices  18.8 us (13%)
  Pallas kernels  16.4 us (11%)
  local copies, waits for them, and re-layouts  7.36 us (5%)
    all_gather x1, blocking collectives, per_device(): wide = lax.all_gather(both, 'col', axis=0)  31.8 us
    all_to_all x1, blocking collectives, per_device(): summed = lax.all_to_all(paired, 'row', 0, 0, axis_index_groups=same_core)  14.7 us
    all_to_all x1, blocking collectives, per_device(): mine = lax.all_to_all(own, 'row', 0, 0, axis_index_groups=same_core)  11.8 us
    ppermute x1, starting transfers between devices, per_device(): other = lax.ppermute(theirs, 'row', pair)  9.31 us
    ppermute x1, waiting for transfers between devices, per_device(): given = lax.ppermute(give, 'col', [(i, i ^ 1) for i in range(n_col)])  7.9 us
    all_to_all x1, starting transfers between devices, per_device(): lax.all_to_all(halved, 'col', 0, 0, axis_index_groups=same_parity)  7.85 us
    ppermute x1, starting transfers between devices, per_device(): far_high = lax.ppermute(next_[:, :, cut:], 'dp', behind)  5.32 us
    pallas_call x1, Pallas kernels, per_device(): call(spread_kernel, 'spread', (arr(2, width, toks), terms, terms), [SMEM]...  4.83 us
  transfers between devices with their start and end apart: 9, of which 6 were waited for; matrix products, arithmetic and copies ran while one was open for 0% of the time, Pallas kernels for 3%

profile of v4, /device:TPU:1, one launch (start us, length us, event | category | flops | bytes accessed | tf_op | source)
XLA Modules:
  0.0 144.3 jit_solution(12768412902390871459)
XLA Ops:
  0.6 0.0 copy-start.5
  0.6 0.8 pad_maximum_fusion
  1.4 31.8 %all-gather = bf16[256,1024]{1,0:T(8,128)(2,1)S(1)} all-gather(bf16[16,1024]{1,0:T(8,128)(2,1)S(1)} %pad_maximum_fusion), channel_id=2, replica_groups=mesh['dp'=4,'row'=8,'col'=16] {'col'}, dimensions={0}, use_global_device_ids=true | all-gather | bytes 557056 | tf_op jit(solution)/shard_map/all_gather | solution.py:193
  33.2 0.0 copy-start.6
  33.2 1.8 %reshape.27.gate = bf16[44,64,64]{2,1,0:T(8,128)(2,1)S(1)} reshape(bf16[1,1,44,4096]{3,2,1,0:T(8,128)(2,1)} %param.9) | data formatting | bytes 720896 | tf_op jit(solution)/shard_map/reshape | solution.py:184
  35.0 0.0 copy-done.5
  35.0 0.0 copy-start.3
  35.0 0.0 copy-start.4
  35.0 0.8 reshape.28.up
  35.8 0.0 copy-done.6
  35.8 0.8 reshape.29.down
  36.6 0.0 copy-done.3
  36.6 0.0 copy-done.4
  36.6 4.8 %spread.1 = (bf16[2,1024,128]{2,1,0:T(8,128)(2,1)S(1)}, bf16[4,3,224,128]{3,2,1,0:T(8,128)(2,1)S(1)}, bf16[4,3,224,128]{3,2,1,0:T(8,128)(2,1)S(1)}) custom-call(s32[3,2,44]{2,1,0:T(2,128)S(1)} %bitcast.7, s32[3]{0:T(128)S(1)} %bitcast.10, bf16[16,16,1024]{2,1,0:T(8,128)(2,1)S(1)} %bitcast.6, bf16[44,64,64]{2,1,0:T(8,128)(2,1)S(1)} %reshape.27.gate, ...), custom_call_target="tpu_custom_call" | custom-call | tf_op jit(solution)/shard_map/spread/pallas_call | solution.py:195
  41.4 9.3 %collective-permute-start = (bf16[4,3,224,128]{3,2,1,0:T(8,128)(2,1)S(1)}, bf16[4,3,224,128]{3,2,1,0:T(8,128)(2,1)S(1)}, u32[]{:S(2)}, u32[]{:S(2)}) collective-permute-start(bf16[4,3,224,128]{3,2,1,0:T(8,128)(2,1)S(1)} %get-tuple-element.16), channel_id=1, source_target_pairs={{0,16},{16,0},{32,48},{48,32},{64,80},{80,64},{96,112},{112,96},{1... | collective-permute-start | bytes 2064392 | tf_op jit(solution)/shard_map/ppermute | solution.py:203
  50.8 1.7 %collective-permute-done.other = bf16[4,3,224,128]{3,2,1,0:T(8,128)(2,1)S(1)} collective-permute-done((bf16[4,3,224,128]{3,2,1,0:T(8,128)(2,1)S(1)}, bf16[4,3,224,128]{3,2,1,0:T(8,128)(2,1)S(1)}, u32[]{:S(2)}, u32[]{:S(2)}) %collective-permute-start) | collective-permute-done | bytes 688160 | tf_op jit(solution)/shard_map/ppermute | solution.py:203
  52.5 0.2 pair_sum.1
  52.7 14.7 %all_to_all.20.terms = bf16[4,3,224,128]{3,2,1,0:T(8,128)(2,1)S(1)} all-to-all(bf16[4,3,224,128]{3,2,1,0:T(8,128)(2,1)S(1)} %pair_sum.1), channel_id=1, replica_groups={{0,32,64,96},{16,48,80,112},{1,33,65,97},{17,49,81,113},{2,34,66,98},{1..., dimensions={0} | all-to-all | bytes 1376256 | tf_op jit(solution)/shard_map/all_to_all | solution.py:205
  67.4 0.1 hidden.1
  67.5 11.8 %all_to_all.21.mine = bf16[4,3,224,128]{3,2,1,0:T(8,128)(2,1)S(1)} all-to-all(bf16[4,3,224,128]{3,2,1,0:T(8,128)(2,1)S(1)} %hidden.1), channel_id=1, replica_groups={{0,32,64,96},{16,48,80,112},{1,33,65,97},{17,49,81,113},{2,34,66,98},{1..., dimensions={0} | all-to-all | bytes 1376256 | tf_op jit(solution)/shard_map/all_to_all | solution.py:207
  79.3 4.6 %collective-permute-start.1 = (bf16[4,3,224,128]{3,2,1,0:T(8,128)(2,1)S(1)}, bf16[4,3,224,128]{3,2,1,0:T(8,128)(2,1)S(1)}, u32[]{:S(2)}, u32[]{:S(2)}) collective-permute-start(bf16[4,3,224,128]{3,2,1,0:T(8,128)(2,1)S(1)} %all_to_all.21.mine), channel_id=1, source_target_pairs={{0,16},{16,0},{32,48},{48,32},{64,80},{80,64},{96,112},{112,96},{1... | collective-permute-start | bytes 2064392 | tf_op jit(solution)/shard_map/ppermute | solution.py:208
  84.0 1.7 %collective-permute-done.1.theirs = bf16[4,3,224,128]{3,2,1,0:T(8,128)(2,1)S(1)} collective-permute-done((bf16[4,3,224,128]{3,2,1,0:T(8,128)(2,1)S(1)}, bf16[4,3,224,128]{3,2,1,0:T(8,128)(2,1)S(1)}, u32[]{:S(2)}, u32[]{:S(2)}) %collective-permute-start.1) | collective-permute-done | bytes 688160 | tf_op jit(solution)/shard_map/ppermute | solution.py:208
  85.7 4.1 %grads.1 = (bf16[3,1792,128]{2,1,0:T(8,128)(2,1)S(1)}, bf16[4,3,11,32,128]{4,3,2,1,0:T(8,128)(2,1)S(1)}) custom-call(s32[3,2,44]{2,1,0:T(2,128)S(1)} %bitcast.8, s32[3]{0:T(128)S(1)} %bitcast.11, bf16[4,3,224,128]{3,2,1,0:T(8,128)(2,1)S(1)} %all_to_all.21.mine, bf16[4,3,224,128]{3,2,1,0:T(8,128)(2,1)S(1)} %collective-permute-done.1.theirs, ...), custom_call_target="tpu_custom_call" | custom-call | tf_op jit(solution)/shard_map/grads/pallas_call | solution.py:210
  89.8 0.0 copy-start
  89.8 1.1 copy-done
  90.9 0.0 copy-start.2
  90.9 1.0 copy-done.2
  91.9 4.2 %all-to-all-start.3 = ((bf16[4,3,11,32,128]{4,3,2,1,0:T(8,128)(2,1)}), bf16[4,3,11,32,128]{4,3,2,1,0:T(8,128)(2,1)S(1)}, u32[]{:S(2)}, u32[]{:S(2)}) async-start(bf16[4,3,11,32,128]{4,3,2,1,0:T(8,128)(2,1)} %copy-done.2), calls=%async_computation.3 | async-start | bytes 2162688 | tf_op jit(solution)/shard_map/all_to_all | solution.py:217
  96.1 0.0 copy-start.1
  96.1 1.3 copy-done.1
  97.4 3.7 %back.1 = (bf16[8,16,1024]{2,1,0:T(8,128)(2,1)S(1)}, bf16[8,16,1024]{2,1,0:T(8,128)(2,1)S(1)}) custom-call(s32[3,2,44]{2,1,0:T(2,128)S(1)} %bitcast.9, s32[3]{0:T(128)S(1)} %bitcast.12, bf16[3,1792,128]{2,1,0:T(8,128)(2,1)S(1)} %copy-done.1, bf16[44,64,64]{2,1,0:T(8,128)(2,1)S(1)} %reshape.27.gate, bf16[44,64,64]{2,1,0:T(8,128)(2,1)S(1)} %reshape.28.up, ...), custom_call_target="tpu_custom_call" | custom-call | tf_op jit(solution)/shard_map/back/pallas_call | solution.py:219
  101.1 1.9 %collective-permute-start.2 = (bf16[8,16,1024]{2,1,0:T(8,128)(2,1)S(1)}, bf16[8,16,1024]{2,1,0:T(8,128)(2,1)S(1)}, u32[]{:S(2)}, u32[]{:S(2)}) collective-permute-start(bf16[8,16,1024]{2,1,0:T(8,128)(2,1)S(1)} %get-tuple-element.20), channel_id=1, source_target_pairs={{0,1},{1,0},{2,3},{3,2},{4,5},{5,4},{6,7},{7,6},{8,9},{9,8},{10,11... | collective-permute-start | bytes 786440 | tf_op jit(solution)/shard_map/ppermute | solution.py:227
  103.1 7.9 %collective-permute-done.2.other = bf16[8,16,1024]{2,1,0:T(8,128)(2,1)S(1)} collective-permute-done((bf16[8,16,1024]{2,1,0:T(8,128)(2,1)S(1)}, bf16[8,16,1024]{2,1,0:T(8,128)(2,1)S(1)}, u32[]{:S(2)}, u32[]{:S(2)}) %collective-permute-start.2) | collective-permute-done | bytes 262176 | tf_op jit(solution)/shard_map/ppermute | solution.py:227
  111.0 0.8 col_pair_sum.1
  111.7 0.0 all-to-all-done.3.terms
  111.7 7.8 %all-to-all-start.2 = ((bf16[8,16,1024]{2,1,0:T(8,128)(2,1)}), bf16[8,16,1024]{2,1,0:T(8,128)(2,1)S(1)}, u32[]{:S(2)}, u32[]{:S(2)}) async-start(bf16[8,16,1024]{2,1,0:T(8,128)(2,1)} %col_pair_sum.1), calls=%async_computation.2 | async-start | bytes 524288 | tf_op jit(solution)/shard_map/all_to_all | solution.py:231
  119.6 0.1 dp_sum.1.own
  119.7 4.6 %collective-permute-start.4 = (bf16[3,11,32,128]{3,2,1,0:T(8,128)(2,1)S(1)}, bf16[3,11,32,128]{3,2,1,0:T(8,128)(2,1)S(1)}, u32[]{:S(2)}, u32[]{:S(2)}) collective-permute-start(bf16[3,11,32,128]{3,2,1,0:T(8,128)(2,1)S(1)} %dp_sum.1.own), channel_id=1, source_target_pairs={{0,384},{128,0},{256,128},{384,256},{1,385},{129,1},{257,129},{385... | collective-permute-start | bytes 811016 | tf_op jit(solution)/shard_map/ppermute | solution.py:233
  124.3 1.9 %collective-permute-start.3 = (bf16[3,11,32,128]{3,2,1,0:T(8,128)(2,1)S(1)}, bf16[3,11,32,128]{3,2,1,0:T(8,128)(2,1)S(1)}, u32[]{:S(2)}, u32[]{:S(2)}) collective-permute-start(bf16[3,11,32,128]{3,2,1,0:T(8,128)(2,1)S(1)} %dp_sum.1.own), channel_id=1, source_target_pairs={{0,128},{128,256},{256,384},{384,0},{1,129},{129,257},{257,385},{3... | collective-permute-start | bytes 811016 | tf_op jit(solution)/shard_map/ppermute | solution.py:232
  126.3 3.1 %collective-permute-done.4.next_ = bf16[3,11,32,128]{3,2,1,0:T(8,128)(2,1)S(1)} collective-permute-done((bf16[3,11,32,128]{3,2,1,0:T(8,128)(2,1)S(1)}, bf16[3,11,32,128]{3,2,1,0:T(8,128)(2,1)S(1)}, u32[]{:S(2)}, u32[]{:S(2)}) %collective-permute-start.4) | collective-permute-done | bytes 270368 | tf_op jit(solution)/shard_map/ppermute | solution.py:233
  129.3 5.3 %collective-permute-start.6 = (bf16[3,11,16,128]{3,2,1,0:T(8,128)(2,1)S(1)}, bf16[3,11,16,128]{3,2,1,0:T(8,128)(2,1)S(1)}, u32[]{:S(2)}, u32[]{:S(2)}) collective-permute-start(bf16[3,11,16,128]{3,2,1,0:T(8,128)(2,1)S(1)} %slice.19), channel_id=1, source_target_pairs={{0,384},{128,0},{256,128},{384,256},{1,385},{129,1},{257,129},{385... | collective-permute-start | bytes 405512 | tf_op jit(solution)/shard_map/ppermute | solution.py:236
  134.7 0.0 collective-permute-done.3.prev
  134.7 1.9 %collective-permute-start.5 = (bf16[3,11,16,128]{3,2,1,0:T(8,128)(2,1)S(1)}, bf16[3,11,16,128]{3,2,1,0:T(8,128)(2,1)S(1)}, u32[]{:S(2)}, u32[]{:S(2)}) collective-permute-start(bf16[3,11,16,128]{3,2,1,0:T(8,128)(2,1)S(1)} %slice.18), channel_id=1, source_target_pairs={{0,128},{128,256},{256,384},{384,0},{1,129},{129,257},{257,385},{3... | collective-permute-start | bytes 405512 | tf_op jit(solution)/shard_map/ppermute | solution.py:235
  136.6 3.2 %all-to-all-done.2 = bf16[8,16,1024]{2,1,0:T(8,128)(2,1)S(1)} async-done(((bf16[8,16,1024]{2,1,0:T(8,128)(2,1)}), bf16[8,16,1024]{2,1,0:T(8,128)(2,1)S(1)}, u32[]{:S(2)}, u32[]{:S(2)}) %all-to-all-start.2) | async-done | bytes 262176 | tf_op jit(solution)/shard_map/all_to_all | solution.py:231
  139.9 0.6 fusion
  140.5 0.0 collective-permute-done.6.far_high
  140.5 1.2 collective-permute-done.5.far_low
  141.7 2.6 %unpack.1 = (bf16[44,4096]{1,0:T(8,128)(2,1)}, bf16[44,4096]{1,0:T(8,128)(2,1)}, bf16[44,4096]{1,0:T(8,128)(2,1)}) custom-call(bf16[3,11,32,128]{3,2,1,0:T(8,128)(2,1)S(1)} %dp_sum.1.own, bf16[3,11,32,128]{3,2,1,0:T(8,128)(2,1)S(1)} %collective-permute-done.3.prev, bf16[3,11,32,128]{3,2,1,0:T(8,128)(2,1)S(1)} %collective-permute-done.4.next_, ...), custom_call_target="tpu_custom_call" | custom-call | tf_op jit(solution)/shard_map/unpack/pallas_call | solution.py:238
  (3 shorter events, 0.1 us)
Async XLA Ops:
  0.6 34.4 %copy-start.5 = (bf16[1,1,44,4096]{3,2,1,0:T(8,128)(2,1)S(1)}, bf16[1,1,44,4096]{3,2,1,0:T(8,128)(2,1)}, u32[]{:S(2)}) copy-start(bf16[1,1,44,4096]{3,2,1,0:T(8,128)(2,1)} %param.10) | copy-start | bytes 1081348
  33.2 2.6 %copy-start.6 = (bf16[1,1,44,4096]{3,2,1,0:T(8,128)(2,1)S(1)}, bf16[1,1,44,4096]{3,2,1,0:T(8,128)(2,1)}, u32[]{:S(2)}) copy-start(bf16[1,1,44,4096]{3,2,1,0:T(8,128)(2,1)} %param.11) | copy-start | bytes 1081348
  35.0 1.6 %copy-start.3 = (s32[3,1,1,2,44]{4,3,2,1,0:T(2,128)S(1)}, s32[3,1,1,2,44]{4,3,2,1,0:T(2,128)}, u32[]{:S(2)}) copy-start(s32[3,1,1,2,44]{4,3,2,1,0:T(2,128)} %param.12) | copy-start | bytes 3172
  35.0 1.6 %copy-start.4 = (s32[3,1,1]{0,2,1:T(1,128)S(1)}, s32[3,1,1]{0,2,1:T(1,128)}, u32[]{:S(2)}) copy-start(s32[3,1,1]{0,2,1:T(1,128)} %param.13) | copy-start | bytes 40
  41.4 11.1 %collective-permute-start = (bf16[4,3,224,128]{3,2,1,0:T(8,128)(2,1)S(1)}, bf16[4,3,224,128]{3,2,1,0:T(8,128)(2,1)S(1)}, u32[]{:S(2)}, u32[]{:S(2)}) collective-permute-start(bf16[4,3,224,128]{3,2,1,0:T(8,128)(2,1)S(1)} %get-tuple-element.16), channel_id=1, source_target_pairs={{0,16},{16,0},{32,48},{48,32},{64,80},{80,64},{96,112},{112,96},{1... | collective-permute-start | bytes 2064392 | tf_op jit(solution)/shard_map/ppermute | solution.py:203
  79.3 6.4 %collective-permute-start.1 = (bf16[4,3,224,128]{3,2,1,0:T(8,128)(2,1)S(1)}, bf16[4,3,224,128]{3,2,1,0:T(8,128)(2,1)S(1)}, u32[]{:S(2)}, u32[]{:S(2)}) collective-permute-start(bf16[4,3,224,128]{3,2,1,0:T(8,128)(2,1)S(1)} %all_to_all.21.mine), channel_id=1, source_target_pairs={{0,16},{16,0},{32,48},{48,32},{64,80},{80,64},{96,112},{112,96},{1... | collective-permute-start | bytes 2064392 | tf_op jit(solution)/shard_map/ppermute | solution.py:208
  89.8 1.1 copy-start
  90.9 1.0 copy-start.2
  91.9 19.9 %all-to-all-start.3 = ((bf16[4,3,11,32,128]{4,3,2,1,0:T(8,128)(2,1)}), bf16[4,3,11,32,128]{4,3,2,1,0:T(8,128)(2,1)S(1)}, u32[]{:S(2)}, u32[]{:S(2)}) async-start(bf16[4,3,11,32,128]{4,3,2,1,0:T(8,128)(2,1)} %copy-done.2), calls=%async_computation.3 | async-start | bytes 2162688 | tf_op jit(solution)/shard_map/all_to_all | solution.py:217
  96.1 1.3 copy-start.1
  101.1 9.8 %collective-permute-start.2 = (bf16[8,16,1024]{2,1,0:T(8,128)(2,1)S(1)}, bf16[8,16,1024]{2,1,0:T(8,128)(2,1)S(1)}, u32[]{:S(2)}, u32[]{:S(2)}) collective-permute-start(bf16[8,16,1024]{2,1,0:T(8,128)(2,1)S(1)} %get-tuple-element.20), channel_id=1, source_target_pairs={{0,1},{1,0},{2,3},{3,2},{4,5},{5,4},{6,7},{7,6},{8,9},{9,8},{10,11... | collective-permute-start | bytes 786440 | tf_op jit(solution)/shard_map/ppermute | solution.py:227
  111.7 28.1 %all-to-all-start.2 = ((bf16[8,16,1024]{2,1,0:T(8,128)(2,1)}), bf16[8,16,1024]{2,1,0:T(8,128)(2,1)S(1)}, u32[]{:S(2)}, u32[]{:S(2)}) async-start(bf16[8,16,1024]{2,1,0:T(8,128)(2,1)} %col_pair_sum.1), calls=%async_computation.2 | async-start | bytes 524288 | tf_op jit(solution)/shard_map/all_to_all | solution.py:231
  119.7 9.6 %collective-permute-start.4 = (bf16[3,11,32,128]{3,2,1,0:T(8,128)(2,1)S(1)}, bf16[3,11,32,128]{3,2,1,0:T(8,128)(2,1)S(1)}, u32[]{:S(2)}, u32[]{:S(2)}) collective-permute-start(bf16[3,11,32,128]{3,2,1,0:T(8,128)(2,1)S(1)} %dp_sum.1.own), channel_id=1, source_target_pairs={{0,384},{128,0},{256,128},{384,256},{1,385},{129,1},{257,129},{385... | collective-permute-start | bytes 811016 | tf_op jit(solution)/shard_map/ppermute | solution.py:233
  124.3 10.3 %collective-permute-start.3 = (bf16[3,11,32,128]{3,2,1,0:T(8,128)(2,1)S(1)}, bf16[3,11,32,128]{3,2,1,0:T(8,128)(2,1)S(1)}, u32[]{:S(2)}, u32[]{:S(2)}) collective-permute-start(bf16[3,11,32,128]{3,2,1,0:T(8,128)(2,1)S(1)} %dp_sum.1.own), channel_id=1, source_target_pairs={{0,128},{128,256},{256,384},{384,0},{1,129},{129,257},{257,385},{3... | collective-permute-start | bytes 811016 | tf_op jit(solution)/shard_map/ppermute | solution.py:232
  129.3 11.2 %collective-permute-start.6 = (bf16[3,11,16,128]{3,2,1,0:T(8,128)(2,1)S(1)}, bf16[3,11,16,128]{3,2,1,0:T(8,128)(2,1)S(1)}, u32[]{:S(2)}, u32[]{:S(2)}) collective-permute-start(bf16[3,11,16,128]{3,2,1,0:T(8,128)(2,1)S(1)} %slice.19), channel_id=1, source_target_pairs={{0,384},{128,0},{256,128},{384,256},{1,385},{129,1},{257,129},{385... | collective-permute-start | bytes 405512 | tf_op jit(solution)/shard_map/ppermute | solution.py:236
  134.7 7.0 %collective-permute-start.5 = (bf16[3,11,16,128]{3,2,1,0:T(8,128)(2,1)S(1)}, bf16[3,11,16,128]{3,2,1,0:T(8,128)(2,1)S(1)}, u32[]{:S(2)}, u32[]{:S(2)}) collective-permute-start(bf16[3,11,16,128]{3,2,1,0:T(8,128)(2,1)S(1)} %slice.18), channel_id=1, source_target_pairs={{0,128},{128,256},{256,384},{384,0},{1,129},{129,257},{257,385},{3... | collective-permute-start | bytes 405512 | tf_op jit(solution)/shard_map/ppermute | solution.py:235

commit v5 on v3

--- a/solution.py
+++ b/solution.py
@@ -7,6 +7,7 @@
 
 BS = 64
 UNROLL = 4
+REST = 8
 VMEM = pl.BlockSpec(memory_space=pltpu.VMEM)
 SMEM = pl.BlockSpec(memory_space=pltpu.SMEM)
 PARAMS = pltpu.CompilerParams(vmem_limit_bytes=40 * 1024 * 1024)
@@ -91,24 +92,29 @@
                 band[m, pl.ds(first, share), :] = half[x, m]
     outs = (own, ahead, across, behind)
     n_dp = len(outs)
-    per = own.shape[1]
+    rest = REST
+    per = own.shape[0] - rest
+    slots = index.shape[2]
     here = lax.axis_index("dp")
+
+    def packed(q):
+        m, s = q // slots, q % slots
+        unit = band[m, rows_of(index[m, 1, s]), :]
+        source = cols[m // 2, rows_of(index[m, 0, s]), :]
+        grad = lax.dot_general(source, unit, (((1,), (1,)), ((), ())), preferred_element_type=F32)
+        grad = jnp.where(s < count[m], grad, 0.0)
+        return jnp.concatenate([grad[: BS // 2], grad[BS // 2 :]], axis=1).astype(BF16)
 
     def step(p, carry):
         for away, out in enumerate(outs):
-            s = ((here + away) % n_dp) * per + p
-            for m in range(3):
-                unit = band[m, rows_of(index[m, 1, s]), :]
-                source = cols[m // 2, rows_of(index[m, 0, s]), :]
-                grad = lax.dot_general(
-                    source, unit, (((1,), (1,)), ((), ())), preferred_element_type=F32
-                )
-                grad = jnp.where(s < count[m], grad, 0.0)
-                packed = jnp.concatenate([grad[: BS // 2], grad[BS // 2 :]], axis=1)
-                out[m, p] = packed.astype(BF16)
+            out[p] = packed(((here + away) % n_dp) * per + p)
         return carry
 
-    lax.fori_loop(0, per, step, 0)
+    lax.fori_loop(0, per, step, 0, unroll=2)
+    for p in range(rest):
+        left = packed(n_dp * per + p)
+        for out in outs:
+            out[per + p] = left
 
 
 def back_kernel(index, count, band, gate, up, down, rows, out_total, in_total):
@@ -132,27 +138,28 @@
         rows[:, :, j : j + 128] = jnp.concatenate([out_piece, in_piece], axis=1).astype(BF16)
 
 
-def dp_sum_kernel(a, b, c, d, out):
-    out[...] = (
-        (a[...].astype(F32) + b[...].astype(F32)) + (c[...].astype(F32) + d[...].astype(F32))
-    ).astype(BF16)
-
-
-def unpack_kernel(own, prev, next_, far_low, far_high, gate, up, down, flat):
-    n_dp = 4
-    _, per, depth, lanes = own.shape
-    slots = n_dp * per
-    here = lax.axis_index("dp")
+def dp_sum_kernel(here, far, prev, next_, own, rest):
+    total = (here[...].astype(F32) + far[...].astype(F32)) + (
+        prev[...].astype(F32) + next_[...].astype(F32)
+    )
+    own[...] = total[: own.shape[0]].astype(BF16)
+    rest[...] = total[own.shape[0] :].astype(BF16)
+
+
+def unpack_kernel(owned, rest, gate, up, down, flat):
+    n_dp, per, depth, lanes = owned.shape
+    slots = gate.shape[0]
     low = lax.broadcasted_iota(jnp.int32, (slots, lanes), 1) < BS
+    for g in range(n_dp):
+        flat[g * per * depth : (g + 1) * per * depth, :] = (
+            owned[g].astype(F32).reshape(per * depth, lanes)
+        )
+    flat[n_dp * per * depth :, :] = rest[...].astype(F32).reshape(-1, lanes)
     for m, out in enumerate((gate, up, down)):
-        for away, piece in ((0, own[m]), (3, prev[m]), (1, next_[m]), (2, None)):
-            if piece is None:
-                piece = jnp.concatenate([far_low[m], far_high[m]], axis=1)
-            first = pl.multiple_of(((here + away) % n_dp) * per * depth, 32)
-            flat[pl.ds(first, per * depth), :] = piece.astype(F32).reshape(per * depth, lanes)
+        base = m * slots * depth
         for k in range(0, depth, 2):
-            even = flat[pl.ds(k, slots, stride=depth), :]
-            odd = flat[pl.ds(k + 1, slots, stride=depth), :]
+            even = flat[pl.ds(base + k, slots, stride=depth), :]
+            odd = flat[pl.ds(base + k + 1, slots, stride=depth), :]
             out[:, k * BS : k * BS + lanes] = jnp.where(low, even, pltpu.roll(odd, BS, 1)).astype(BF16)
             start = (depth + k) * BS
             out[:, start : start + lanes] = jnp.where(low, pltpu.roll(even, BS, 1), odd).astype(BF16)
@@ -205,7 +212,8 @@
     own = call(hidden_kernel, "hidden", terms, [VMEM], VMEM)(summed)
     mine = lax.all_to_all(own, "row", 0, 0, axis_index_groups=same_core)
     theirs = lax.ppermute(mine, "row", pair)
-    packed = arr(3, slots // n_dp, BS // 2, 2 * BS)
+    per = (3 * slots - REST) // n_dp
+    packed = arr(per + REST, BS // 2, 2 * BS)
     band, own, to_next, to_far, to_prev = call(
         grads_kernel,
         "grads",
@@ -225,21 +233,23 @@
     from_far = lax.ppermute(to_far, "dp", across)
     from_prev = lax.ppermute(to_next, "dp", ahead)
     from_next = lax.ppermute(to_prev, "dp", behind)
-    own = call(dp_sum_kernel, "dp_sum", packed, [VMEM] * 4, VMEM)(own, from_far, from_prev, from_next)
-    prev = lax.ppermute(own, "dp", ahead)
-    next_ = lax.ppermute(own, "dp", behind)
-    cut = BS // 4
-    far_low = lax.ppermute(prev[:, :, :cut], "dp", ahead)
-    far_high = lax.ppermute(next_[:, :, cut:], "dp", behind)
+    own, rest = call(
+        dp_sum_kernel,
+        "dp_sum",
+        (arr(per, BS // 2, 2 * BS), arr(REST, BS // 2, 2 * BS)),
+        [VMEM] * 4,
+        (VMEM,) * 2,
+    )(own, from_far, from_prev, from_next)
+    owned = lax.all_gather(own, "dp", axis=0)
     flat = arr(slots, BS * BS)
     block_grads = call(
         unpack_kernel,
         "unpack",
         (flat, flat, flat),
-        [VMEM] * 5,
+        [VMEM] * 2,
         (VMEM,) * 3,
-        [pltpu.VMEM((slots * BS // 2, 2 * BS), F32)],
-    )(own, prev, next_, far_low, far_high)
+        [pltpu.VMEM((3 * slots * BS // 2, 2 * BS), F32)],
+    )(owned, rest)
     row_sum = jnp.sum(row_terms.astype(F32), axis=0).astype(BF16)
     return (row_sum[:half], row_sum[half:], *(b[None, None] for b in block_grads))
 

time: 147 us -> 142 us (0.966)
  the two profiles are of different devices: /device:TPU:2 before, /device:TPU:1 now
where the time goes in v5:
time: 142 us; the launch traced here: 141 us
  blocking collectives  73.1 us (51%)
  starting transfers between devices  31.1 us (22%)
  Pallas kernels  19.2 us (14%)
  waiting for transfers between devices  11.7 us (8%)
  local copies, waits for them, and re-layouts  3.88 us (3%)
    all_gather x1, blocking collectives, per_device(): wide = lax.all_gather(both, 'col', axis=0)  31.9 us
    all_to_all x1, blocking collectives, per_device(): summed = lax.all_to_all(paired, 'row', 0, 0, axis_index_groups=same_core)  15.9 us
    all_gather x1, blocking collectives, per_device(): owned = lax.all_gather(own, 'dp', axis=0)  13.5 us
    all_to_all x1, blocking collectives, per_device(): mine = lax.all_to_all(own, 'row', 0, 0, axis_index_groups=same_core)  11.8 us
    ppermute x1, starting transfers between devices, per_device(): other = lax.ppermute(theirs, 'row', pair)  9.11 us
    ppermute x1, waiting for transfers between devices, per_device(): from_prev = lax.ppermute(to_next, 'dp', ahead)  7.88 us
    all_to_all x1, starting transfers between devices, per_device(): row_terms = lax.all_to_all(rows, 'col', 0, 0)  6.05 us
    pallas_call x1, Pallas kernels, per_device(): call(grads_kernel, 'grads', (arr(3, units, toks),) + (packed,) * n_dp, [S...  6.02 us
  transfers between devices with their start and end apart: 6, of which 4 were waited for; matrix products, arithmetic and copies ran while one was open for 0% of the time, Pallas kernels for 2%

profile of v5, /device:TPU:1, one launch (start us, length us, event | category | flops | bytes accessed | tf_op | source)
XLA Modules:
  0.0 140.6 jit_solution(190010109235085307)
XLA Ops:
  0.6 0.0 copy-start.2
  0.6 0.8 pad_maximum_fusion
  1.4 0.0 copy-start.3
  1.4 31.9 %all-gather = bf16[256,1024]{1,0:T(8,128)(2,1)S(1)} all-gather(bf16[16,1024]{1,0:T(8,128)(2,1)S(1)} %pad_maximum_fusion), channel_id=2, replica_groups=mesh['dp'=4,'row'=8,'col'=16] {'col'}, dimensions={0}, use_global_device_ids=true | all-gather | bytes 557056 | tf_op jit(solution)/shard_map/all_gather | solution.py:199
  33.4 1.7 %reshape.27.gate = bf16[44,64,64]{2,1,0:T(8,128)(2,1)S(1)} reshape(bf16[1,1,44,4096]{3,2,1,0:T(8,128)(2,1)} %param.9) | data formatting | bytes 720896 | tf_op jit(solution)/shard_map/reshape | solution.py:190
  35.1 0.0 copy-done.2
  35.1 0.0 copy-start
  35.1 0.0 copy-start.1
  35.1 0.8 reshape.28.up
  35.9 0.0 copy-done.3
  35.9 0.8 reshape.29.down
  36.7 0.0 copy-done
  36.7 0.0 copy-done.1
  36.7 5.2 %spread.1 = (bf16[2,1024,128]{2,1,0:T(8,128)(2,1)S(1)}, bf16[4,3,224,128]{3,2,1,0:T(8,128)(2,1)S(1)}, bf16[4,3,224,128]{3,2,1,0:T(8,128)(2,1)S(1)}) custom-call(s32[3,2,44]{2,1,0:T(2,128)S(1)} %bitcast.9, s32[3]{0:T(128)S(1)} %bitcast.12, bf16[16,16,1024]{2,1,0:T(8,128)(2,1)S(1)} %bitcast.8, bf16[44,64,64]{2,1,0:T(8,128)(2,1)S(1)} %reshape.27.gate, ...), custom_call_target="tpu_custom_call" | custom-call | tf_op jit(solution)/shard_map/spread/pallas_call | solution.py:201
  41.9 9.1 %collective-permute-start = (bf16[4,3,224,128]{3,2,1,0:T(8,128)(2,1)S(1)}, bf16[4,3,224,128]{3,2,1,0:T(8,128)(2,1)S(1)}, u32[]{:S(2)}, u32[]{:S(2)}) collective-permute-start(bf16[4,3,224,128]{3,2,1,0:T(8,128)(2,1)S(1)} %get-tuple-element.19), channel_id=1, source_target_pairs={{0,16},{16,0},{32,48},{48,32},{64,80},{80,64},{96,112},{112,96},{1... | collective-permute-start | bytes 2064392 | tf_op jit(solution)/shard_map/ppermute | solution.py:209
  51.0 1.7 %collective-permute-done.other = bf16[4,3,224,128]{3,2,1,0:T(8,128)(2,1)S(1)} collective-permute-done((bf16[4,3,224,128]{3,2,1,0:T(8,128)(2,1)S(1)}, bf16[4,3,224,128]{3,2,1,0:T(8,128)(2,1)S(1)}, u32[]{:S(2)}, u32[]{:S(2)}) %collective-permute-start) | collective-permute-done | bytes 688160 | tf_op jit(solution)/shard_map/ppermute | solution.py:209
  52.8 0.2 pair_sum.1
  53.0 15.9 %all_to_all.15.terms = bf16[4,3,224,128]{3,2,1,0:T(8,128)(2,1)S(1)} all-to-all(bf16[4,3,224,128]{3,2,1,0:T(8,128)(2,1)S(1)} %pair_sum.1), channel_id=1, replica_groups={{0,32,64,96},{16,48,80,112},{1,33,65,97},{17,49,81,113},{2,34,66,98},{1..., dimensions={0} | all-to-all | bytes 1376256 | tf_op jit(solution)/shard_map/all_to_all | solution.py:211
  68.9 0.1 hidden.1
  69.0 11.8 %all_to_all.16.mine = bf16[4,3,224,128]{3,2,1,0:T(8,128)(2,1)S(1)} all-to-all(bf16[4,3,224,128]{3,2,1,0:T(8,128)(2,1)S(1)} %hidden.1), channel_id=1, replica_groups={{0,32,64,96},{16,48,80,112},{1,33,65,97},{17,49,81,113},{2,34,66,98},{1..., dimensions={0} | all-to-all | bytes 1376256 | tf_op jit(solution)/shard_map/all_to_all | solution.py:213
  80.9 4.6 %collective-permute-start.1 = (bf16[4,3,224,128]{3,2,1,0:T(8,128)(2,1)S(1)}, bf16[4,3,224,128]{3,2,1,0:T(8,128)(2,1)S(1)}, u32[]{:S(2)}, u32[]{:S(2)}) collective-permute-start(bf16[4,3,224,128]{3,2,1,0:T(8,128)(2,1)S(1)} %all_to_all.16.mine), channel_id=1, source_target_pairs={{0,16},{16,0},{32,48},{48,32},{64,80},{80,64},{96,112},{112,96},{1... | collective-permute-start | bytes 2064392 | tf_op jit(solution)/shard_map/ppermute | solution.py:214
  85.5 1.7 %collective-permute-done.1.theirs = bf16[4,3,224,128]{3,2,1,0:T(8,128)(2,1)S(1)} collective-permute-done((bf16[4,3,224,128]{3,2,1,0:T(8,128)(2,1)S(1)}, bf16[4,3,224,128]{3,2,1,0:T(8,128)(2,1)S(1)}, u32[]{:S(2)}, u32[]{:S(2)}) %collective-permute-start.1) | collective-permute-done | bytes 688160 | tf_op jit(solution)/shard_map/ppermute | solution.py:214
  87.3 6.0 %grads.1 = (bf16[3,1792,128]{2,1,0:T(8,128)(2,1)S(1)}, bf16[39,32,128]{2,1,0:T(8,128)(2,1)S(1)}, bf16[39,32,128]{2,1,0:T(8,128)(2,1)S(1)}, bf16[39,32,128]{2,1,0:T(8,128)(2,1)S(1)}, bf16[39,32,128]{2,1,0:T(8,128)(2,1)S(1)}) custom-call(s32[3,2,44]{2,1,0:T(2,128)S(1)} %bitcast.10, s32[3]{0:T(128)S(1)} %bitcast.13, ...), custom_call_target="tpu_custom_call" | custom-call | tf_op jit(solution)/shard_map/grads/pallas_call | solution.py:217
  93.3 4.8 %back.1 = bf16[16,16,1024]{2,1,0:T(8,128)(2,1)} custom-call(s32[3,2,44]{2,1,0:T(2,128)S(1)} %bitcast.11, s32[3]{0:T(128)S(1)} %bitcast.14, bf16[3,1792,128]{2,1,0:T(8,128)(2,1)S(1)} %get-tuple-element.21.band, bf16[44,64,64]{2,1,0:T(8,128)(2,1)S(1)} %reshape.27.gate, bf16[44,64,64]{2,1,0:T(8,128)(2,1)S(1)} %reshape.28.up, bf16[44,64,64]{2,1,0:T(8,128)(2,1)S(1)} %reshape.29.down), custom_call_target="tpu_custom_call" | custom-call | tf_op jit(solution)/shard_map/back/pallas_call | solution.py:224
  98.1 6.0 %all-to-all-start.2 = ((bf16[16,16,1024]{2,1,0:T(8,128)(2,1)}), bf16[16,16,1024]{2,1,0:T(8,128)(2,1)S(1)}, u32[]{:S(2)}, u32[]{:S(2)}) async-start(bf16[16,16,1024]{2,1,0:T(8,128)(2,1)} %back.1), calls=%async_computation.2 | async-start | bytes 1048576 | tf_op jit(solution)/shard_map/all_to_all | solution.py:232
  104.2 4.8 %collective-permute-start.2 = (bf16[39,32,128]{2,1,0:T(8,128)(2,1)S(1)}, bf16[39,32,128]{2,1,0:T(8,128)(2,1)S(1)}, u32[]{:S(2)}, u32[]{:S(2)}) collective-permute-start(bf16[39,32,128]{2,1,0:T(8,128)(2,1)S(1)} %get-tuple-element.23), channel_id=1, source_target_pairs={{0,256},{128,384},{256,0},{384,128},{1,257},{129,385},{257,1},{385... | collective-permute-start | bytes 958472 | tf_op jit(solution)/shard_map/ppermute | solution.py:233
  109.0 2.3 %collective-permute-start.3 = (bf16[39,32,128]{2,1,0:T(8,128)(2,1)S(1)}, bf16[39,32,128]{2,1,0:T(8,128)(2,1)S(1)}, u32[]{:S(2)}, u32[]{:S(2)}) collective-permute-start(bf16[39,32,128]{2,1,0:T(8,128)(2,1)S(1)} %get-tuple-element.24), channel_id=1, source_target_pairs={{0,128},{128,256},{256,384},{384,0},{1,129},{129,257},{257,385},{3... | collective-permute-start | bytes 958472 | tf_op jit(solution)/shard_map/ppermute | solution.py:234
  111.3 4.2 %collective-permute-start.4 = (bf16[39,32,128]{2,1,0:T(8,128)(2,1)S(1)}, bf16[39,32,128]{2,1,0:T(8,128)(2,1)S(1)}, u32[]{:S(2)}, u32[]{:S(2)}) collective-permute-start(bf16[39,32,128]{2,1,0:T(8,128)(2,1)S(1)} %get-tuple-element.25), channel_id=1, source_target_pairs={{0,384},{128,0},{256,128},{384,256},{1,385},{129,1},{257,129},{385... | collective-permute-start | bytes 958472 | tf_op jit(solution)/shard_map/ppermute | solution.py:235
  115.5 0.3 collective-permute-done.2.far
  115.8 7.9 %collective-permute-done.3.prev = bf16[39,32,128]{2,1,0:T(8,128)(2,1)S(1)} collective-permute-done((bf16[39,32,128]{2,1,0:T(8,128)(2,1)S(1)}, bf16[39,32,128]{2,1,0:T(8,128)(2,1)S(1)}, u32[]{:S(2)}, u32[]{:S(2)}) %collective-permute-start.3) | collective-permute-done | bytes 319520 | tf_op jit(solution)/shard_map/ppermute | solution.py:234
  123.7 0.0 collective-permute-done.4.next_
  123.7 0.2 dp_sum.1
  123.9 13.5 %all-gather.1 = bf16[124,32,128]{2,1,0:T(8,128)(2,1)S(1)} all-gather(bf16[31,32,128]{2,1,0:T(8,128)(2,1)S(1)} %get-tuple-element.26), channel_id=3, replica_groups=mesh['dp'=4,'row'=8,'col'=16] {'dp'}, dimensions={0}, use_global_device_ids=true | all-gather | bytes 1269760 | tf_op jit(solution)/shard_map/all_gather | solution.py:243
  137.3 2.6 %unpack.1 = (bf16[44,4096]{1,0:T(8,128)(2,1)}, bf16[44,4096]{1,0:T(8,128)(2,1)}, bf16[44,4096]{1,0:T(8,128)(2,1)}) custom-call(bf16[4,31,32,128]{3,2,1,0:T(8,128)(2,1)S(1)} %bitcast.7, bf16[8,32,128]{2,1,0:T(8,128)(2,1)S(1)} %get-tuple-element.27.rest), custom_call_target="tpu_custom_call" | custom-call | tf_op jit(solution)/shard_map/unpack/pallas_call | solution.py:245
  139.9 0.0 all-to-all-done.2
  139.9 0.1 reduce_sum.12
  140.0 0.6 fusion
Async XLA Ops:
  0.6 34.4 %copy-start.2 = (bf16[1,1,44,4096]{3,2,1,0:T(8,128)(2,1)S(1)}, bf16[1,1,44,4096]{3,2,1,0:T(8,128)(2,1)}, u32[]{:S(2)}) copy-start(bf16[1,1,44,4096]{3,2,1,0:T(8,128)(2,1)} %param.10) | copy-start | bytes 1081348
  1.4 34.5 %copy-start.3 = (bf16[1,1,44,4096]{3,2,1,0:T(8,128)(2,1)S(1)}, bf16[1,1,44,4096]{3,2,1,0:T(8,128)(2,1)}, u32[]{:S(2)}) copy-start(bf16[1,1,44,4096]{3,2,1,0:T(8,128)(2,1)} %param.11) | copy-start | bytes 1081348
  35.1 1.6 %copy-start = (s32[3,1,1,2,44]{4,3,2,1,0:T(2,128)S(1)}, s32[3,1,1,2,44]{4,3,2,1,0:T(2,128)}, u32[]{:S(2)}) copy-start(s32[3,1,1,2,44]{4,3,2,1,0:T(2,128)} %param.12) | copy-start | bytes 3172
  35.1 1.6 %copy-start.1 = (s32[3,1,1]{0,2,1:T(1,128)S(1)}, s32[3,1,1]{0,2,1:T(1,128)}, u32[]{:S(2)}) copy-start(s32[3,1,1]{0,2,1:T(1,128)} %param.13) | copy-start | bytes 40
  41.9 10.9 %collective-permute-start = (bf16[4,3,224,128]{3,2,1,0:T(8,128)(2,1)S(1)}, bf16[4,3,224,128]{3,2,1,0:T(8,128)(2,1)S(1)}, u32[]{:S(2)}, u32[]{:S(2)}) collective-permute-start(bf16[4,3,224,128]{3,2,1,0:T(8,128)(2,1)S(1)} %get-tuple-element.19), channel_id=1, source_target_pairs={{0,16},{16,0},{32,48},{48,32},{64,80},{80,64},{96,112},{112,96},{1... | collective-permute-start | bytes 2064392 | tf_op jit(solution)/shard_map/ppermute | solution.py:209
  80.9 6.4 %collective-permute-start.1 = (bf16[4,3,224,128]{3,2,1,0:T(8,128)(2,1)S(1)}, bf16[4,3,224,128]{3,2,1,0:T(8,128)(2,1)S(1)}, u32[]{:S(2)}, u32[]{:S(2)}) collective-permute-start(bf16[4,3,224,128]{3,2,1,0:T(8,128)(2,1)S(1)} %all_to_all.16.mine), channel_id=1, source_target_pairs={{0,16},{16,0},{32,48},{48,32},{64,80},{80,64},{96,112},{112,96},{1... | collective-permute-start | bytes 2064392 | tf_op jit(solution)/shard_map/ppermute | solution.py:214
  98.1 41.8 %all-to-all-start.2 = ((bf16[16,16,1024]{2,1,0:T(8,128)(2,1)}), bf16[16,16,1024]{2,1,0:T(8,128)(2,1)S(1)}, u32[]{:S(2)}, u32[]{:S(2)}) async-start(bf16[16,16,1024]{2,1,0:T(8,128)(2,1)} %back.1), calls=%async_computation.2 | async-start | bytes 1048576 | tf_op jit(solution)/shard_map/all_to_all | solution.py:232
  104.2 11.6 %collective-permute-start.2 = (bf16[39,32,128]{2,1,0:T(8,128)(2,1)S(1)}, bf16[39,32,128]{2,1,0:T(8,128)(2,1)S(1)}, u32[]{:S(2)}, u32[]{:S(2)}) collective-permute-start(bf16[39,32,128]{2,1,0:T(8,128)(2,1)S(1)} %get-tuple-element.23), channel_id=1, source_target_pairs={{0,256},{128,384},{256,0},{384,128},{1,257},{129,385},{257,1},{385... | collective-permute-start | bytes 958472 | tf_op jit(solution)/shard_map/ppermute | solution.py:233
  109.0 14.7 %collective-permute-start.3 = (bf16[39,32,128]{2,1,0:T(8,128)(2,1)S(1)}, bf16[39,32,128]{2,1,0:T(8,128)(2,1)S(1)}, u32[]{:S(2)}, u32[]{:S(2)}) collective-permute-start(bf16[39,32,128]{2,1,0:T(8,128)(2,1)S(1)} %get-tuple-element.24), channel_id=1, source_target_pairs={{0,128},{128,256},{256,384},{384,0},{1,129},{129,257},{257,385},{3... | collective-permute-start | bytes 958472 | tf_op jit(solution)/shard_map/ppermute | solution.py:234
  111.3 12.4 %collective-permute-start.4 = (bf16[39,32,128]{2,1,0:T(8,128)(2,1)S(1)}, bf16[39,32,128]{2,1,0:T(8,128)(2,1)S(1)}, u32[]{:S(2)}, u32[]{:S(2)}) collective-permute-start(bf16[39,32,128]{2,1,0:T(8,128)(2,1)S(1)} %get-tuple-element.25), channel_id=1, source_target_pairs={{0,384},{128,0},{256,128},{384,256},{1,385},{129,1},{257,129},{385... | collective-permute-start | bytes 958472 | tf_op jit(solution)/shard_map/ppermute | solution.py:235

commit v6 on v5

v6 whole, which is shorter than its diff:
```python
import jax
import jax.numpy as jnp
from jax import lax
from jax.experimental import pallas as pl
from jax.experimental.pallas import tpu as pltpu
from jax.sharding import PartitionSpec as P

BS = 64
REST = 192
VMEM = pl.BlockSpec(memory_space=pltpu.VMEM)
SMEM = pl.BlockSpec(memory_space=pltpu.SMEM)
PARAMS = pltpu.CompilerParams(vmem_limit_bytes=40 * 1024 * 1024)
F32 = jnp.float32
BF16 = jnp.bfloat16


def rows_of(block):
    return pl.ds(pl.multiple_of(block * BS, BS), BS)


def feature_major(wide, cols):
    n_col, pair, width = wide.shape
    half = pair // 2
    toks = n_col * half
    for j in range(0, width, 128):
        piece = wide[:, :, j : j + 128].astype(F32).reshape(n_col, 2, half, 128)
        for side in range(2):
            cols[side, j : j + 128, :] = piece[:, side].reshape(toks, 128).T.astype(BF16)


def unflatten(flat, blocks, spaced):
    slots, area = flat.shape
    apart = BS + 1
    for j in range(0, area, 2 * BS):
        pair = flat[:, j : j + 2 * BS].astype(F32)
        d = j // BS
        spaced[pl.ds(d, slots, stride=apart), :] = pair
        spaced[pl.ds(d + 1, slots, stride=apart), :] = pltpu.roll(pair, BS, 1)
    for s in range(slots):
        blocks[s] = spaced[s * apart : s * apart + BS, :BS].astype(BF16)


def live_block(blocks, s, count):
    return jnp.where(s < count, blocks[s], jnp.zeros_like(blocks[s]))


def spread_kernel(
    index, count, wide, gate_in, up_in, down_in,
    cols, mine, theirs, gate, up, down,
    total, spaced,
):
    feature_major(wide, cols)
    total[...] = jnp.zeros_like(total)
    for m, (flat, blocks) in enumerate(((gate_in, gate), (up_in, up), (down_in, down))):
        unflatten(flat, blocks, spaced)
        for s in range(blocks.shape[0]):
            source = cols[m // 2, rows_of(index[m, 0, s]), :]
            place = rows_of(index[m, 1, s])
            total[m, place, :] += lax.dot_general(
                live_block(blocks, s, count[m]),
                source,
                (((0,), (0,)), ((), ())),
                preferred_element_type=F32,
            )
    core = lax.axis_index("row") % 2
    share = mine.shape[2]
    for x in range(mine.shape[0]):
        for m in range(3):
            for out, side in ((theirs, 1 - core), (mine, core)):
                first = pl.multiple_of((2 * x + side) * share, 32)
                out[x, m] = total[m, pl.ds(first, share), :].astype(BF16)


def pair_sum_kernel(mine, other, out):
    out[...] = (mine[...].astype(F32) + other[...].astype(F32)).astype(BF16)


def hidden_kernel(terms, out):
    sums = [terms[0, m].astype(F32) for m in range(3)]
    for j in range(1, terms.shape[0]):
        sums = [sums[m] + terms[j, m].astype(F32) for m in range(3)]
    gate, up, hgrad = sums
    sig = jax.nn.sigmoid(gate)
    units = (
        (hgrad * up * sig * (1.0 + gate * (1.0 - sig))).astype(BF16),
        (hgrad * gate * sig).astype(BF16),
        (gate * sig * up).astype(BF16),
    )
    for j in range(out.shape[0]):
        for m in range(3):
            out[j, m] = units[m]


def back_kernel(
    index, count, mine, theirs, cols, gate, up, down,
    rows, own, ahead, across, behind,
    band, out_total, in_total, grads,
):
    core = lax.axis_index("row") % 2
    share = mine.shape[2]
    for x in range(mine.shape[0]):
        for m in range(3):
            for half, side in ((mine, core), (theirs, 1 - core)):
                first = pl.multiple_of((2 * x + side) * share, 32)
                band[m, pl.ds(first, share), :] = half[x, m]
    out_total[...] = jnp.zeros_like(out_total)
    in_total[...] = jnp.zeros_like(in_total)
    depth = BS // 2
    for m, blocks in enumerate((gate, up, down)):
        total = out_total if m == 2 else in_total
        for s in range(blocks.shape[0]):
            unit = band[m, rows_of(index[m, 1, s]), :]
            place = rows_of(index[m, 0, s])
            total[place, :] += jnp.dot(
                live_block(blocks, s, count[m]), unit, preferred_element_type=F32
            )
            grad = lax.dot_general(
                cols[m // 2, place, :], unit, (((1,), (1,)), ((), ())), preferred_element_type=F32
            )
            grad = jnp.where(s < count[m], grad, 0.0)
            first = (m * blocks.shape[0] + s) * depth
            grads[first : first + depth, :] = jnp.concatenate(
                [grad[:depth], grad[depth:]], axis=1
            ).astype(BF16)
    n_col, pair, width = rows.shape
    half = pair // 2
    for j in range(0, width, 128):
        out_piece = out_total[j : j + 128, :].T.reshape(n_col, half, 128)
        in_piece = in_total[j : j + 128, :].T.reshape(n_col, half, 128)
        rows[:, :, j : j + 128] = jnp.concatenate([out_piece, in_piece], axis=1).astype(BF16)
    outs = (own, ahead, across, behind)
    n_dp = len(outs)
    per = own.shape[0] - REST
    for away, out in enumerate(outs):
        owner = (lax.axis_index("dp") + away) % n_dp
        out[:per, :] = grads[pl.ds(pl.multiple_of(owner * per, 16), per), :]
        out[per:, :] = grads[n_dp * per :, :]


def dp_sum_kernel(here, far, prev, next_, own, rest):
    total = (here[...].astype(F32) + far[...].astype(F32)) + (
        prev[...].astype(F32) + next_[...].astype(F32)
    )
    own[...] = total[: own.shape[0]].astype(BF16)
    rest[...] = total[own.shape[0] :].astype(BF16)


def unpack_kernel(owned, rest, gate, up, down, spaced):
    n_dp, per, lanes = owned.shape
    slots = gate.shape[0]
    depth = BS // 2
    apart = depth + 1
    piece = depth // 2
    for first in range(0, 3 * slots * depth, piece):
        owner, row = first // per, first % per
        if owner < n_dp:
            part = owned[owner, row : row + piece, :]
        else:
            part = rest[row : row + piece, :]
        to = first // depth * apart + first % depth
        spaced[to : to + piece, :] = part.astype(F32)
    low = lax.broadcasted_iota(jnp.int32, (slots, lanes), 1) < BS
    for m, out in enumerate((gate, up, down)):
        base = m * slots * apart
        for k in range(0, depth, 2):
            even = spaced[pl.ds(base + k, slots, stride=apart), :]
            odd = spaced[pl.ds(base + k + 1, slots, stride=apart), :]
            out[:, k * BS : k * BS + lanes] = jnp.where(low, even, pltpu.roll(odd, BS, 1)).astype(BF16)
            start = (depth + k) * BS
            out[:, start : start + lanes] = jnp.where(low, pltpu.roll(even, BS, 1), odd).astype(BF16)


def arr(*shape):
    return jax.ShapeDtypeStruct(shape, BF16)


def call(body, name, out_shape, ins, outs, scratch=()):
    return pl.pallas_call(
        body,
        out_shape=out_shape,
        in_specs=ins,
        out_specs=outs,
        scratch_shapes=list(scratch),
        compiler_params=PARAMS,
        name=name,
    )


def per_device(tokens, grad_out, gate_blocks, up_blocks, down_blocks, block_index, block_count):
    n_dp, n_row, n_col = (lax.axis_size(a) for a in ("dp", "row", "col"))
    slots = gate_blocks.shape[2]
    half, width = tokens.shape
    toks = half * n_col
    units = 28 * BS
    share = units // n_row
    chips = n_row // 2
    index = block_index.reshape(3, 2, slots)
    count = block_count.reshape(3)
    flat_blocks = [w.reshape(slots, BS * BS) for w in (gate_blocks, up_blocks, down_blocks)]
    blocks = arr(slots, BS, BS)
    pair = [(i, i ^ 1) for i in range(n_row)]
    same_core = [[2 * x + k for x in range(chips)] for k in range(2)]
    ahead, behind, across = ([(i, (i + d) % n_dp) for i in range(n_dp)] for d in (1, 3, 2))

    both = jnp.concatenate([tokens, grad_out], axis=0)
    wide = lax.all_gather(both, "col", axis=0)
    terms = arr(chips, 3, share, toks)
    cols, mine, theirs, gate, up, down = call(
        spread_kernel,
        "spread",
        (arr(2, width, toks), terms, terms, blocks, blocks, blocks),
        [SMEM] * 2 + [VMEM] * 4,
        (VMEM,) * 6,
        [
            pltpu.VMEM((3, units, toks), F32),
            pltpu.VMEM((slots * (BS + 1), 2 * BS), F32),
        ],
    )(index, count, wide, *flat_blocks)
    other = lax.ppermute(theirs, "row", pair)
    paired = call(pair_sum_kernel, "pair_sum", terms, [VMEM] * 2, VMEM)(mine, other)
    summed = lax.all_to_all(paired, "row", 0, 0, axis_index_groups=same_core)
    own = call(hidden_kernel, "hidden", terms, [VMEM], VMEM)(summed)
    mine = lax.all_to_all(own, "row", 0, 0, axis_index_groups=same_core)
    theirs = lax.ppermute(mine, "row", pair)
    depth = BS // 2
    per = (3 * slots * depth - REST) // n_dp
    packed = arr(per + REST, 2 * BS)
    rows, own, to_next, to_far, to_prev = call(
        back_kernel,
        "back",
        (arr(n_col, 2 * half, width),) + (packed,) * n_dp,
        [SMEM] * 2 + [VMEM] * 6,
        (VMEM,) * (1 + n_dp),
        [
            pltpu.VMEM((3, units, toks), BF16),
            pltpu.VMEM((width, toks), F32),
            pltpu.VMEM((width, toks), F32),
            pltpu.VMEM((3 * slots * depth, 2 * BS), BF16),
        ],
    )(index, count, mine, theirs, cols, gate, up, down)
    row_terms = lax.all_to_all(rows, "col", 0, 0)
    from_far = lax.ppermute(to_far, "dp", across)
    from_prev = lax.ppermute(to_next, "dp", ahead)
    from_next = lax.ppermute(to_prev, "dp", behind)
    own, rest = call(
        dp_sum_kernel,
        "dp_sum",
        (arr(per, 2 * BS), arr(REST, 2 * BS)),
        [VMEM] * 4,
        (VMEM,) * 2,
    )(own, from_far, from_prev, from_next)
    owned = lax.all_gather(own, "dp", axis=0)
    flat = arr(slots, BS * BS)
    block_grads = call(
        unpack_kernel,
        "unpack",
        (flat, flat, flat),
        [VMEM] * 2,
        (VMEM,) * 3,
        [pltpu.VMEM((3 * slots * (depth + 1), 2 * BS), F32)],
    )(owned, rest)
    row_sum = jnp.sum(row_terms.astype(F32), axis=0).astype(BF16)
    return (row_sum[:half], row_sum[half:], *(b[None, None] for b in block_grads))


def solution(mesh):
    placed = (
        P(("dp", "col"), "row"),
        P(("dp", "col"), "row"),
        P("row", "col", None, None),
        P("row", "col", None, None),
        P("row", "col", None, None),
        P(None, "row", "col", None, None),
        P(None, "row", "col"),
    )
    return jax.shard_map(
        per_device,
        mesh=mesh,
        in_specs=placed,
        out_specs=(
            P(("dp", "col"), "row"),
            P(("dp", "col"), "row"),
            P("row", "col", None, None),
            P("row", "col", None, None),
            P("row", "col", None, None),
        ),
        check_vma=False,
    )
```

time: 142 us -> 131 us (0.923)
  Pallas kernels: 19.2 us -> 9.71 us
    pallas_call x4 -> x3, Pallas kernels: 16.3 us -> 7.91 us  [the longest x1 4.55 us: per_device(): call(back_kernel, 'back', (arr(n_col, 2 * half, width),) + (packed,) * n_...]
    reshape x3 -> x0, local copies, waits for them, and re-layouts: 3.24 us -> none  [per_device(): w.reshape(slots, BS, BS)]
    unnamed x8 -> x10, local copies, waits for them, and re-layouts: 0.02 us -> 2.68 us
    all_to_all x1, blocking collectives: 15.9 us -> 14.5 us  [per_device(): summed = lax.all_to_all(paired, 'row', 0, 0, axis_index_groups=same_core)]
  transfers between devices with their start and end apart: 6 -> 6, of which waited for: 4 -> 4; matrix products, arithmetic and copies ran while one was open for 0% -> 0% of each run, Pallas kernels for 2% -> 1%
where the time goes in v6:
time: 131 us; the launch traced here: 130 us
  blocking collectives  71.7 us (55%)
  starting transfers between devices  32.2 us (25%)
  waiting for transfers between devices  11.2 us (9%)
  Pallas kernels  9.71 us (7%)
  local copies, waits for them, and re-layouts  3.29 us (3%)
    all_gather x1, blocking collectives, per_device(): wide = lax.all_gather(both, 'col', axis=0)  31.8 us
    all_to_all x1, blocking collectives, per_device(): summed = lax.all_to_all(paired, 'row', 0, 0, axis_index_groups=same_core)  14.5 us
    all_gather x1, blocking collectives, per_device(): owned = lax.all_gather(own, 'dp', axis=0)  13.6 us
    all_to_all x1, blocking collectives, per_device(): mine = lax.all_to_all(own, 'row', 0, 0, axis_index_groups=same_core)  11.8 us
    ppermute x1, starting transfers between devices, per_device(): other = lax.ppermute(theirs, 'row', pair)  10.1 us
    ppermute x1, waiting for transfers between devices, per_device(): from_prev = lax.ppermute(to_next, 'dp', ahead)  7.47 us
    all_to_all x1, starting transfers between devices, per_device(): row_terms = lax.all_to_all(rows, 'col', 0, 0)  6.11 us
    ppermute x1, starting transfers between devices, per_device(): from_far = lax.ppermute(to_far, 'dp', across)  4.82 us
  transfers between devices with their start and end apart: 6, of which 4 were waited for; matrix products, arithmetic and copies ran while one was open for 0% of the time, Pallas kernels for 1%

profile of v6, /device:TPU:1, one launch (start us, length us, event | category | flops | bytes accessed | tf_op | source)
XLA Modules:
  0.0 129.6 jit_solution(13051875248560249393)
XLA Ops:
  0.6 0.0 copy-start
  0.6 0.8 pad_maximum_fusion
  1.4 31.8 %all-gather = bf16[256,1024]{1,0:T(8,128)(2,1)S(1)} all-gather(bf16[16,1024]{1,0:T(8,128)(2,1)S(1)} %pad_maximum_fusion), channel_id=2, replica_groups=mesh['dp'=4,'row'=8,'col'=16] {'col'}, dimensions={0}, use_global_device_ids=true | all-gather | bytes 557056 | tf_op jit(solution)/shard_map/all_gather | solution.py:206
  33.2 0.0 copy-start.3
  33.2 0.0 copy-start.4
  33.2 0.0 copy-done
  33.2 0.7 copy-done.3
  33.9 0.0 copy-done.4
  33.9 0.0 copy-start.1
  33.9 1.0 copy-done.1
  34.9 0.0 copy-start.2
  34.9 1.0 copy-done.2
  35.9 3.2 %spread.1 = (bf16[2,1024,128]{2,1,0:T(8,128)(2,1)S(1)}, bf16[4,3,224,128]{3,2,1,0:T(8,128)(2,1)S(1)}, bf16[4,3,224,128]{3,2,1,0:T(8,128)(2,1)S(1)}, bf16[44,64,6...) custom-call(s32[3,2,44]{2,1,0:T(2,128)S(1)} %bitcast.15, s32[3]{0:T(128)S(1)} %bitcast.17, ...), custom_call_target="tpu_custom_call" | custom-call | tf_op jit(solution)/shard_map/spread/pallas_call | solution.py:208
  39.1 10.1 %collective-permute-start = (bf16[4,3,224,128]{3,2,1,0:T(8,128)(2,1)S(1)}, bf16[4,3,224,128]{3,2,1,0:T(8,128)(2,1)S(1)}, u32[]{:S(2)}, u32[]{:S(2)}) collective-permute-start(bf16[4,3,224,128]{3,2,1,0:T(8,128)(2,1)S(1)} %get-tuple-element.22), channel_id=1, source_target_pairs={{0,16},{16,0},{32,48},{48,32},{64,80},{80,64},{96,112},{112,96},{1... | collective-permute-start | bytes 2064392 | tf_op jit(solution)/shard_map/ppermute | solution.py:219
  49.3 1.7 %collective-permute-done.other = bf16[4,3,224,128]{3,2,1,0:T(8,128)(2,1)S(1)} collective-permute-done((bf16[4,3,224,128]{3,2,1,0:T(8,128)(2,1)S(1)}, bf16[4,3,224,128]{3,2,1,0:T(8,128)(2,1)S(1)}, u32[]{:S(2)}, u32[]{:S(2)}) %collective-permute-start) | collective-permute-done | bytes 688160 | tf_op jit(solution)/shard_map/ppermute | solution.py:219
  51.0 0.2 pair_sum.1
  51.2 14.5 %all_to_all.15.terms = bf16[4,3,224,128]{3,2,1,0:T(8,128)(2,1)S(1)} all-to-all(bf16[4,3,224,128]{3,2,1,0:T(8,128)(2,1)S(1)} %pair_sum.1), channel_id=1, replica_groups={{0,32,64,96},{16,48,80,112},{1,33,65,97},{17,49,81,113},{2,34,66,98},{1..., dimensions={0} | all-to-all | bytes 1376256 | tf_op jit(solution)/shard_map/all_to_all | solution.py:221
  65.6 0.1 hidden.1
  65.8 11.8 %all_to_all.16.mine = bf16[4,3,224,128]{3,2,1,0:T(8,128)(2,1)S(1)} all-to-all(bf16[4,3,224,128]{3,2,1,0:T(8,128)(2,1)S(1)} %hidden.1), channel_id=1, replica_groups={{0,32,64,96},{16,48,80,112},{1,33,65,97},{17,49,81,113},{2,34,66,98},{1..., dimensions={0} | all-to-all | bytes 1376256 | tf_op jit(solution)/shard_map/all_to_all | solution.py:223
  77.6 4.6 %collective-permute-start.1 = (bf16[4,3,224,128]{3,2,1,0:T(8,128)(2,1)S(1)}, bf16[4,3,224,128]{3,2,1,0:T(8,128)(2,1)S(1)}, u32[]{:S(2)}, u32[]{:S(2)}) collective-permute-start(bf16[4,3,224,128]{3,2,1,0:T(8,128)(2,1)S(1)} %all_to_all.16.mine), channel_id=1, source_target_pairs={{0,16},{16,0},{32,48},{48,32},{64,80},{80,64},{96,112},{112,96},{1... | collective-permute-start | bytes 2064392 | tf_op jit(solution)/shard_map/ppermute | solution.py:224
  82.3 1.7 %collective-permute-done.1.theirs = bf16[4,3,224,128]{3,2,1,0:T(8,128)(2,1)S(1)} collective-permute-done((bf16[4,3,224,128]{3,2,1,0:T(8,128)(2,1)S(1)}, bf16[4,3,224,128]{3,2,1,0:T(8,128)(2,1)S(1)}, u32[]{:S(2)}, u32[]{:S(2)}) %collective-permute-start.1) | collective-permute-done | bytes 688160 | tf_op jit(solution)/shard_map/ppermute | solution.py:224
  84.0 4.6 %back.1 = (bf16[16,16,1024]{2,1,0:T(8,128)(2,1)}, bf16[1200,128]{1,0:T(8,128)(2,1)S(1)}, bf16[1200,128]{1,0:T(8,128)(2,1)S(1)}, bf16[1200,128]{1,0:T(8,128)(2,1)S(1)}, bf16[1200,128]{1,0:T(8,128)(2,1)S(1)}) custom-call(s32[3,2,44]{2,1,0:T(2,128)S(1)} %bitcast.16, s32[3]{0:T(128)S(1)} %bitcast.18, bf16[4,3,224,128]{3,2,1,0:T(8,128)(2,1)S(1)} %all_to_all.16.mine, ...), custom_call_target="tpu_custom_call" | custom-call | tf_op jit(solution)/shard_map/back/pallas_call | solution.py:228
  88.6 6.1 %all-to-all-start.2 = ((bf16[16,16,1024]{2,1,0:T(8,128)(2,1)}), bf16[16,16,1024]{2,1,0:T(8,128)(2,1)S(1)}, u32[]{:S(2)}, u32[]{:S(2)}) async-start(bf16[16,16,1024]{2,1,0:T(8,128)(2,1)} %get-tuple-element.27), calls=%async_computation.2 | async-start | bytes 1048576 | tf_op jit(solution)/shard_map/all_to_all | solution.py:241
  94.7 4.8 %collective-permute-start.2 = (bf16[1200,128]{1,0:T(8,128)(2,1)S(1)}, bf16[1200,128]{1,0:T(8,128)(2,1)S(1)}, u32[]{:S(2)}, u32[]{:S(2)}) collective-permute-start(bf16[1200,128]{1,0:T(8,128)(2,1)S(1)} %get-tuple-element.29), channel_id=1, source_target_pairs={{0,256},{128,384},{256,0},{384,128},{1,257},{129,385},{257,1},{385... | collective-permute-start | bytes 921608 | tf_op jit(solution)/shard_map/ppermute | solution.py:242
  99.5 2.3 %collective-permute-start.3 = (bf16[1200,128]{1,0:T(8,128)(2,1)S(1)}, bf16[1200,128]{1,0:T(8,128)(2,1)S(1)}, u32[]{:S(2)}, u32[]{:S(2)}) collective-permute-start(bf16[1200,128]{1,0:T(8,128)(2,1)S(1)} %get-tuple-element.30), channel_id=1, source_target_pairs={{0,128},{128,256},{256,384},{384,0},{1,129},{129,257},{257,385},{3... | collective-permute-start | bytes 921608 | tf_op jit(solution)/shard_map/ppermute | solution.py:243
  101.8 4.2 %collective-permute-start.4 = (bf16[1200,128]{1,0:T(8,128)(2,1)S(1)}, bf16[1200,128]{1,0:T(8,128)(2,1)S(1)}, u32[]{:S(2)}, u32[]{:S(2)}) collective-permute-start(bf16[1200,128]{1,0:T(8,128)(2,1)S(1)} %get-tuple-element.31), channel_id=1, source_target_pairs={{0,384},{128,0},{256,128},{384,256},{1,385},{129,1},{257,129},{385... | collective-permute-start | bytes 921608 | tf_op jit(solution)/shard_map/ppermute | solution.py:244
  106.0 0.2 collective-permute-done.2.far
  106.3 7.5 %collective-permute-done.3.prev = bf16[1200,128]{1,0:T(8,128)(2,1)S(1)} collective-permute-done((bf16[1200,128]{1,0:T(8,128)(2,1)S(1)}, bf16[1200,128]{1,0:T(8,128)(2,1)S(1)}, u32[]{:S(2)}, u32[]{:S(2)}) %collective-permute-start.3) | collective-permute-done | bytes 307232 | tf_op jit(solution)/shard_map/ppermute | solution.py:243
  113.7 0.0 collective-permute-done.4.next_
  113.7 0.2 dp_sum.1
  113.9 13.6 %all-gather.1 = bf16[4032,128]{1,0:T(8,128)(2,1)S(1)} all-gather(bf16[1008,128]{1,0:T(8,128)(2,1)S(1)} %get-tuple-element.32), channel_id=3, replica_groups=mesh['dp'=4,'row'=8,'col'=16] {'dp'}, dimensions={0}, use_global_device_ids=true | all-gather | bytes 1290240 | tf_op jit(solution)/shard_map/all_gather | solution.py:252
  127.4 1.5 %unpack.1 = (bf16[44,4096]{1,0:T(8,128)(2,1)}, bf16[44,4096]{1,0:T(8,128)(2,1)}, bf16[44,4096]{1,0:T(8,128)(2,1)}) custom-call(bf16[4,1008,128]{2,1,0:T(8,128)(2,1)S(1)} %bitcast.10, bf16[192,128]{1,0:T(8,128)(2,1)S(1)} %get-tuple-element.33.rest), custom_call_target="tpu_custom_call" | custom-call | tf_op jit(solution)/shard_map/unpack/pallas_call | solution.py:254
  128.9 0.0 all-to-all-done.2
  128.9 0.1 reduce_sum.12
  129.0 0.6 fusion
Async XLA Ops:
  0.6 32.6 %copy-start = (bf16[1,1,44,4096]{3,2,1,0:T(8,128)(2,1)S(1)}, bf16[1,1,44,4096]{3,2,1,0:T(8,128)(2,1)}, u32[]{:S(2)}) copy-start(bf16[1,1,44,4096]{3,2,1,0:T(8,128)(2,1)} %param.9) | copy-start | bytes 1081348
  33.2 0.7 copy-start.3
  33.2 0.7 copy-start.4
  33.9 1.0 copy-start.1
  34.9 1.0 copy-start.2
  39.1 11.9 %collective-permute-start = (bf16[4,3,224,128]{3,2,1,0:T(8,128)(2,1)S(1)}, bf16[4,3,224,128]{3,2,1,0:T(8,128)(2,1)S(1)}, u32[]{:S(2)}, u32[]{:S(2)}) collective-permute-start(bf16[4,3,224,128]{3,2,1,0:T(8,128)(2,1)S(1)} %get-tuple-element.22), channel_id=1, source_target_pairs={{0,16},{16,0},{32,48},{48,32},{64,80},{80,64},{96,112},{112,96},{1... | collective-permute-start | bytes 2064392 | tf_op jit(solution)/shard_map/ppermute | solution.py:219
  77.6 6.4 %collective-permute-start.1 = (bf16[4,3,224,128]{3,2,1,0:T(8,128)(2,1)S(1)}, bf16[4,3,224,128]{3,2,1,0:T(8,128)(2,1)S(1)}, u32[]{:S(2)}, u32[]{:S(2)}) collective-permute-start(bf16[4,3,224,128]{3,2,1,0:T(8,128)(2,1)S(1)} %all_to_all.16.mine), channel_id=1, source_target_pairs={{0,16},{16,0},{32,48},{48,32},{64,80},{80,64},{96,112},{112,96},{1... | collective-permute-start | bytes 2064392 | tf_op jit(solution)/shard_map/ppermute | solution.py:224
  88.6 40.4 %all-to-all-start.2 = ((bf16[16,16,1024]{2,1,0:T(8,128)(2,1)}), bf16[16,16,1024]{2,1,0:T(8,128)(2,1)S(1)}, u32[]{:S(2)}, u32[]{:S(2)}) async-start(bf16[16,16,1024]{2,1,0:T(8,128)(2,1)} %get-tuple-element.27), calls=%async_computation.2 | async-start | bytes 1048576 | tf_op jit(solution)/shard_map/all_to_all | solution.py:241
  94.7 11.6 %collective-permute-start.2 = (bf16[1200,128]{1,0:T(8,128)(2,1)S(1)}, bf16[1200,128]{1,0:T(8,128)(2,1)S(1)}, u32[]{:S(2)}, u32[]{:S(2)}) collective-permute-start(bf16[1200,128]{1,0:T(8,128)(2,1)S(1)} %get-tuple-element.29), channel_id=1, source_target_pairs={{0,256},{128,384},{256,0},{384,128},{1,257},{129,385},{257,1},{385... | collective-permute-start | bytes 921608 | tf_op jit(solution)/shard_map/ppermute | solution.py:242
  99.5 14.2 %collective-permute-start.3 = (bf16[1200,128]{1,0:T(8,128)(2,1)S(1)}, bf16[1200,128]{1,0:T(8,128)(2,1)S(1)}, u32[]{:S(2)}, u32[]{:S(2)}) collective-permute-start(bf16[1200,128]{1,0:T(8,128)(2,1)S(1)} %get-tuple-element.30), channel_id=1, source_target_pairs={{0,128},{128,256},{256,384},{384,0},{1,129},{129,257},{257,385},{3... | collective-permute-start | bytes 921608 | tf_op jit(solution)/shard_map/ppermute | solution.py:243
  101.8 11.9 %collective-permute-start.4 = (bf16[1200,128]{1,0:T(8,128)(2,1)S(1)}, bf16[1200,128]{1,0:T(8,128)(2,1)S(1)}, u32[]{:S(2)}, u32[]{:S(2)}) collective-permute-start(bf16[1200,128]{1,0:T(8,128)(2,1)S(1)} %get-tuple-element.31), channel_id=1, source_target_pairs={{0,384},{128,0},{256,128},{384,256},{1,385},{129,1},{257,129},{385... | collective-permute-start | bytes 921608 | tf_op jit(solution)/shard_map/ppermute | solution.py:244

commit v7 on v6

--- a/solution.py
+++ b/solution.py
@@ -7,6 +7,7 @@
 
 BS = 64
 REST = 192
+HIDE = 10**12
 VMEM = pl.BlockSpec(memory_space=pltpu.VMEM)
 SMEM = pl.BlockSpec(memory_space=pltpu.SMEM)
 PARAMS = pltpu.CompilerParams(vmem_limit_bytes=40 * 1024 * 1024)
@@ -137,15 +138,24 @@
         out[per:, :] = grads[n_dp * per :, :]
 
 
-def dp_sum_kernel(here, far, prev, next_, own, rest):
-    total = (here[...].astype(F32) + far[...].astype(F32)) + (
-        prev[...].astype(F32) + next_[...].astype(F32)
-    )
+def far_sum_kernel(here, far, out):
+    out[...] = here[...].astype(F32) + far[...].astype(F32)
+
+
+def dp_sum_kernel(opposite, prev, next_, own, rest):
+    total = opposite[...] + (prev[...].astype(F32) + next_[...].astype(F32))
     own[...] = total[: own.shape[0]].astype(BF16)
     rest[...] = total[own.shape[0] :].astype(BF16)
 
 
-def unpack_kernel(owned, rest, gate, up, down, spaced):
+def unpack_kernel(owned, rest, terms, gate, up, down, mixed, tokens_grad, spaced):
+    half, width = mixed.shape
+    for j in range(0, width, 128):
+        total = terms[0, :, j : j + 128].astype(F32)
+        for c in range(1, terms.shape[0]):
+            total += terms[c, :, j : j + 128].astype(F32)
+        mixed[:, j : j + 128] = total[:half].astype(BF16)
+        tokens_grad[:, j : j + 128] = total[half:].astype(BF16)
     n_dp, per, lanes = owned.shape
     slots = gate.shape[0]
     depth = BS // 2
@@ -174,7 +184,7 @@
     return jax.ShapeDtypeStruct(shape, BF16)
 
 
-def call(body, name, out_shape, ins, outs, scratch=()):
+def call(body, name, out_shape, ins, outs, scratch=(), flops=0):
     return pl.pallas_call(
         body,
         out_shape=out_shape,
@@ -182,6 +192,7 @@
         out_specs=outs,
         scratch_shapes=list(scratch),
         compiler_params=PARAMS,
+        cost_estimate=pl.CostEstimate(flops=flops, bytes_accessed=0, transcendentals=0),
         name=name,
     )
 
@@ -242,25 +253,33 @@
     from_far = lax.ppermute(to_far, "dp", across)
     from_prev = lax.ppermute(to_next, "dp", ahead)
     from_next = lax.ppermute(to_prev, "dp", behind)
+    opposite = call(
+        far_sum_kernel,
+        "far_sum",
+        jax.ShapeDtypeStruct(packed.shape, F32),
+        [VMEM] * 2,
+        VMEM,
+        flops=HIDE,
+    )(own, from_far)
     own, rest = call(
         dp_sum_kernel,
         "dp_sum",
         (arr(per, 2 * BS), arr(REST, 2 * BS)),
-        [VMEM] * 4,
+        [VMEM] * 3,
         (VMEM,) * 2,
-    )(own, from_far, from_prev, from_next)
+        flops=HIDE,
+    )(opposite, from_prev, from_next)
     owned = lax.all_gather(own, "dp", axis=0)
     flat = arr(slots, BS * BS)
-    block_grads = call(
+    *block_grads, mixed, tokens_grad = call(
         unpack_kernel,
         "unpack",
-        (flat, flat, flat),
-        [VMEM] * 2,
-        (VMEM,) * 3,
+        (flat, flat, flat, arr(half, width), arr(half, width)),
+        [VMEM] * 3,
+        (VMEM,) * 5,
         [pltpu.VMEM((3 * slots * (depth + 1), 2 * BS), F32)],
-    )(owned, rest)
-    row_sum = jnp.sum(row_terms.astype(F32), axis=0).astype(BF16)
-    return (row_sum[:half], row_sum[half:], *(b[None, None] for b in block_grads))
+    )(owned, rest, row_terms)
+    return (mixed, tokens_grad, *(b[None, None] for b in block_grads))
 
 
 def solution(mesh):

time: 131 us -> 132 us (level)
  the two profiles are of different devices: /device:TPU:1 before, /device:TPU:8 now
where the time goes in v7:
time: 132 us; the launch traced here: 131 us
  blocking collectives  83.8 us (63%)
  starting transfers between devices  20.3 us (15%)
  Pallas kernels  11.9 us (9%)
  waiting for transfers between devices  11.2 us (8%)
  local copies, waits for them, and re-layouts  2.68 us (2%)
    all_gather x1, blocking collectives, per_device(): wide = lax.all_gather(both, 'col', axis=0)  38.5 us
    all_gather x1, blocking collectives, per_device(): owned = lax.all_gather(own, 'dp', axis=0)  16.6 us
    all_to_all x1, blocking collectives, per_device(): summed = lax.all_to_all(paired, 'row', 0, 0, axis_index_groups=same_core)  15.6 us
    all_to_all x1, blocking collectives, per_device(): mine = lax.all_to_all(own, 'row', 0, 0, axis_index_groups=same_core)  13 us
    all_to_all x1, starting transfers between devices, per_device(): row_terms = lax.all_to_all(rows, 'col', 0, 0)  6.44 us
    ppermute x1, waiting for transfers between devices, per_device(): from_prev = lax.ppermute(to_next, 'dp', ahead)  5.02 us
    pallas_call x1, Pallas kernels, per_device(): call(back_kernel, 'back', (arr(n_col, 2 * half, width),) + (packed,) * n_...  4.63 us
    ppermute x1, starting transfers between devices, per_device(): from_far = lax.ppermute(to_far, 'dp', across)  4.2 us
  transfers between devices with their start and end apart: 6, of which 4 were waited for; matrix products, arithmetic and copies ran while one was open for 0% of the time, Pallas kernels for 1%

profile of v7, /device:TPU:8, one launch (start us, length us, event | category | flops | bytes accessed | tf_op | source)
XLA Modules:
  0.0 131.4 jit_solution(9392481188407174485)
XLA Ops:
  0.6 0.0 copy-start
  0.6 0.8 pad_maximum_fusion
  1.4 38.5 %all-gather = bf16[256,1024]{1,0:T(8,128)(2,1)S(1)} all-gather(bf16[16,1024]{1,0:T(8,128)(2,1)S(1)} %pad_maximum_fusion), channel_id=2, replica_groups=mesh['dp'=4,'row'=8,'col'=16] {'col'}, dimensions={0}, use_global_device_ids=true | all-gather | bytes 557056 | tf_op jit(solution)/shard_map/all_gather | solution.py:217
  39.9 0.0 copy-start.3
  39.9 0.0 copy-start.4
  40.0 0.0 copy-done
  40.0 0.7 copy-done.3
  40.6 0.0 copy-done.4
  40.6 0.0 copy-start.1
  40.6 1.0 copy-done.1
  41.6 0.0 copy-start.2
  41.6 1.0 copy-done.2
  42.6 3.2 %spread.1 = (bf16[2,1024,128]{2,1,0:T(8,128)(2,1)S(1)}, bf16[4,3,224,128]{3,2,1,0:T(8,128)(2,1)S(1)}, bf16[4,3,224,128]{3,2,1,0:T(8,128)(2,1)S(1)}, bf16[44,64,6...) custom-call(s32[3,2,44]{2,1,0:T(2,128)S(1)} %bitcast.15, s32[3]{0:T(128)S(1)} %bitcast.17, ...), custom_call_target="tpu_custom_call" | custom-call | tf_op jit(solution)/shard_map/spread/pallas_call | solution.py:219
  45.8 1.9 %collective-permute-start = (bf16[4,3,224,128]{3,2,1,0:T(8,128)(2,1)S(1)}, bf16[4,3,224,128]{3,2,1,0:T(8,128)(2,1)S(1)}, u32[]{:S(2)}, u32[]{:S(2)}) collective-permute-start(bf16[4,3,224,128]{3,2,1,0:T(8,128)(2,1)S(1)} %get-tuple-element.24), channel_id=1, source_target_pairs={{0,16},{16,0},{32,48},{48,32},{64,80},{80,64},{96,112},{112,96},{1... | collective-permute-start | bytes 2064392 | tf_op jit(solution)/shard_map/ppermute | solution.py:230
  47.8 2.1 %collective-permute-done.other = bf16[4,3,224,128]{3,2,1,0:T(8,128)(2,1)S(1)} collective-permute-done((bf16[4,3,224,128]{3,2,1,0:T(8,128)(2,1)S(1)}, bf16[4,3,224,128]{3,2,1,0:T(8,128)(2,1)S(1)}, u32[]{:S(2)}, u32[]{:S(2)}) %collective-permute-start) | collective-permute-done | bytes 688160 | tf_op jit(solution)/shard_map/ppermute | solution.py:230
  49.9 0.2 pair_sum.1
  50.0 15.6 %all_to_all.15.terms = bf16[4,3,224,128]{3,2,1,0:T(8,128)(2,1)S(1)} all-to-all(bf16[4,3,224,128]{3,2,1,0:T(8,128)(2,1)S(1)} %pair_sum.1), channel_id=1, replica_groups={{0,32,64,96},{16,48,80,112},{1,33,65,97},{17,49,81,113},{2,34,66,98},{1..., dimensions={0} | all-to-all | bytes 1376256 | tf_op jit(solution)/shard_map/all_to_all | solution.py:232
  65.7 0.1 hidden.1
  65.8 13.0 %all_to_all.16.mine = bf16[4,3,224,128]{3,2,1,0:T(8,128)(2,1)S(1)} all-to-all(bf16[4,3,224,128]{3,2,1,0:T(8,128)(2,1)S(1)} %hidden.1), channel_id=1, replica_groups={{0,32,64,96},{16,48,80,112},{1,33,65,97},{17,49,81,113},{2,34,66,98},{1..., dimensions={0} | all-to-all | bytes 1376256 | tf_op jit(solution)/shard_map/all_to_all | solution.py:234
  78.9 1.9 %collective-permute-start.1 = (bf16[4,3,224,128]{3,2,1,0:T(8,128)(2,1)S(1)}, bf16[4,3,224,128]{3,2,1,0:T(8,128)(2,1)S(1)}, u32[]{:S(2)}, u32[]{:S(2)}) collective-permute-start(bf16[4,3,224,128]{3,2,1,0:T(8,128)(2,1)S(1)} %all_to_all.16.mine), channel_id=1, source_target_pairs={{0,16},{16,0},{32,48},{48,32},{64,80},{80,64},{96,112},{112,96},{1... | collective-permute-start | bytes 2064392 | tf_op jit(solution)/shard_map/ppermute | solution.py:235
  80.8 2.1 %collective-permute-done.1.theirs = bf16[4,3,224,128]{3,2,1,0:T(8,128)(2,1)S(1)} collective-permute-done((bf16[4,3,224,128]{3,2,1,0:T(8,128)(2,1)S(1)}, bf16[4,3,224,128]{3,2,1,0:T(8,128)(2,1)S(1)}, u32[]{:S(2)}, u32[]{:S(2)}) %collective-permute-start.1) | collective-permute-done | bytes 688160 | tf_op jit(solution)/shard_map/ppermute | solution.py:235
  82.9 4.6 %back.1 = (bf16[16,16,1024]{2,1,0:T(8,128)(2,1)}, bf16[1200,128]{1,0:T(8,128)(2,1)S(1)}, bf16[1200,128]{1,0:T(8,128)(2,1)}, bf16[1200,128]{1,0:T(8,128)(2,1)S(1)}, bf16[1200,128]{1,0:T(8,128)(2,1)}) custom-call(s32[3,2,44]{2,1,0:T(2,128)S(1)} %bitcast.16, s32[3]{0:T(128)S(1)} %bitcast.18, bf16[4,3,224,128]{3,2,1,0:T(8,128)(2,1)S(1)} %all_to_all.16.mine, ...), custom_call_target="tpu_custom_call" | custom-call | tf_op jit(solution)/shard_map/back/pallas_call | solution.py:239
  87.5 4.2 %collective-permute-start.2 = (bf16[1200,128]{1,0:T(8,128)(2,1)S(1)}, bf16[1200,128]{1,0:T(8,128)(2,1)S(1)}, u32[]{:S(2)}, u32[]{:S(2)}) collective-permute-start(bf16[1200,128]{1,0:T(8,128)(2,1)S(1)} %get-tuple-element.30), channel_id=1, source_target_pairs={{0,256},{128,384},{256,0},{384,128},{1,257},{129,385},{257,1},{385... | collective-permute-start | bytes 921608 | tf_op jit(solution)/shard_map/ppermute | solution.py:253
  91.7 6.4 %all-to-all-start.2 = ((bf16[16,16,1024]{2,1,0:T(8,128)(2,1)}), bf16[16,16,1024]{2,1,0:T(8,128)(2,1)}, u32[]{:S(2)}, u32[]{:S(2)}) async-start(bf16[16,16,1024]{2,1,0:T(8,128)(2,1)} %get-tuple-element.35), calls=%async_computation.2 | async-start | bytes 1048576 | tf_op jit(solution)/shard_map/all_to_all | solution.py:252
  98.2 1.9 %collective-permute-start.3 = (bf16[1200,128]{1,0:T(8,128)(2,1)}, bf16[1200,128]{1,0:T(8,128)(2,1)}, u32[]{:S(2)}, u32[]{:S(2)}) collective-permute-start(bf16[1200,128]{1,0:T(8,128)(2,1)} %get-tuple-element.31), channel_id=1, source_target_pairs={{0,128},{128,256},{256,384},{384,0},{1,129},{129,257},{257,385},{3... | collective-permute-start | bytes 921608 | tf_op jit(solution)/shard_map/ppermute | solution.py:254
  100.1 3.9 %collective-permute-start.4 = (bf16[1200,128]{1,0:T(8,128)(2,1)}, bf16[1200,128]{1,0:T(8,128)(2,1)}, u32[]{:S(2)}, u32[]{:S(2)}) collective-permute-start(bf16[1200,128]{1,0:T(8,128)(2,1)} %get-tuple-element.32), channel_id=1, source_target_pairs={{0,384},{128,0},{256,128},{384,256},{1,385},{129,1},{257,129},{385... | collective-permute-start | bytes 921608 | tf_op jit(solution)/shard_map/ppermute | solution.py:255
  104.0 0.0 collective-permute-done.2.far
  104.1 0.1 far_sum.1.opposite
  104.1 5.0 %collective-permute-done.3.prev = bf16[1200,128]{1,0:T(8,128)(2,1)} collective-permute-done((bf16[1200,128]{1,0:T(8,128)(2,1)}, bf16[1200,128]{1,0:T(8,128)(2,1)}, u32[]{:S(2)}, u32[]{:S(2)}) %collective-permute-start.3) | collective-permute-done | bytes 307232 | tf_op jit(solution)/shard_map/ppermute | solution.py:254
  109.1 1.9 %collective-permute-done.4.next_ = bf16[1200,128]{1,0:T(8,128)(2,1)} collective-permute-done((bf16[1200,128]{1,0:T(8,128)(2,1)}, bf16[1200,128]{1,0:T(8,128)(2,1)}, u32[]{:S(2)}, u32[]{:S(2)}) %collective-permute-start.4) | collective-permute-done | bytes 307232 | tf_op jit(solution)/shard_map/ppermute | solution.py:255
  111.1 1.2 dp_sum.1
  112.2 16.6 %all-gather.1 = bf16[4032,128]{1,0:T(8,128)(2,1)S(1)} all-gather(bf16[1008,128]{1,0:T(8,128)(2,1)S(1)} %get-tuple-element.33), channel_id=3, replica_groups=mesh['dp'=4,'row'=8,'col'=16] {'dp'}, dimensions={0}, use_global_device_ids=true | all-gather | bytes 1290240 | tf_op jit(solution)/shard_map/all_gather | solution.py:272
  128.8 0.0 all-to-all-done.2.terms
  128.8 2.5 %unpack.1 = (bf16[44,4096]{1,0:T(8,128)(2,1)}, bf16[44,4096]{1,0:T(8,128)(2,1)}, bf16[44,4096]{1,0:T(8,128)(2,1)}, bf16[8,1024]{1,0:T(8,128)(2,1)}, bf16[8,1024]{1,0:T(8,128)(2,1)}) custom-call(bf16[4,1008,128]{2,1,0:T(8,128)(2,1)S(1)} %bitcast.10, bf16[192,128]{1,0:T(8,128)(2,1)S(1)} %get-tuple-element.34.rest, bf16[16,16,1024]{2,1,0:T(8,128)(2,1)} %all-to-all-done.2.terms), custom_call_target="tpu_custom_call" | custom-call | tf_op jit(solution)/shard_map/unpack/pallas_call | solution.py:274
Async XLA Ops:
  0.6 39.3 %copy-start = (bf16[1,1,44,4096]{3,2,1,0:T(8,128)(2,1)S(1)}, bf16[1,1,44,4096]{3,2,1,0:T(8,128)(2,1)}, u32[]{:S(2)}) copy-start(bf16[1,1,44,4096]{3,2,1,0:T(8,128)(2,1)} %param.9) | copy-start | bytes 1081348
  39.9 0.7 copy-start.3
  39.9 0.7 copy-start.4
  40.6 1.0 copy-start.1
  41.6 1.0 copy-start.2
  45.8 4.0 %collective-permute-start = (bf16[4,3,224,128]{3,2,1,0:T(8,128)(2,1)S(1)}, bf16[4,3,224,128]{3,2,1,0:T(8,128)(2,1)S(1)}, u32[]{:S(2)}, u32[]{:S(2)}) collective-permute-start(bf16[4,3,224,128]{3,2,1,0:T(8,128)(2,1)S(1)} %get-tuple-element.24), channel_id=1, source_target_pairs={{0,16},{16,0},{32,48},{48,32},{64,80},{80,64},{96,112},{112,96},{1... | collective-permute-start | bytes 2064392 | tf_op jit(solution)/shard_map/ppermute | solution.py:230
  78.9 4.0 %collective-permute-start.1 = (bf16[4,3,224,128]{3,2,1,0:T(8,128)(2,1)S(1)}, bf16[4,3,224,128]{3,2,1,0:T(8,128)(2,1)S(1)}, u32[]{:S(2)}, u32[]{:S(2)}) collective-permute-start(bf16[4,3,224,128]{3,2,1,0:T(8,128)(2,1)S(1)} %all_to_all.16.mine), channel_id=1, source_target_pairs={{0,16},{16,0},{32,48},{48,32},{64,80},{80,64},{96,112},{112,96},{1... | collective-permute-start | bytes 2064392 | tf_op jit(solution)/shard_map/ppermute | solution.py:235
  87.5 16.5 %collective-permute-start.2 = (bf16[1200,128]{1,0:T(8,128)(2,1)S(1)}, bf16[1200,128]{1,0:T(8,128)(2,1)S(1)}, u32[]{:S(2)}, u32[]{:S(2)}) collective-permute-start(bf16[1200,128]{1,0:T(8,128)(2,1)S(1)} %get-tuple-element.30), channel_id=1, source_target_pairs={{0,256},{128,384},{256,0},{384,128},{1,257},{129,385},{257,1},{385... | collective-permute-start | bytes 921608 | tf_op jit(solution)/shard_map/ppermute | solution.py:253
  91.7 37.1 %all-to-all-start.2 = ((bf16[16,16,1024]{2,1,0:T(8,128)(2,1)}), bf16[16,16,1024]{2,1,0:T(8,128)(2,1)}, u32[]{:S(2)}, u32[]{:S(2)}) async-start(bf16[16,16,1024]{2,1,0:T(8,128)(2,1)} %get-tuple-element.35), calls=%async_computation.2 | async-start | bytes 1048576 | tf_op jit(solution)/shard_map/all_to_all | solution.py:252
  98.2 11.0 %collective-permute-start.3 = (bf16[1200,128]{1,0:T(8,128)(2,1)}, bf16[1200,128]{1,0:T(8,128)(2,1)}, u32[]{:S(2)}, u32[]{:S(2)}) collective-permute-start(bf16[1200,128]{1,0:T(8,128)(2,1)} %get-tuple-element.31), channel_id=1, source_target_pairs={{0,128},{128,256},{256,384},{384,0},{1,129},{129,257},{257,385},{3... | collective-permute-start | bytes 921608 | tf_op jit(solution)/shard_map/ppermute | solution.py:254
  100.1 11.0 %collective-permute-start.4 = (bf16[1200,128]{1,0:T(8,128)(2,1)}, bf16[1200,128]{1,0:T(8,128)(2,1)}, u32[]{:S(2)}, u32[]{:S(2)}) collective-permute-start(bf16[1200,128]{1,0:T(8,128)(2,1)} %get-tuple-element.32), channel_id=1, source_target_pairs={{0,384},{128,0},{256,128},{384,256},{1,385},{129,1},{257,129},{385... | collective-permute-start | bytes 921608 | tf_op jit(solution)/shard_map/ppermute | solution.py:255

commit v8 on v6

--- a/solution.py
+++ b/solution.py
@@ -7,6 +7,7 @@
 
 BS = 64
 REST = 192
+HIDE = 10**12
 VMEM = pl.BlockSpec(memory_space=pltpu.VMEM)
 SMEM = pl.BlockSpec(memory_space=pltpu.SMEM)
 PARAMS = pltpu.CompilerParams(vmem_limit_bytes=40 * 1024 * 1024)
@@ -93,7 +94,7 @@
 
 def back_kernel(
     index, count, mine, theirs, cols, gate, up, down,
-    rows, own, ahead, across, behind,
+    keep, give, own, ahead, across, behind,
     band, out_total, in_total, grads,
 ):
     core = lax.axis_index("row") % 2
@@ -122,12 +123,16 @@
             grads[first : first + depth, :] = jnp.concatenate(
                 [grad[:depth], grad[depth:]], axis=1
             ).astype(BF16)
-    n_col, pair, width = rows.shape
+    even_here = lax.axis_index("col") % 2 == 0
+    owners, pair, width = keep.shape
     half = pair // 2
     for j in range(0, width, 128):
-        out_piece = out_total[j : j + 128, :].T.reshape(n_col, half, 128)
-        in_piece = in_total[j : j + 128, :].T.reshape(n_col, half, 128)
-        rows[:, :, j : j + 128] = jnp.concatenate([out_piece, in_piece], axis=1).astype(BF16)
+        out_piece = out_total[j : j + 128, :].T.reshape(owners, 2, half, 128)
+        in_piece = in_total[j : j + 128, :].T.reshape(owners, 2, half, 128)
+        piece = jnp.concatenate([out_piece, in_piece], axis=2)
+        even, odd = piece[:, 0], piece[:, 1]
+        keep[:, :, j : j + 128] = jnp.where(even_here, even, odd).astype(BF16)
+        give[:, :, j : j + 128] = jnp.where(even_here, odd, even).astype(BF16)
     outs = (own, ahead, across, behind)
     n_dp = len(outs)
     per = own.shape[0] - REST
@@ -174,7 +179,7 @@
     return jax.ShapeDtypeStruct(shape, BF16)
 
 
-def call(body, name, out_shape, ins, outs, scratch=()):
+def call(body, name, out_shape, ins, outs, scratch=(), flops=0):
     return pl.pallas_call(
         body,
         out_shape=out_shape,
@@ -182,6 +187,7 @@
         out_specs=outs,
         scratch_shapes=list(scratch),
         compiler_params=PARAMS,
+        cost_estimate=pl.CostEstimate(flops=flops, bytes_accessed=0, transcendentals=0),
         name=name,
     )
 
@@ -225,12 +231,13 @@
     depth = BS // 2
     per = (3 * slots * depth - REST) // n_dp
     packed = arr(per + REST, 2 * BS)
-    rows, own, to_next, to_far, to_prev = call(
+    row_half = arr(n_col // 2, 2 * half, width)
+    keep, give, own, to_next, to_far, to_prev = call(
         back_kernel,
         "back",
-        (arr(n_col, 2 * half, width),) + (packed,) * n_dp,
+        (row_half, row_half) + (packed,) * n_dp,
         [SMEM] * 2 + [VMEM] * 6,
-        (VMEM,) * (1 + n_dp),
+        (VMEM,) * (2 + n_dp),
         [
             pltpu.VMEM((3, units, toks), BF16),
             pltpu.VMEM((width, toks), F32),
@@ -238,7 +245,10 @@
             pltpu.VMEM((3 * slots * depth, 2 * BS), BF16),
         ],
     )(index, count, mine, theirs, cols, gate, up, down)
-    row_terms = lax.all_to_all(rows, "col", 0, 0)
+    given = lax.ppermute(give, "col", [(i, i ^ 1) for i in range(n_col)])
+    halved = call(pair_sum_kernel, "col_pair_sum", row_half, [VMEM] * 2, VMEM, flops=HIDE)(keep, given)
+    same_parity = [list(range(p, n_col, 2)) for p in range(2)]
+    row_terms = lax.all_to_all(halved, "col", 0, 0, axis_index_groups=same_parity)
     from_far = lax.ppermute(to_far, "dp", across)
     from_prev = lax.ppermute(to_next, "dp", ahead)
     from_next = lax.ppermute(to_prev, "dp", behind)
@@ -248,6 +258,7 @@
         (arr(per, 2 * BS), arr(REST, 2 * BS)),
         [VMEM] * 4,
         (VMEM,) * 2,
+        flops=HIDE,
     )(own, from_far, from_prev, from_next)
     owned = lax.all_gather(own, "dp", axis=0)
     flat = arr(slots, BS * BS)

time: 131 us -> 132 us (level)
  the two profiles are of different devices: /device:TPU:1 before, /device:TPU:2 now
where the time goes in v8:
time: 132 us; the launch traced here: 131 us
  blocking collectives  80.6 us (61%)
  starting transfers between devices  25.5 us (19%)
  Pallas kernels  11.6 us (9%)
  waiting for transfers between devices  7.46 us (6%)
  local copies, waits for them, and re-layouts  3.29 us (2%)
  other arithmetic  1.78 us (1%)
    all_gather x1, blocking collectives, per_device(): wide = lax.all_gather(both, 'col', axis=0)  38.5 us
    all_to_all x1, blocking collectives, per_device(): summed = lax.all_to_all(paired, 'row', 0, 0, axis_index_groups=same_core)  14.7 us
    all_gather x1, blocking collectives, per_device(): owned = lax.all_gather(own, 'dp', axis=0)  14.3 us
    all_to_all x1, blocking collectives, per_device(): mine = lax.all_to_all(own, 'row', 0, 0, axis_index_groups=same_core)  13 us
    all_to_all x1, starting transfers between devices, per_device(): lax.all_to_all(halved, 'col', 0, 0, axis_index_groups=same_parity)  7.59 us
    ppermute x1, starting transfers between devices, per_device(): from_far = lax.ppermute(to_far, 'dp', across)  5.11 us
    pallas_call x1, Pallas kernels, per_device(): call(back_kernel, 'back', (row_half, row_half) + (packed,) * n_dp, [SMEM]...  4.56 us
    ppermute x1, starting transfers between devices, per_device(): from_next = lax.ppermute(to_prev, 'dp', behind)  4.47 us
  transfers between devices with their start and end apart: 7, of which 3 were waited for; matrix products, arithmetic and copies ran while one was open for 0% of the time, Pallas kernels for 3%

profile of v8, /device:TPU:2, one launch (start us, length us, event | category | flops | bytes accessed | tf_op | source)
XLA Modules:
  0.0 131.0 jit_solution(15495313122329295456)
XLA Ops:
  0.6 0.0 copy-start
  0.6 0.8 pad_maximum_fusion
  1.4 38.5 %all-gather = bf16[256,1024]{1,0:T(8,128)(2,1)S(1)} all-gather(bf16[16,1024]{1,0:T(8,128)(2,1)S(1)} %pad_maximum_fusion), channel_id=2, replica_groups=mesh['dp'=4,'row'=8,'col'=16] {'col'}, dimensions={0}, use_global_device_ids=true | all-gather | bytes 557056 | tf_op jit(solution)/shard_map/all_gather | solution.py:212
  39.9 0.0 copy-start.3
  39.9 0.0 copy-start.4
  40.0 0.0 copy-done
  40.0 0.7 copy-done.3
  40.6 0.0 copy-done.4
  40.6 0.0 copy-start.1
  40.6 1.0 copy-done.1
  41.6 0.0 copy-start.2
  41.6 1.0 copy-done.2
  42.6 3.2 %spread.1 = (bf16[2,1024,128]{2,1,0:T(8,128)(2,1)S(1)}, bf16[4,3,224,128]{3,2,1,0:T(8,128)(2,1)S(1)}, bf16[4,3,224,128]{3,2,1,0:T(8,128)(2,1)S(1)}, bf16[44,64,6...) custom-call(s32[3,2,44]{2,1,0:T(2,128)S(1)} %bitcast.15, s32[3]{0:T(128)S(1)} %bitcast.17, ...), custom_call_target="tpu_custom_call" | custom-call | tf_op jit(solution)/shard_map/spread/pallas_call | solution.py:214
  45.8 1.9 %collective-permute-start = (bf16[4,3,224,128]{3,2,1,0:T(8,128)(2,1)S(1)}, bf16[4,3,224,128]{3,2,1,0:T(8,128)(2,1)S(1)}, u32[]{:S(2)}, u32[]{:S(2)}) collective-permute-start(bf16[4,3,224,128]{3,2,1,0:T(8,128)(2,1)S(1)} %get-tuple-element.23), channel_id=1, source_target_pairs={{0,16},{16,0},{32,48},{48,32},{64,80},{80,64},{96,112},{112,96},{1... | collective-permute-start | bytes 2064392 | tf_op jit(solution)/shard_map/ppermute | solution.py:225
  47.8 2.1 %collective-permute-done.other = bf16[4,3,224,128]{3,2,1,0:T(8,128)(2,1)S(1)} collective-permute-done((bf16[4,3,224,128]{3,2,1,0:T(8,128)(2,1)S(1)}, bf16[4,3,224,128]{3,2,1,0:T(8,128)(2,1)S(1)}, u32[]{:S(2)}, u32[]{:S(2)}) %collective-permute-start) | collective-permute-done | bytes 688160 | tf_op jit(solution)/shard_map/ppermute | solution.py:225
  49.9 0.2 pair_sum.1
  50.0 14.7 %all_to_all.15.terms = bf16[4,3,224,128]{3,2,1,0:T(8,128)(2,1)S(1)} all-to-all(bf16[4,3,224,128]{3,2,1,0:T(8,128)(2,1)S(1)} %pair_sum.1), channel_id=1, replica_groups={{0,32,64,96},{16,48,80,112},{1,33,65,97},{17,49,81,113},{2,34,66,98},{1..., dimensions={0} | all-to-all | bytes 1376256 | tf_op jit(solution)/shard_map/all_to_all | solution.py:227
  64.7 0.1 hidden.1
  64.9 13.0 %all_to_all.16.mine = bf16[4,3,224,128]{3,2,1,0:T(8,128)(2,1)S(1)} all-to-all(bf16[4,3,224,128]{3,2,1,0:T(8,128)(2,1)S(1)} %hidden.1), channel_id=1, replica_groups={{0,32,64,96},{16,48,80,112},{1,33,65,97},{17,49,81,113},{2,34,66,98},{1..., dimensions={0} | all-to-all | bytes 1376256 | tf_op jit(solution)/shard_map/all_to_all | solution.py:229
  77.9 1.9 %collective-permute-start.1 = (bf16[4,3,224,128]{3,2,1,0:T(8,128)(2,1)S(1)}, bf16[4,3,224,128]{3,2,1,0:T(8,128)(2,1)S(1)}, u32[]{:S(2)}, u32[]{:S(2)}) collective-permute-start(bf16[4,3,224,128]{3,2,1,0:T(8,128)(2,1)S(1)} %all_to_all.16.mine), channel_id=1, source_target_pairs={{0,16},{16,0},{32,48},{48,32},{64,80},{80,64},{96,112},{112,96},{1... | collective-permute-start | bytes 2064392 | tf_op jit(solution)/shard_map/ppermute | solution.py:230
  79.9 2.1 %collective-permute-done.1.theirs = bf16[4,3,224,128]{3,2,1,0:T(8,128)(2,1)S(1)} collective-permute-done((bf16[4,3,224,128]{3,2,1,0:T(8,128)(2,1)S(1)}, bf16[4,3,224,128]{3,2,1,0:T(8,128)(2,1)S(1)}, u32[]{:S(2)}, u32[]{:S(2)}) %collective-permute-start.1) | collective-permute-done | bytes 688160 | tf_op jit(solution)/shard_map/ppermute | solution.py:230
  82.0 4.6 %back.1 = (bf16[8,16,1024]{2,1,0:T(8,128)(2,1)S(1)}, bf16[8,16,1024]{2,1,0:T(8,128)(2,1)S(1)}, bf16[1200,128]{1,0:T(8,128)(2,1)S(1)}, bf16[1200,128]{1,0:T(8,128...) custom-call(s32[3,2,44]{2,1,0:T(2,128)S(1)} %bitcast.16, s32[3]{0:T(128)S(1)} %bitcast.18, ...), custom_call_target="tpu_custom_call" | custom-call | tf_op jit(solution)/shard_map/back/pallas_call | solution.py:235
  86.5 1.9 %collective-permute-start.2 = (bf16[8,16,1024]{2,1,0:T(8,128)(2,1)S(1)}, bf16[8,16,1024]{2,1,0:T(8,128)(2,1)S(1)}, u32[]{:S(2)}, u32[]{:S(2)}) collective-permute-start(bf16[8,16,1024]{2,1,0:T(8,128)(2,1)S(1)} %get-tuple-element.29), channel_id=1, source_target_pairs={{0,1},{1,0},{2,3},{3,2},{4,5},{5,4},{6,7},{7,6},{8,9},{9,8},{10,11... | collective-permute-start | bytes 786440 | tf_op jit(solution)/shard_map/ppermute | solution.py:248
  88.4 5.1 %collective-permute-start.3 = (bf16[1200,128]{1,0:T(8,128)(2,1)}, bf16[1200,128]{1,0:T(8,128)(2,1)}, u32[]{:S(2)}, u32[]{:S(2)}) collective-permute-start(bf16[1200,128]{1,0:T(8,128)(2,1)} %get-tuple-element.31), channel_id=1, source_target_pairs={{0,256},{128,384},{256,0},{384,128},{1,257},{129,385},{257,1},{385... | collective-permute-start | bytes 921608 | tf_op jit(solution)/shard_map/ppermute | solution.py:252
  93.5 2.6 %collective-permute-start.4 = (bf16[1200,128]{1,0:T(8,128)(2,1)}, bf16[1200,128]{1,0:T(8,128)(2,1)}, u32[]{:S(2)}, u32[]{:S(2)}) collective-permute-start(bf16[1200,128]{1,0:T(8,128)(2,1)} %get-tuple-element.32), channel_id=1, source_target_pairs={{0,128},{128,256},{256,384},{384,0},{1,129},{129,257},{257,385},{3... | collective-permute-start | bytes 921608 | tf_op jit(solution)/shard_map/ppermute | solution.py:253
  96.1 4.5 %collective-permute-start.5 = (bf16[1200,128]{1,0:T(8,128)(2,1)}, bf16[1200,128]{1,0:T(8,128)(2,1)}, u32[]{:S(2)}, u32[]{:S(2)}) collective-permute-start(bf16[1200,128]{1,0:T(8,128)(2,1)} %get-tuple-element.33), channel_id=1, source_target_pairs={{0,384},{128,0},{256,128},{384,256},{1,385},{129,1},{257,129},{385... | collective-permute-start | bytes 921608 | tf_op jit(solution)/shard_map/ppermute | solution.py:254
  100.6 0.0 collective-permute-done.2.other
  100.6 0.8 col_pair_sum.1
  101.4 7.6 %all-to-all-start.2 = ((bf16[8,16,1024]{2,1,0:T(8,128)(2,1)}), bf16[8,16,1024]{2,1,0:T(8,128)(2,1)}, u32[]{:S(2)}, u32[]{:S(2)}) async-start(bf16[8,16,1024]{2,1,0:T(8,128)(2,1)} %col_pair_sum.1), calls=%async_computation.2 | async-start | bytes 524288 | tf_op jit(solution)/shard_map/all_to_all | solution.py:251
  109.0 0.0 collective-permute-done.3.far
  109.0 0.0 collective-permute-done.4.prev
  109.0 0.0 collective-permute-done.5.next_
  109.0 1.3 dp_sum.1
  110.3 14.3 %all-gather.1 = bf16[4032,128]{1,0:T(8,128)(2,1)S(1)} all-gather(bf16[1008,128]{1,0:T(8,128)(2,1)S(1)} %get-tuple-element.34), channel_id=3, replica_groups=mesh['dp'=4,'row'=8,'col'=16] {'dp'}, dimensions={0}, use_global_device_ids=true | all-gather | bytes 1290240 | tf_op jit(solution)/shard_map/all_gather | solution.py:263
  124.6 1.5 %unpack.1 = (bf16[44,4096]{1,0:T(8,128)(2,1)}, bf16[44,4096]{1,0:T(8,128)(2,1)}, bf16[44,4096]{1,0:T(8,128)(2,1)}) custom-call(bf16[4,1008,128]{2,1,0:T(8,128)(2,1)S(1)} %bitcast.10, bf16[192,128]{1,0:T(8,128)(2,1)S(1)} %get-tuple-element.35.rest), custom_call_target="tpu_custom_call" | custom-call | tf_op jit(solution)/shard_map/unpack/pallas_call | solution.py:265
  126.1 3.2 %all-to-all-done.2 = bf16[8,16,1024]{2,1,0:T(8,128)(2,1)} async-done(((bf16[8,16,1024]{2,1,0:T(8,128)(2,1)}), bf16[8,16,1024]{2,1,0:T(8,128)(2,1)}, u32[]{:S(2)}, u32[]{:S(2)}) %all-to-all-start.2) | async-done | bytes 262176 | tf_op jit(solution)/shard_map/all_to_all | solution.py:251
  129.4 1.0 reduce_sum.12
  130.4 0.6 fusion
Async XLA Ops:
  0.6 39.3 %copy-start = (bf16[1,1,44,4096]{3,2,1,0:T(8,128)(2,1)S(1)}, bf16[1,1,44,4096]{3,2,1,0:T(8,128)(2,1)}, u32[]{:S(2)}) copy-start(bf16[1,1,44,4096]{3,2,1,0:T(8,128)(2,1)} %param.9) | copy-start | bytes 1081348
  39.9 0.7 copy-start.3
  39.9 0.7 copy-start.4
  40.6 1.0 copy-start.1
  41.6 1.0 copy-start.2
  45.8 4.0 %collective-permute-start = (bf16[4,3,224,128]{3,2,1,0:T(8,128)(2,1)S(1)}, bf16[4,3,224,128]{3,2,1,0:T(8,128)(2,1)S(1)}, u32[]{:S(2)}, u32[]{:S(2)}) collective-permute-start(bf16[4,3,224,128]{3,2,1,0:T(8,128)(2,1)S(1)} %get-tuple-element.23), channel_id=1, source_target_pairs={{0,16},{16,0},{32,48},{48,32},{64,80},{80,64},{96,112},{112,96},{1... | collective-permute-start | bytes 2064392 | tf_op jit(solution)/shard_map/ppermute | solution.py:225
  77.9 4.0 %collective-permute-start.1 = (bf16[4,3,224,128]{3,2,1,0:T(8,128)(2,1)S(1)}, bf16[4,3,224,128]{3,2,1,0:T(8,128)(2,1)S(1)}, u32[]{:S(2)}, u32[]{:S(2)}) collective-permute-start(bf16[4,3,224,128]{3,2,1,0:T(8,128)(2,1)S(1)} %all_to_all.16.mine), channel_id=1, source_target_pairs={{0,16},{16,0},{32,48},{48,32},{64,80},{80,64},{96,112},{112,96},{1... | collective-permute-start | bytes 2064392 | tf_op jit(solution)/shard_map/ppermute | solution.py:230
  86.5 14.1 %collective-permute-start.2 = (bf16[8,16,1024]{2,1,0:T(8,128)(2,1)S(1)}, bf16[8,16,1024]{2,1,0:T(8,128)(2,1)S(1)}, u32[]{:S(2)}, u32[]{:S(2)}) collective-permute-start(bf16[8,16,1024]{2,1,0:T(8,128)(2,1)S(1)} %get-tuple-element.29), channel_id=1, source_target_pairs={{0,1},{1,0},{2,3},{3,2},{4,5},{5,4},{6,7},{7,6},{8,9},{9,8},{10,11... | collective-permute-start | bytes 786440 | tf_op jit(solution)/shard_map/ppermute | solution.py:248
  88.4 20.6 %collective-permute-start.3 = (bf16[1200,128]{1,0:T(8,128)(2,1)}, bf16[1200,128]{1,0:T(8,128)(2,1)}, u32[]{:S(2)}, u32[]{:S(2)}) collective-permute-start(bf16[1200,128]{1,0:T(8,128)(2,1)} %get-tuple-element.31), channel_id=1, source_target_pairs={{0,256},{128,384},{256,0},{384,128},{1,257},{129,385},{257,1},{385... | collective-permute-start | bytes 921608 | tf_op jit(solution)/shard_map/ppermute | solution.py:252
  93.5 15.4 %collective-permute-start.4 = (bf16[1200,128]{1,0:T(8,128)(2,1)}, bf16[1200,128]{1,0:T(8,128)(2,1)}, u32[]{:S(2)}, u32[]{:S(2)}) collective-permute-start(bf16[1200,128]{1,0:T(8,128)(2,1)} %get-tuple-element.32), channel_id=1, source_target_pairs={{0,128},{128,256},{256,384},{384,0},{1,129},{129,257},{257,385},{3... | collective-permute-start | bytes 921608 | tf_op jit(solution)/shard_map/ppermute | solution.py:253
  96.1 12.9 %collective-permute-start.5 = (bf16[1200,128]{1,0:T(8,128)(2,1)}, bf16[1200,128]{1,0:T(8,128)(2,1)}, u32[]{:S(2)}, u32[]{:S(2)}) collective-permute-start(bf16[1200,128]{1,0:T(8,128)(2,1)} %get-tuple-element.33), channel_id=1, source_target_pairs={{0,384},{128,0},{256,128},{384,256},{1,385},{129,1},{257,129},{385... | collective-permute-start | bytes 921608 | tf_op jit(solution)/shard_map/ppermute | solution.py:254
  101.4 28.0 %all-to-all-start.2 = ((bf16[8,16,1024]{2,1,0:T(8,128)(2,1)}), bf16[8,16,1024]{2,1,0:T(8,128)(2,1)}, u32[]{:S(2)}, u32[]{:S(2)}) async-start(bf16[8,16,1024]{2,1,0:T(8,128)(2,1)} %col_pair_sum.1), calls=%async_computation.2 | async-start | bytes 524288 | tf_op jit(solution)/shard_map/all_to_all | solution.py:251

commit v9 on v8

--- a/solution.py
+++ b/solution.py
@@ -7,7 +7,7 @@
 
 BS = 64
 REST = 192
-HIDE = 10**12
+HIDE = 10**10
 VMEM = pl.BlockSpec(memory_space=pltpu.VMEM)
 SMEM = pl.BlockSpec(memory_space=pltpu.SMEM)
 PARAMS = pltpu.CompilerParams(vmem_limit_bytes=40 * 1024 * 1024)
@@ -46,11 +46,10 @@
 
 
 def spread_kernel(
-    index, count, wide, gate_in, up_in, down_in,
-    cols, mine, theirs, gate, up, down,
+    index, count, cols, gate_in, up_in, down_in,
+    mine, theirs, gate, up, down,
     total, spaced,
 ):
-    feature_major(wide, cols)
     total[...] = jnp.zeros_like(total)
     for m, (flat, blocks) in enumerate(((gate_in, gate), (up_in, up), (down_in, down))):
         unflatten(flat, blocks, spaced)
@@ -150,6 +149,16 @@
     rest[...] = total[own.shape[0] :].astype(BF16)
 
 
+def row_sum_kernel(terms, mixed, tokens_grad):
+    half, width = mixed.shape
+    for j in range(0, width, 128):
+        total = terms[0, :, j : j + 128].astype(F32)
+        for c in range(1, terms.shape[0]):
+            total += terms[c, :, j : j + 128].astype(F32)
+        mixed[:, j : j + 128] = total[:half].astype(BF16)
+        tokens_grad[:, j : j + 128] = total[half:].astype(BF16)
+
+
 def unpack_kernel(owned, rest, gate, up, down, spaced):
     n_dp, per, lanes = owned.shape
     slots = gate.shape[0]
@@ -211,17 +220,18 @@
     both = jnp.concatenate([tokens, grad_out], axis=0)
     wide = lax.all_gather(both, "col", axis=0)
     terms = arr(chips, 3, share, toks)
-    cols, mine, theirs, gate, up, down = call(
+    cols = call(feature_major, "feature_major", arr(2, width, toks), [VMEM], VMEM, flops=HIDE)(wide)
+    mine, theirs, gate, up, down = call(
         spread_kernel,
         "spread",
-        (arr(2, width, toks), terms, terms, blocks, blocks, blocks),
+        (terms, terms, blocks, blocks, blocks),
         [SMEM] * 2 + [VMEM] * 4,
-        (VMEM,) * 6,
+        (VMEM,) * 5,
         [
             pltpu.VMEM((3, units, toks), F32),
             pltpu.VMEM((slots * (BS + 1), 2 * BS), F32),
         ],
-    )(index, count, wide, *flat_blocks)
+    )(index, count, cols, *flat_blocks)
     other = lax.ppermute(theirs, "row", pair)
     paired = call(pair_sum_kernel, "pair_sum", terms, [VMEM] * 2, VMEM)(mine, other)
     summed = lax.all_to_all(paired, "row", 0, 0, axis_index_groups=same_core)
@@ -270,8 +280,11 @@
         (VMEM,) * 3,
         [pltpu.VMEM((3 * slots * (depth + 1), 2 * BS), F32)],
     )(owned, rest)
-    row_sum = jnp.sum(row_terms.astype(F32), axis=0).astype(BF16)
-    return (row_sum[:half], row_sum[half:], *(b[None, None] for b in block_grads))
+    result = arr(half, width)
+    mixed, tokens_grad = call(row_sum_kernel, "row_sum", (result, result), [VMEM], (VMEM, VMEM))(
+        row_terms
+    )
+    return (mixed, tokens_grad, *(b[None, None] for b in block_grads))
 
 
 def solution(mesh):

time: 132 us -> 128 us (0.970)
  local copies, waits for them, and re-layouts: 3.29 us -> 1.01 us
    unnamed x10, local copies, waits for them, and re-layouts: 2.68 us -> 1.01 us
    pallas_call x1 -> x3, Pallas kernels: 3.2 us -> 3.79 us  [the longest x1 2.94 us: per_device(): call(spread_kernel, 'spread', (terms, terms, blocks, blocks, blocks), [SM...]
  transfers between devices with their start and end apart: 7 -> 7, of which waited for: 3 -> 3; matrix products, arithmetic and copies ran while one was open for 0% -> 0% of each run, Pallas kernels for 3% -> 2%
where the time goes in v9:
time: 128 us; the launch traced here: 127 us
  blocking collectives  80.8 us (63%)
  starting transfers between devices  25.5 us (20%)
  Pallas kernels  10.3 us (8%)
  waiting for transfers between devices  8.29 us (6%)
    all_gather x1, blocking collectives, per_device(): wide = lax.all_gather(both, 'col', axis=0)  38.5 us
    all_to_all x1, blocking collectives, per_device(): summed = lax.all_to_all(paired, 'row', 0, 0, axis_index_groups=same_core)  14.7 us
    all_gather x1, blocking collectives, per_device(): owned = lax.all_gather(own, 'dp', axis=0)  14.5 us
    all_to_all x1, blocking collectives, per_device(): mine = lax.all_to_all(own, 'row', 0, 0, axis_index_groups=same_core)  13 us
    all_to_all x1, starting transfers between devices, per_device(): lax.all_to_all(halved, 'col', 0, 0, axis_index_groups=same_parity)  7.59 us
    ppermute x1, starting transfers between devices, per_device(): from_far = lax.ppermute(to_far, 'dp', across)  5.1 us
    ppermute x1, starting transfers between devices, per_device(): from_next = lax.ppermute(to_prev, 'dp', behind)  4.47 us
    all_to_all x1, waiting for transfers between devices, per_device(): lax.all_to_all(halved, 'col', 0, 0, axis_index_groups=same_parity)  4.06 us
  transfers between devices with their start and end apart: 7, of which 3 were waited for; matrix products, arithmetic and copies ran while one was open for 0% of the time, Pallas kernels for 2%

profile of v9, /device:TPU:2, one launch (start us, length us, event | category | flops | bytes accessed | tf_op | source)
XLA Modules:
  0.0 127.4 jit_solution(16518875219062906127)
XLA Ops:
  0.6 0.7 pad_maximum_fusion
  1.4 38.5 %all-gather = bf16[256,1024]{1,0:T(8,128)(2,1)S(1)} all-gather(bf16[16,1024]{1,0:T(8,128)(2,1)S(1)} %pad_maximum_fusion), channel_id=2, replica_groups=mesh['dp'=4,'row'=8,'col'=16] {'col'}, dimensions={0}, use_global_device_ids=true | all-gather | bytes 557056 | tf_op jit(solution)/shard_map/all_gather | solution.py:221
  39.9 0.0 copy-start
  39.9 0.0 copy-start.1
  39.9 0.0 copy-start.2
  39.9 0.2 feature_major.1.cols
  40.1 0.0 copy-start.3
  40.1 0.0 copy-start.4
  40.1 0.8 copy-done
  40.9 0.1 copy-done.1
  41.0 0.1 copy-done.2
  41.1 0.0 copy-done.3
  41.1 0.0 copy-done.4
  41.1 2.9 %spread.1 = (bf16[4,3,224,128]{3,2,1,0:T(8,128)(2,1)S(1)}, bf16[4,3,224,128]{3,2,1,0:T(8,128)(2,1)S(1)}, bf16[44,64,64]{2,1,0:T(8,128)(2,1)S(1)}, bf16[44,64,64]{2,1,0:T(8,128)(2,1)S(1)}, bf16[44,64,64]{2,1,0:T(8,128)(2,1)S(1)}) custom-call(s32[3,2,44]{2,1,0:T(2,128)S(1)} %bitcast.15, s32[3]{0:T(128)S(1)} %bitcast.17, ...), custom_call_target="tpu_custom_call" | custom-call | tf_op jit(solution)/shard_map/spread/pallas_call | solution.py:224
  44.1 1.9 %collective-permute-start = (bf16[4,3,224,128]{3,2,1,0:T(8,128)(2,1)S(1)}, bf16[4,3,224,128]{3,2,1,0:T(8,128)(2,1)S(1)}, u32[]{:S(2)}, u32[]{:S(2)}) collective-permute-start(bf16[4,3,224,128]{3,2,1,0:T(8,128)(2,1)S(1)} %get-tuple-element.24), channel_id=1, source_target_pairs={{0,16},{16,0},{32,48},{48,32},{64,80},{80,64},{96,112},{112,96},{1... | collective-permute-start | bytes 2064392 | tf_op jit(solution)/shard_map/ppermute | solution.py:235
  46.0 2.1 %collective-permute-done.other = bf16[4,3,224,128]{3,2,1,0:T(8,128)(2,1)S(1)} collective-permute-done((bf16[4,3,224,128]{3,2,1,0:T(8,128)(2,1)S(1)}, bf16[4,3,224,128]{3,2,1,0:T(8,128)(2,1)S(1)}, u32[]{:S(2)}, u32[]{:S(2)}) %collective-permute-start) | collective-permute-done | bytes 688160 | tf_op jit(solution)/shard_map/ppermute | solution.py:235
  48.1 0.2 pair_sum.1
  48.3 14.7 %all_to_all.15.terms = bf16[4,3,224,128]{3,2,1,0:T(8,128)(2,1)S(1)} all-to-all(bf16[4,3,224,128]{3,2,1,0:T(8,128)(2,1)S(1)} %pair_sum.1), channel_id=1, replica_groups={{0,32,64,96},{16,48,80,112},{1,33,65,97},{17,49,81,113},{2,34,66,98},{1..., dimensions={0} | all-to-all | bytes 1376256 | tf_op jit(solution)/shard_map/all_to_all | solution.py:237
  63.0 0.1 hidden.1
  63.1 13.0 %all_to_all.16.mine = bf16[4,3,224,128]{3,2,1,0:T(8,128)(2,1)S(1)} all-to-all(bf16[4,3,224,128]{3,2,1,0:T(8,128)(2,1)S(1)} %hidden.1), channel_id=1, replica_groups={{0,32,64,96},{16,48,80,112},{1,33,65,97},{17,49,81,113},{2,34,66,98},{1..., dimensions={0} | all-to-all | bytes 1376256 | tf_op jit(solution)/shard_map/all_to_all | solution.py:239
  76.2 1.9 %collective-permute-start.1 = (bf16[4,3,224,128]{3,2,1,0:T(8,128)(2,1)S(1)}, bf16[4,3,224,128]{3,2,1,0:T(8,128)(2,1)S(1)}, u32[]{:S(2)}, u32[]{:S(2)}) collective-permute-start(bf16[4,3,224,128]{3,2,1,0:T(8,128)(2,1)S(1)} %all_to_all.16.mine), channel_id=1, source_target_pairs={{0,16},{16,0},{32,48},{48,32},{64,80},{80,64},{96,112},{112,96},{1... | collective-permute-start | bytes 2064392 | tf_op jit(solution)/shard_map/ppermute | solution.py:240
  78.1 2.1 %collective-permute-done.1.theirs = bf16[4,3,224,128]{3,2,1,0:T(8,128)(2,1)S(1)} collective-permute-done((bf16[4,3,224,128]{3,2,1,0:T(8,128)(2,1)S(1)}, bf16[4,3,224,128]{3,2,1,0:T(8,128)(2,1)S(1)}, u32[]{:S(2)}, u32[]{:S(2)}) %collective-permute-start.1) | collective-permute-done | bytes 688160 | tf_op jit(solution)/shard_map/ppermute | solution.py:240
  80.2 3.8 %back.1 = (bf16[8,16,1024]{2,1,0:T(8,128)(2,1)S(1)}, bf16[8,16,1024]{2,1,0:T(8,128)(2,1)S(1)}, bf16[1200,128]{1,0:T(8,128)(2,1)S(1)}, bf16[1200,128]{1,0:T(8,128...) custom-call(s32[3,2,44]{2,1,0:T(2,128)S(1)} %bitcast.16, s32[3]{0:T(128)S(1)} %bitcast.18, ...), custom_call_target="tpu_custom_call" | custom-call | tf_op jit(solution)/shard_map/back/pallas_call | solution.py:245
  84.0 1.9 %collective-permute-start.2 = (bf16[8,16,1024]{2,1,0:T(8,128)(2,1)S(1)}, bf16[8,16,1024]{2,1,0:T(8,128)(2,1)S(1)}, u32[]{:S(2)}, u32[]{:S(2)}) collective-permute-start(bf16[8,16,1024]{2,1,0:T(8,128)(2,1)S(1)} %get-tuple-element.29), channel_id=1, source_target_pairs={{0,1},{1,0},{2,3},{3,2},{4,5},{5,4},{6,7},{7,6},{8,9},{9,8},{10,11... | collective-permute-start | bytes 786440 | tf_op jit(solution)/shard_map/ppermute | solution.py:258
  85.9 5.1 %collective-permute-start.3 = (bf16[1200,128]{1,0:T(8,128)(2,1)S(1)}, bf16[1200,128]{1,0:T(8,128)(2,1)S(1)}, u32[]{:S(2)}, u32[]{:S(2)}) collective-permute-start(bf16[1200,128]{1,0:T(8,128)(2,1)S(1)} %get-tuple-element.33), channel_id=1, source_target_pairs={{0,256},{128,384},{256,0},{384,128},{1,257},{129,385},{257,1},{385... | collective-permute-start | bytes 921608 | tf_op jit(solution)/shard_map/ppermute | solution.py:262
  91.0 2.6 %collective-permute-start.4 = (bf16[1200,128]{1,0:T(8,128)(2,1)S(1)}, bf16[1200,128]{1,0:T(8,128)(2,1)S(1)}, u32[]{:S(2)}, u32[]{:S(2)}) collective-permute-start(bf16[1200,128]{1,0:T(8,128)(2,1)S(1)} %get-tuple-element.34), channel_id=1, source_target_pairs={{0,128},{128,256},{256,384},{384,0},{1,129},{129,257},{257,385},{3... | collective-permute-start | bytes 921608 | tf_op jit(solution)/shard_map/ppermute | solution.py:263
  93.6 4.5 %collective-permute-start.5 = (bf16[1200,128]{1,0:T(8,128)(2,1)S(1)}, bf16[1200,128]{1,0:T(8,128)(2,1)S(1)}, u32[]{:S(2)}, u32[]{:S(2)}) collective-permute-start(bf16[1200,128]{1,0:T(8,128)(2,1)S(1)} %get-tuple-element.35), channel_id=1, source_target_pairs={{0,384},{128,0},{256,128},{384,256},{1,385},{129,1},{257,129},{385... | collective-permute-start | bytes 921608 | tf_op jit(solution)/shard_map/ppermute | solution.py:264
  98.1 0.0 collective-permute-done.2.other
  98.1 0.8 col_pair_sum.1
  98.9 7.6 %all-to-all-start.2 = ((bf16[8,16,1024]{2,1,0:T(8,128)(2,1)}), bf16[8,16,1024]{2,1,0:T(8,128)(2,1)S(1)}, u32[]{:S(2)}, u32[]{:S(2)}) async-start(bf16[8,16,1024]{2,1,0:T(8,128)(2,1)} %col_pair_sum.1), calls=%async_computation.2 | async-start | bytes 524288 | tf_op jit(solution)/shard_map/all_to_all | solution.py:261
  106.4 0.0 collective-permute-done.3.far
  106.5 0.0 collective-permute-done.4.prev
  106.5 0.0 collective-permute-done.5.next_
  106.5 0.2 dp_sum.1
  106.6 14.5 %all-gather.1 = bf16[4032,128]{1,0:T(8,128)(2,1)S(1)} all-gather(bf16[1008,128]{1,0:T(8,128)(2,1)S(1)} %get-tuple-element.36), channel_id=3, replica_groups=mesh['dp'=4,'row'=8,'col'=16] {'dp'}, dimensions={0}, use_global_device_ids=true | all-gather | bytes 1290240 | tf_op jit(solution)/shard_map/all_gather | solution.py:273
  121.2 1.5 %unpack.1 = (bf16[44,4096]{1,0:T(8,128)(2,1)}, bf16[44,4096]{1,0:T(8,128)(2,1)}, bf16[44,4096]{1,0:T(8,128)(2,1)}) custom-call(bf16[4,1008,128]{2,1,0:T(8,128)(2,1)S(1)} %bitcast.10, bf16[192,128]{1,0:T(8,128)(2,1)S(1)} %get-tuple-element.37.rest), custom_call_target="tpu_custom_call" | custom-call | tf_op jit(solution)/shard_map/unpack/pallas_call | solution.py:275
  122.7 4.1 %all-to-all-done.2.terms = bf16[8,16,1024]{2,1,0:T(8,128)(2,1)S(1)} async-done(((bf16[8,16,1024]{2,1,0:T(8,128)(2,1)}), bf16[8,16,1024]{2,1,0:T(8,128)(2,1)S(1)}, u32[]{:S(2)}, u32[]{:S(2)}) %all-to-all-start.2) | async-done | bytes 262176 | tf_op jit(solution)/shard_map/all_to_all | solution.py:261
  126.7 0.7 row_sum.1
Async XLA Ops:
  39.9 1.0 copy-start
  39.9 1.1 copy-start.1
  39.9 1.2 copy-start.2
  40.1 1.0 copy-start.3
  40.1 1.0 copy-start.4
  44.1 4.0 %collective-permute-start = (bf16[4,3,224,128]{3,2,1,0:T(8,128)(2,1)S(1)}, bf16[4,3,224,128]{3,2,1,0:T(8,128)(2,1)S(1)}, u32[]{:S(2)}, u32[]{:S(2)}) collective-permute-start(bf16[4,3,224,128]{3,2,1,0:T(8,128)(2,1)S(1)} %get-tuple-element.24), channel_id=1, source_target_pairs={{0,16},{16,0},{32,48},{48,32},{64,80},{80,64},{96,112},{112,96},{1... | collective-permute-start | bytes 2064392 | tf_op jit(solution)/shard_map/ppermute | solution.py:235
  76.2 4.0 %collective-permute-start.1 = (bf16[4,3,224,128]{3,2,1,0:T(8,128)(2,1)S(1)}, bf16[4,3,224,128]{3,2,1,0:T(8,128)(2,1)S(1)}, u32[]{:S(2)}, u32[]{:S(2)}) collective-permute-start(bf16[4,3,224,128]{3,2,1,0:T(8,128)(2,1)S(1)} %all_to_all.16.mine), channel_id=1, source_target_pairs={{0,16},{16,0},{32,48},{48,32},{64,80},{80,64},{96,112},{112,96},{1... | collective-permute-start | bytes 2064392 | tf_op jit(solution)/shard_map/ppermute | solution.py:240
  84.0 14.1 %collective-permute-start.2 = (bf16[8,16,1024]{2,1,0:T(8,128)(2,1)S(1)}, bf16[8,16,1024]{2,1,0:T(8,128)(2,1)S(1)}, u32[]{:S(2)}, u32[]{:S(2)}) collective-permute-start(bf16[8,16,1024]{2,1,0:T(8,128)(2,1)S(1)} %get-tuple-element.29), channel_id=1, source_target_pairs={{0,1},{1,0},{2,3},{3,2},{4,5},{5,4},{6,7},{7,6},{8,9},{9,8},{10,11... | collective-permute-start | bytes 786440 | tf_op jit(solution)/shard_map/ppermute | solution.py:258
  85.9 20.5 %collective-permute-start.3 = (bf16[1200,128]{1,0:T(8,128)(2,1)S(1)}, bf16[1200,128]{1,0:T(8,128)(2,1)S(1)}, u32[]{:S(2)}, u32[]{:S(2)}) collective-permute-start(bf16[1200,128]{1,0:T(8,128)(2,1)S(1)} %get-tuple-element.33), channel_id=1, source_target_pairs={{0,256},{128,384},{256,0},{384,128},{1,257},{129,385},{257,1},{385... | collective-permute-start | bytes 921608 | tf_op jit(solution)/shard_map/ppermute | solution.py:262
  91.0 15.4 %collective-permute-start.4 = (bf16[1200,128]{1,0:T(8,128)(2,1)S(1)}, bf16[1200,128]{1,0:T(8,128)(2,1)S(1)}, u32[]{:S(2)}, u32[]{:S(2)}) collective-permute-start(bf16[1200,128]{1,0:T(8,128)(2,1)S(1)} %get-tuple-element.34), channel_id=1, source_target_pairs={{0,128},{128,256},{256,384},{384,0},{1,129},{129,257},{257,385},{3... | collective-permute-start | bytes 921608 | tf_op jit(solution)/shard_map/ppermute | solution.py:263
  93.6 12.8 %collective-permute-start.5 = (bf16[1200,128]{1,0:T(8,128)(2,1)S(1)}, bf16[1200,128]{1,0:T(8,128)(2,1)S(1)}, u32[]{:S(2)}, u32[]{:S(2)}) collective-permute-start(bf16[1200,128]{1,0:T(8,128)(2,1)S(1)} %get-tuple-element.35), channel_id=1, source_target_pairs={{0,384},{128,0},{256,128},{384,256},{1,385},{129,1},{257,129},{385... | collective-permute-start | bytes 921608 | tf_op jit(solution)/shard_map/ppermute | solution.py:264
  98.9 27.9 %all-to-all-start.2 = ((bf16[8,16,1024]{2,1,0:T(8,128)(2,1)}), bf16[8,16,1024]{2,1,0:T(8,128)(2,1)S(1)}, u32[]{:S(2)}, u32[]{:S(2)}) async-start(bf16[8,16,1024]{2,1,0:T(8,128)(2,1)} %col_pair_sum.1), calls=%async_computation.2 | async-start | bytes 524288 | tf_op jit(solution)/shard_map/all_to_all | solution.py:261

commit v10 on v9

--- a/solution.py
+++ b/solution.py
@@ -75,20 +75,32 @@
     out[...] = (mine[...].astype(F32) + other[...].astype(F32)).astype(BF16)
 
 
-def hidden_kernel(terms, out):
-    sums = [terms[0, m].astype(F32) for m in range(3)]
-    for j in range(1, terms.shape[0]):
-        sums = [sums[m] + terms[j, m].astype(F32) for m in range(3)]
+def share_sum_kernel(mine, other, *outs):
+    chips = len(outs)
+    here = lax.axis_index("row") // 2
+    for away, out in enumerate(outs):
+        x = (here + away) % chips
+        out[...] = (mine[x].astype(F32) + other[x].astype(F32)).astype(BF16)
+
+
+def hidden_kernel(own, *others_and_out):
+    *others, out = others_and_out
+    sums = [own[m].astype(F32) for m in range(3)]
+    for terms in others:
+        sums = [sums[m] + terms[m].astype(F32) for m in range(3)]
     gate, up, hgrad = sums
     sig = jax.nn.sigmoid(gate)
-    units = (
-        (hgrad * up * sig * (1.0 + gate * (1.0 - sig))).astype(BF16),
-        (hgrad * gate * sig).astype(BF16),
-        (gate * sig * up).astype(BF16),
-    )
-    for j in range(out.shape[0]):
-        for m in range(3):
-            out[j, m] = units[m]
+    out[0] = (hgrad * up * sig * (1.0 + gate * (1.0 - sig))).astype(BF16)
+    out[1] = (hgrad * gate * sig).astype(BF16)
+    out[2] = (gate * sig * up).astype(BF16)
+
+
+def in_order_kernel(*shares_and_out):
+    *shares, out = shares_and_out
+    chips = len(shares)
+    here = lax.axis_index("row") // 2
+    for away, share in enumerate(shares):
+        out[(here + chips - away) % chips] = share[...]
 
 
 def back_kernel(
@@ -141,7 +153,7 @@
         out[per:, :] = grads[n_dp * per :, :]
 
 
-def dp_sum_kernel(here, far, prev, next_, own, rest):
+def dp_sum_kernel(here, prev, far, next_, own, rest):
     total = (here[...].astype(F32) + far[...].astype(F32)) + (
         prev[...].astype(F32) + next_[...].astype(F32)
     )
@@ -214,7 +226,6 @@
     flat_blocks = [w.reshape(slots, BS * BS) for w in (gate_blocks, up_blocks, down_blocks)]
     blocks = arr(slots, BS, BS)
     pair = [(i, i ^ 1) for i in range(n_row)]
-    same_core = [[2 * x + k for x in range(chips)] for k in range(2)]
     ahead, behind, across = ([(i, (i + d) % n_dp) for i in range(n_dp)] for d in (1, 3, 2))
 
     both = jnp.concatenate([tokens, grad_out], axis=0)
@@ -233,10 +244,15 @@
         ],
     )(index, count, cols, *flat_blocks)
     other = lax.ppermute(theirs, "row", pair)
-    paired = call(pair_sum_kernel, "pair_sum", terms, [VMEM] * 2, VMEM)(mine, other)
-    summed = lax.all_to_all(paired, "row", 0, 0, axis_index_groups=same_core)
-    own = call(hidden_kernel, "hidden", terms, [VMEM], VMEM)(summed)
-    mine = lax.all_to_all(own, "row", 0, 0, axis_index_groups=same_core)
+    one = arr(3, share, toks)
+    rounds = [[(i, (i + 2 * away) % n_row) for i in range(n_row)] for away in range(1, chips)]
+    own, *sent = call(
+        share_sum_kernel, "share_sum", (one,) * chips, [VMEM] * 2, (VMEM,) * chips
+    )(mine, other)
+    received = [lax.ppermute(part, "row", move) for part, move in zip(sent, rounds)]
+    own = call(hidden_kernel, "hidden", one, [VMEM] * chips, VMEM)(own, *received)
+    received = [lax.ppermute(own, "row", move) for move in rounds]
+    mine = call(in_order_kernel, "in_order", terms, [VMEM] * chips, VMEM)(own, *received)
     theirs = lax.ppermute(mine, "row", pair)
     depth = BS // 2
     per = (3 * slots * depth - REST) // n_dp
@@ -259,8 +275,8 @@
     halved = call(pair_sum_kernel, "col_pair_sum", row_half, [VMEM] * 2, VMEM, flops=HIDE)(keep, given)
     same_parity = [list(range(p, n_col, 2)) for p in range(2)]
     row_terms = lax.all_to_all(halved, "col", 0, 0, axis_index_groups=same_parity)
+    from_prev = lax.ppermute(to_next, "dp", ahead)
     from_far = lax.ppermute(to_far, "dp", across)
-    from_prev = lax.ppermute(to_next, "dp", ahead)
     from_next = lax.ppermute(to_prev, "dp", behind)
     own, rest = call(
         dp_sum_kernel,
@@ -269,7 +285,7 @@
         [VMEM] * 4,
         (VMEM,) * 2,
         flops=HIDE,
-    )(own, from_far, from_prev, from_next)
+    )(own, from_prev, from_far, from_next)
     owned = lax.all_gather(own, "dp", axis=0)
     flat = arr(slots, BS * BS)
     block_grads = call(

time: 128 us -> 132 us (1.031)
  the two profiles are of different devices: /device:TPU:2 before, /device:TPU:1 now
where the time goes in v10:
time: 132 us; the launch traced here: 130 us
  starting transfers between devices  54.7 us (41%)
  blocking collectives  45.8 us (35%)
  waiting for transfers between devices  16.1 us (12%)
  Pallas kernels  10.4 us (8%)
    all_gather x1, blocking collectives, per_device(): wide = lax.all_gather(both, 'col', axis=0)  31.8 us
    all_gather x1, blocking collectives, per_device(): owned = lax.all_gather(own, 'dp', axis=0)  14 us
    ppermute x3, starting transfers between devices, per_device(): received = [lax.ppermute(own, 'row', move) for move in rounds]  10.9 us
    ppermute x3, starting transfers between devices, per_device(): lax.ppermute(part, 'row', move)  10.5 us
    ppermute x1, starting transfers between devices, per_device(): other = lax.ppermute(theirs, 'row', pair)  10.1 us
    all_to_all x1, starting transfers between devices, per_device(): lax.all_to_all(halved, 'col', 0, 0, axis_index_groups=same_parity)  7.02 us
    ppermute x3, waiting for transfers between devices, per_device(): received = [lax.ppermute(own, 'row', move) for move in rounds]  6.85 us
    ppermute x1, starting transfers between devices, per_device(): from_far = lax.ppermute(to_far, 'dp', across)  4.54 us
  transfers between devices with their start and end apart: 13, of which 8 were waited for; matrix products, arithmetic and copies ran while one was open for 0% of the time, Pallas kernels for 2%

profile of v10, /device:TPU:1, one launch (start us, length us, event | category | flops | bytes accessed | tf_op | source)
XLA Modules:
  0.0 129.6 jit_solution(16779012806588633591)
XLA Ops:
  0.6 0.7 pad_maximum_fusion
  1.4 31.8 %all-gather = bf16[256,1024]{1,0:T(8,128)(2,1)S(1)} all-gather(bf16[16,1024]{1,0:T(8,128)(2,1)S(1)} %pad_maximum_fusion), channel_id=2, replica_groups=mesh['dp'=4,'row'=8,'col'=16] {'col'}, dimensions={0}, use_global_device_ids=true | all-gather | bytes 557056 | tf_op jit(solution)/shard_map/all_gather | solution.py:232
  33.2 0.0 copy-start
  33.2 0.0 copy-start.1
  33.2 0.0 copy-start.2
  33.2 0.2 feature_major.1.cols
  33.4 0.0 copy-start.3
  33.4 0.0 copy-start.4
  33.4 0.8 copy-done
  34.2 0.1 copy-done.1
  34.3 0.1 copy-done.2
  34.4 0.0 copy-done.3
  34.4 0.0 copy-done.4
  34.4 2.9 %spread.1 = (bf16[4,3,224,128]{3,2,1,0:T(8,128)(2,1)S(1)}, bf16[4,3,224,128]{3,2,1,0:T(8,128)(2,1)S(1)}, bf16[44,64,64]{2,1,0:T(8,128)(2,1)S(1)}, bf16[44,64,64]{2,1,0:T(8,128)(2,1)S(1)}, bf16[44,64,64]{2,1,0:T(8,128)(2,1)S(1)}) custom-call(s32[3,2,44]{2,1,0:T(2,128)S(1)} %bitcast.15, s32[3]{0:T(128)S(1)} %bitcast.17, ...), custom_call_target="tpu_custom_call" | custom-call | tf_op jit(solution)/shard_map/spread/pallas_call | solution.py:235
  37.3 10.1 %collective-permute-start = (bf16[4,3,224,128]{3,2,1,0:T(8,128)(2,1)S(1)}, bf16[4,3,224,128]{3,2,1,0:T(8,128)(2,1)S(1)}, u32[]{:S(2)}, u32[]{:S(2)}) collective-permute-start(bf16[4,3,224,128]{3,2,1,0:T(8,128)(2,1)S(1)} %get-tuple-element.28), channel_id=1, source_target_pairs={{0,16},{16,0},{32,48},{48,32},{64,80},{80,64},{96,112},{112,96},{1... | collective-permute-start | bytes 2064392 | tf_op jit(solution)/shard_map/ppermute | solution.py:246
  47.5 1.7 %collective-permute-done.other = bf16[4,3,224,128]{3,2,1,0:T(8,128)(2,1)S(1)} collective-permute-done((bf16[4,3,224,128]{3,2,1,0:T(8,128)(2,1)S(1)}, bf16[4,3,224,128]{3,2,1,0:T(8,128)(2,1)S(1)}, u32[]{:S(2)}, u32[]{:S(2)}) %collective-permute-start) | collective-permute-done | bytes 688160 | tf_op jit(solution)/shard_map/ppermute | solution.py:246
  49.2 0.2 share_sum.1
  49.4 3.1 %collective-permute-start.1 = (bf16[3,224,128]{2,1,0:T(8,128)(2,1)S(1)}, bf16[3,224,128]{2,1,0:T(8,128)(2,1)S(1)}, u32[]{:S(2)}, u32[]{:S(2)}) collective-permute-start(bf16[3,224,128]{2,1,0:T(8,128)(2,1)S(1)} %get-tuple-element.30), channel_id=1, source_target_pairs={{0,32},{16,48},{32,64},{48,80},{64,96},{80,112},{96,0},{112,16},{1... | collective-permute-start | bytes 516104 | tf_op jit(solution)/shard_map/ppermute | solution.py:252
  52.5 4.4 %collective-permute-start.2 = (bf16[3,224,128]{2,1,0:T(8,128)(2,1)S(1)}, bf16[3,224,128]{2,1,0:T(8,128)(2,1)S(1)}, u32[]{:S(2)}, u32[]{:S(2)}) collective-permute-start(bf16[3,224,128]{2,1,0:T(8,128)(2,1)S(1)} %get-tuple-element.31), channel_id=1, source_target_pairs={{0,64},{16,80},{32,96},{48,112},{64,0},{80,16},{96,32},{112,48},{1... | collective-permute-start | bytes 516104 | tf_op jit(solution)/shard_map/ppermute | solution.py:252
  56.9 3.1 %collective-permute-start.3 = (bf16[3,224,128]{2,1,0:T(8,128)(2,1)S(1)}, bf16[3,224,128]{2,1,0:T(8,128)(2,1)S(1)}, u32[]{:S(2)}, u32[]{:S(2)}) collective-permute-start(bf16[3,224,128]{2,1,0:T(8,128)(2,1)S(1)} %get-tuple-element.32), channel_id=1, source_target_pairs={{0,96},{16,112},{32,0},{48,16},{64,32},{80,48},{96,64},{112,80},{1... | collective-permute-start | bytes 516104 | tf_op jit(solution)/shard_map/ppermute | solution.py:252
  60.0 0.0 collective-permute-done.1.others_and_out_0_
  60.0 2.8 %collective-permute-done.2.others_and_out_1_ = bf16[3,224,128]{2,1,0:T(8,128)(2,1)S(1)} collective-permute-done((bf16[3,224,128]{2,1,0:T(8,128)(2,1)S(1)}, bf16[3,224,128]{2,1,0:T(8,128)(2,1)S(1)}, u32[]{:S(2)}, u32[]{:S(2)}) %collective-permute-start.2) | collective-permute-done | bytes 172064 | tf_op jit(solution)/shard_map/ppermute | solution.py:252
  62.8 1.0 collective-permute-done.3.others_and_out_2_
  63.7 0.1 hidden.1.shares_and_out_0_
  63.9 4.3 %collective-permute-start.6 = (bf16[3,224,128]{2,1,0:T(8,128)(2,1)S(1)}, bf16[3,224,128]{2,1,0:T(8,128)(2,1)S(1)}, u32[]{:S(2)}, u32[]{:S(2)}) collective-permute-start(bf16[3,224,128]{2,1,0:T(8,128)(2,1)S(1)} %hidden.1.shares_and_out_0_), channel_id=1, source_target_pairs={{0,96},{16,112},{32,0},{48,16},{64,32},{80,48},{96,64},{112,80},{1... | collective-permute-start | bytes 516104 | tf_op jit(solution)/shard_map/ppermute | solution.py:254
  68.2 4.7 %collective-permute-start.5 = (bf16[3,224,128]{2,1,0:T(8,128)(2,1)S(1)}, bf16[3,224,128]{2,1,0:T(8,128)(2,1)S(1)}, u32[]{:S(2)}, u32[]{:S(2)}) collective-permute-start(bf16[3,224,128]{2,1,0:T(8,128)(2,1)S(1)} %hidden.1.shares_and_out_0_), channel_id=1, source_target_pairs={{0,64},{16,80},{32,96},{48,112},{64,0},{80,16},{96,32},{112,48},{1... | collective-permute-start | bytes 516104 | tf_op jit(solution)/shard_map/ppermute | solution.py:254
  72.9 1.9 %collective-permute-start.4 = (bf16[3,224,128]{2,1,0:T(8,128)(2,1)S(1)}, bf16[3,224,128]{2,1,0:T(8,128)(2,1)S(1)}, u32[]{:S(2)}, u32[]{:S(2)}) collective-permute-start(bf16[3,224,128]{2,1,0:T(8,128)(2,1)S(1)} %hidden.1.shares_and_out_0_), channel_id=1, source_target_pairs={{0,32},{16,48},{32,64},{48,80},{64,96},{80,112},{96,0},{112,16},{1... | collective-permute-start | bytes 516104 | tf_op jit(solution)/shard_map/ppermute | solution.py:254
  74.8 0.0 collective-permute-done.6.shares_and_out_3_
  74.8 1.0 collective-permute-done.5.shares_and_out_2_
  75.8 5.9 %collective-permute-done.4.shares_and_out_1_ = bf16[3,224,128]{2,1,0:T(8,128)(2,1)S(1)} collective-permute-done((bf16[3,224,128]{2,1,0:T(8,128)(2,1)S(1)}, bf16[3,224,128]{2,1,0:T(8,128)(2,1)S(1)}, u32[]{:S(2)}, u32[]{:S(2)}) %collective-permute-start.4) | collective-permute-done | bytes 172064 | tf_op jit(solution)/shard_map/ppermute | solution.py:254
  81.7 0.1 in_order.1.mine
  81.8 3.4 %collective-permute-start.7 = (bf16[4,3,224,128]{3,2,1,0:T(8,128)(2,1)S(1)}, bf16[4,3,224,128]{3,2,1,0:T(8,128)(2,1)S(1)}, u32[]{:S(2)}, u32[]{:S(2)}) collective-permute-start(bf16[4,3,224,128]{3,2,1,0:T(8,128)(2,1)S(1)} %in_order.1.mine), channel_id=1, source_target_pairs={{0,16},{16,0},{32,48},{48,32},{64,80},{80,64},{96,112},{112,96},{1... | collective-permute-start | bytes 2064392 | tf_op jit(solution)/shard_map/ppermute | solution.py:256
  85.2 1.7 %collective-permute-done.7.theirs = bf16[4,3,224,128]{3,2,1,0:T(8,128)(2,1)S(1)} collective-permute-done((bf16[4,3,224,128]{3,2,1,0:T(8,128)(2,1)S(1)}, bf16[4,3,224,128]{3,2,1,0:T(8,128)(2,1)S(1)}, u32[]{:S(2)}, u32[]{:S(2)}) %collective-permute-start.7) | collective-permute-done | bytes 688160 | tf_op jit(solution)/shard_map/ppermute | solution.py:256
  87.0 3.8 %back.1 = (bf16[8,16,1024]{2,1,0:T(8,128)(2,1)S(1)}, bf16[8,16,1024]{2,1,0:T(8,128)(2,1)S(1)}, bf16[1200,128]{1,0:T(8,128)(2,1)S(1)}, bf16[1200,128]{1,0:T(8,128...) custom-call(s32[3,2,44]{2,1,0:T(2,128)S(1)} %bitcast.16, s32[3]{0:T(128)S(1)} %bitcast.18, ...), custom_call_target="tpu_custom_call" | custom-call | tf_op jit(solution)/shard_map/back/pallas_call | solution.py:261
  90.8 1.9 %collective-permute-start.8 = (bf16[8,16,1024]{2,1,0:T(8,128)(2,1)S(1)}, bf16[8,16,1024]{2,1,0:T(8,128)(2,1)S(1)}, u32[]{:S(2)}, u32[]{:S(2)}) collective-permute-start(bf16[8,16,1024]{2,1,0:T(8,128)(2,1)S(1)} %get-tuple-element.37), channel_id=1, source_target_pairs={{0,1},{1,0},{2,3},{3,2},{4,5},{5,4},{6,7},{7,6},{8,9},{9,8},{10,11... | collective-permute-start | bytes 786440 | tf_op jit(solution)/shard_map/ppermute | solution.py:274
  92.7 3.2 %collective-permute-start.9 = (bf16[1200,128]{1,0:T(8,128)(2,1)S(1)}, bf16[1200,128]{1,0:T(8,128)(2,1)S(1)}, u32[]{:S(2)}, u32[]{:S(2)}) collective-permute-start(bf16[1200,128]{1,0:T(8,128)(2,1)S(1)} %get-tuple-element.41), channel_id=1, source_target_pairs={{0,128},{128,256},{256,384},{384,0},{1,129},{129,257},{257,385},{3... | collective-permute-start | bytes 921608 | tf_op jit(solution)/shard_map/ppermute | solution.py:278
  95.9 4.5 %collective-permute-start.10 = (bf16[1200,128]{1,0:T(8,128)(2,1)S(1)}, bf16[1200,128]{1,0:T(8,128)(2,1)S(1)}, u32[]{:S(2)}, u32[]{:S(2)}) collective-permute-start(bf16[1200,128]{1,0:T(8,128)(2,1)S(1)} %get-tuple-element.42), channel_id=1, source_target_pairs={{0,256},{128,384},{256,0},{384,128},{1,257},{129,385},{257,1},{385... | collective-permute-start | bytes 921608 | tf_op jit(solution)/shard_map/ppermute | solution.py:279
  100.4 3.0 %collective-permute-start.11 = (bf16[1200,128]{1,0:T(8,128)(2,1)S(1)}, bf16[1200,128]{1,0:T(8,128)(2,1)S(1)}, u32[]{:S(2)}, u32[]{:S(2)}) collective-permute-start(bf16[1200,128]{1,0:T(8,128)(2,1)S(1)} %get-tuple-element.43), channel_id=1, source_target_pairs={{0,384},{128,0},{256,128},{384,256},{1,385},{129,1},{257,129},{385... | collective-permute-start | bytes 921608 | tf_op jit(solution)/shard_map/ppermute | solution.py:280
  103.4 0.0 collective-permute-done.8.other
  103.4 0.8 col_pair_sum.1
  104.2 7.0 %all-to-all-start = ((bf16[8,16,1024]{2,1,0:T(8,128)(2,1)}), bf16[8,16,1024]{2,1,0:T(8,128)(2,1)S(1)}, u32[]{:S(2)}, u32[]{:S(2)}) async-start(bf16[8,16,1024]{2,1,0:T(8,128)(2,1)} %col_pair_sum.1), calls=%async_computation | async-start | bytes 524288 | tf_op jit(solution)/shard_map/all_to_all | solution.py:277
  111.2 0.0 collective-permute-done.9.prev
  111.2 0.9 collective-permute-done.10.far
  112.1 1.1 collective-permute-done.11.next_
  113.2 0.2 dp_sum.1
  113.4 14.0 %all-gather.1 = bf16[4032,128]{1,0:T(8,128)(2,1)S(1)} all-gather(bf16[1008,128]{1,0:T(8,128)(2,1)S(1)} %get-tuple-element.44), channel_id=3, replica_groups=mesh['dp'=4,'row'=8,'col'=16] {'dp'}, dimensions={0}, use_global_device_ids=true | all-gather | bytes 1290240 | tf_op jit(solution)/shard_map/all_gather | solution.py:289
  127.4 1.5 %unpack.1 = (bf16[44,4096]{1,0:T(8,128)(2,1)}, bf16[44,4096]{1,0:T(8,128)(2,1)}, bf16[44,4096]{1,0:T(8,128)(2,1)}) custom-call(bf16[4,1008,128]{2,1,0:T(8,128)(2,1)S(1)} %bitcast.10, bf16[192,128]{1,0:T(8,128)(2,1)S(1)} %get-tuple-element.45.rest), custom_call_target="tpu_custom_call" | custom-call | tf_op jit(solution)/shard_map/unpack/pallas_call | solution.py:291
  128.9 0.0 all-to-all-done.terms
  128.9 0.7 row_sum.1
Async XLA Ops:
  33.2 1.0 copy-start
  33.2 1.1 copy-start.1
  33.2 1.2 copy-start.2
  33.4 1.0 copy-start.3
  33.4 1.0 copy-start.4
  37.3 11.9 %collective-permute-start = (bf16[4,3,224,128]{3,2,1,0:T(8,128)(2,1)S(1)}, bf16[4,3,224,128]{3,2,1,0:T(8,128)(2,1)S(1)}, u32[]{:S(2)}, u32[]{:S(2)}) collective-permute-start(bf16[4,3,224,128]{3,2,1,0:T(8,128)(2,1)S(1)} %get-tuple-element.28), channel_id=1, source_target_pairs={{0,16},{16,0},{32,48},{48,32},{64,80},{80,64},{96,112},{112,96},{1... | collective-permute-start | bytes 2064392 | tf_op jit(solution)/shard_map/ppermute | solution.py:246
  49.4 10.6 %collective-permute-start.1 = (bf16[3,224,128]{2,1,0:T(8,128)(2,1)S(1)}, bf16[3,224,128]{2,1,0:T(8,128)(2,1)S(1)}, u32[]{:S(2)}, u32[]{:S(2)}) collective-permute-start(bf16[3,224,128]{2,1,0:T(8,128)(2,1)S(1)} %get-tuple-element.30), channel_id=1, source_target_pairs={{0,32},{16,48},{32,64},{48,80},{64,96},{80,112},{96,0},{112,16},{1... | collective-permute-start | bytes 516104 | tf_op jit(solution)/shard_map/ppermute | solution.py:252
  52.5 10.2 %collective-permute-start.2 = (bf16[3,224,128]{2,1,0:T(8,128)(2,1)S(1)}, bf16[3,224,128]{2,1,0:T(8,128)(2,1)S(1)}, u32[]{:S(2)}, u32[]{:S(2)}) collective-permute-start(bf16[3,224,128]{2,1,0:T(8,128)(2,1)S(1)} %get-tuple-element.31), channel_id=1, source_target_pairs={{0,64},{16,80},{32,96},{48,112},{64,0},{80,16},{96,32},{112,48},{1... | collective-permute-start | bytes 516104 | tf_op jit(solution)/shard_map/ppermute | solution.py:252
  56.9 6.8 %collective-permute-start.3 = (bf16[3,224,128]{2,1,0:T(8,128)(2,1)S(1)}, bf16[3,224,128]{2,1,0:T(8,128)(2,1)S(1)}, u32[]{:S(2)}, u32[]{:S(2)}) collective-permute-start(bf16[3,224,128]{2,1,0:T(8,128)(2,1)S(1)} %get-tuple-element.32), channel_id=1, source_target_pairs={{0,96},{16,112},{32,0},{48,16},{64,32},{80,48},{96,64},{112,80},{1... | collective-permute-start | bytes 516104 | tf_op jit(solution)/shard_map/ppermute | solution.py:252
  63.9 10.9 %collective-permute-start.6 = (bf16[3,224,128]{2,1,0:T(8,128)(2,1)S(1)}, bf16[3,224,128]{2,1,0:T(8,128)(2,1)S(1)}, u32[]{:S(2)}, u32[]{:S(2)}) collective-permute-start(bf16[3,224,128]{2,1,0:T(8,128)(2,1)S(1)} %hidden.1.shares_and_out_0_), channel_id=1, source_target_pairs={{0,96},{16,112},{32,0},{48,16},{64,32},{80,48},{96,64},{112,80},{1... | collective-permute-start | bytes 516104 | tf_op jit(solution)/shard_map/ppermute | solution.py:254
  68.2 7.7 %collective-permute-start.5 = (bf16[3,224,128]{2,1,0:T(8,128)(2,1)S(1)}, bf16[3,224,128]{2,1,0:T(8,128)(2,1)S(1)}, u32[]{:S(2)}, u32[]{:S(2)}) collective-permute-start(bf16[3,224,128]{2,1,0:T(8,128)(2,1)S(1)} %hidden.1.shares_and_out_0_), channel_id=1, source_target_pairs={{0,64},{16,80},{32,96},{48,112},{64,0},{80,16},{96,32},{112,48},{1... | collective-permute-start | bytes 516104 | tf_op jit(solution)/shard_map/ppermute | solution.py:254
  72.9 8.8 %collective-permute-start.4 = (bf16[3,224,128]{2,1,0:T(8,128)(2,1)S(1)}, bf16[3,224,128]{2,1,0:T(8,128)(2,1)S(1)}, u32[]{:S(2)}, u32[]{:S(2)}) collective-permute-start(bf16[3,224,128]{2,1,0:T(8,128)(2,1)S(1)} %hidden.1.shares_and_out_0_), channel_id=1, source_target_pairs={{0,32},{16,48},{32,64},{48,80},{64,96},{80,112},{96,0},{112,16},{1... | collective-permute-start | bytes 516104 | tf_op jit(solution)/shard_map/ppermute | solution.py:254
  81.8 5.2 %collective-permute-start.7 = (bf16[4,3,224,128]{3,2,1,0:T(8,128)(2,1)S(1)}, bf16[4,3,224,128]{3,2,1,0:T(8,128)(2,1)S(1)}, u32[]{:S(2)}, u32[]{:S(2)}) collective-permute-start(bf16[4,3,224,128]{3,2,1,0:T(8,128)(2,1)S(1)} %in_order.1.mine), channel_id=1, source_target_pairs={{0,16},{16,0},{32,48},{48,32},{64,80},{80,64},{96,112},{112,96},{1... | collective-permute-start | bytes 2064392 | tf_op jit(solution)/shard_map/ppermute | solution.py:256
  90.8 12.7 %collective-permute-start.8 = (bf16[8,16,1024]{2,1,0:T(8,128)(2,1)S(1)}, bf16[8,16,1024]{2,1,0:T(8,128)(2,1)S(1)}, u32[]{:S(2)}, u32[]{:S(2)}) collective-permute-start(bf16[8,16,1024]{2,1,0:T(8,128)(2,1)S(1)} %get-tuple-element.37), channel_id=1, source_target_pairs={{0,1},{1,0},{2,3},{3,2},{4,5},{5,4},{6,7},{7,6},{8,9},{9,8},{10,11... | collective-permute-start | bytes 786440 | tf_op jit(solution)/shard_map/ppermute | solution.py:274
  92.7 18.5 %collective-permute-start.9 = (bf16[1200,128]{1,0:T(8,128)(2,1)S(1)}, bf16[1200,128]{1,0:T(8,128)(2,1)S(1)}, u32[]{:S(2)}, u32[]{:S(2)}) collective-permute-start(bf16[1200,128]{1,0:T(8,128)(2,1)S(1)} %get-tuple-element.41), channel_id=1, source_target_pairs={{0,128},{128,256},{256,384},{384,0},{1,129},{129,257},{257,385},{3... | collective-permute-start | bytes 921608 | tf_op jit(solution)/shard_map/ppermute | solution.py:278
  95.9 16.2 %collective-permute-start.10 = (bf16[1200,128]{1,0:T(8,128)(2,1)S(1)}, bf16[1200,128]{1,0:T(8,128)(2,1)S(1)}, u32[]{:S(2)}, u32[]{:S(2)}) collective-permute-start(bf16[1200,128]{1,0:T(8,128)(2,1)S(1)} %get-tuple-element.42), channel_id=1, source_target_pairs={{0,256},{128,384},{256,0},{384,128},{1,257},{129,385},{257,1},{385... | collective-permute-start | bytes 921608 | tf_op jit(solution)/shard_map/ppermute | solution.py:279
  100.4 12.8 %collective-permute-start.11 = (bf16[1200,128]{1,0:T(8,128)(2,1)S(1)}, bf16[1200,128]{1,0:T(8,128)(2,1)S(1)}, u32[]{:S(2)}, u32[]{:S(2)}) collective-permute-start(bf16[1200,128]{1,0:T(8,128)(2,1)S(1)} %get-tuple-element.43), channel_id=1, source_target_pairs={{0,384},{128,0},{256,128},{384,256},{1,385},{129,1},{257,129},{385... | collective-permute-start | bytes 921608 | tf_op jit(solution)/shard_map/ppermute | solution.py:280
  104.2 24.7 %all-to-all-start = ((bf16[8,16,1024]{2,1,0:T(8,128)(2,1)}), bf16[8,16,1024]{2,1,0:T(8,128)(2,1)S(1)}, u32[]{:S(2)}, u32[]{:S(2)}) async-start(bf16[8,16,1024]{2,1,0:T(8,128)(2,1)} %col_pair_sum.1), calls=%async_computation | async-start | bytes 524288 | tf_op jit(solution)/shard_map/all_to_all | solution.py:277

commit v11 on v9

--- a/solution.py
+++ b/solution.py
@@ -7,6 +7,7 @@
 
 BS = 64
 REST = 192
+SPARE = 5
 HIDE = 10**10
 VMEM = pl.BlockSpec(memory_space=pltpu.VMEM)
 SMEM = pl.BlockSpec(memory_space=pltpu.SMEM)
@@ -141,7 +142,7 @@
         out[per:, :] = grads[n_dp * per :, :]
 
 
-def dp_sum_kernel(here, far, prev, next_, own, rest):
+def dp_sum_kernel(here, prev, far, next_, own, rest):
     total = (here[...].astype(F32) + far[...].astype(F32)) + (
         prev[...].astype(F32) + next_[...].astype(F32)
     )
@@ -229,7 +230,7 @@
         (VMEM,) * 5,
         [
             pltpu.VMEM((3, units, toks), F32),
-            pltpu.VMEM((slots * (BS + 1), 2 * BS), F32),
+            pltpu.VMEM(((slots + SPARE) * (BS + 1), 2 * BS), F32),
         ],
     )(index, count, cols, *flat_blocks)
     other = lax.ppermute(theirs, "row", pair)
@@ -269,7 +270,7 @@
         [VMEM] * 4,
         (VMEM,) * 2,
         flops=HIDE,
-    )(own, from_far, from_prev, from_next)
+    )(own, from_prev, from_far, from_next)
     owned = lax.all_gather(own, "dp", axis=0)
     flat = arr(slots, BS * BS)
     block_grads = call(
@@ -278,7 +279,7 @@
         (flat, flat, flat),
         [VMEM] * 2,
         (VMEM,) * 3,
-        [pltpu.VMEM((3 * slots * (depth + 1), 2 * BS), F32)],
+        [pltpu.VMEM(((3 * slots + SPARE) * (depth + 1), 2 * BS), F32)],
     )(owned, rest)
     result = arr(half, width)
     mixed, tokens_grad = call(row_sum_kernel, "row_sum", (result, result), [VMEM], (VMEM, VMEM))(

time: 128 us -> 127 us (level)
  the two profiles are of different devices: /device:TPU:2 before, /device:TPU:1 now
where the time goes in v11:
time: 127 us; the launch traced here: 125 us
  blocking collectives  72.1 us (57%)
  starting transfers between devices  34.4 us (27%)
  Pallas kernels  10.3 us (8%)
  waiting for transfers between devices  5.48 us (4%)
    all_gather x1, blocking collectives, per_device(): wide = lax.all_gather(both, 'col', axis=0)  31.8 us
    all_to_all x1, blocking collectives, per_device(): summed = lax.all_to_all(paired, 'row', 0, 0, axis_index_groups=same_core)  14.5 us
    all_gather x1, blocking collectives, per_device(): owned = lax.all_gather(own, 'dp', axis=0)  14 us
    all_to_all x1, blocking collectives, per_device(): mine = lax.all_to_all(own, 'row', 0, 0, axis_index_groups=same_core)  11.8 us
    ppermute x1, starting transfers between devices, per_device(): other = lax.ppermute(theirs, 'row', pair)  10.1 us
    all_to_all x1, starting transfers between devices, per_device(): lax.all_to_all(halved, 'col', 0, 0, axis_index_groups=same_parity)  7.04 us
    ppermute x1, starting transfers between devices, per_device(): theirs = lax.ppermute(mine, 'row', pair)  4.63 us
    ppermute x1, starting transfers between devices, per_device(): from_far = lax.ppermute(to_far, 'dp', across)  4.54 us
  transfers between devices with their start and end apart: 7, of which 4 were waited for; matrix products, arithmetic and copies ran while one was open for 0% of the time, Pallas kernels for 2%

profile of v11, /device:TPU:1, one launch (start us, length us, event | category | flops | bytes accessed | tf_op | source)
XLA Modules:
  0.0 124.8 jit_solution(15836865597882394482)
XLA Ops:
  0.6 0.7 pad_maximum_fusion
  1.4 31.8 %all-gather = bf16[256,1024]{1,0:T(8,128)(2,1)S(1)} all-gather(bf16[16,1024]{1,0:T(8,128)(2,1)S(1)} %pad_maximum_fusion), channel_id=2, replica_groups=mesh['dp'=4,'row'=8,'col'=16] {'col'}, dimensions={0}, use_global_device_ids=true | all-gather | bytes 557056 | tf_op jit(solution)/shard_map/all_gather | solution.py:222
  33.2 0.0 copy-start
  33.2 0.0 copy-start.1
  33.2 0.0 copy-start.2
  33.2 0.2 feature_major.1.cols
  33.4 0.0 copy-start.3
  33.4 0.0 copy-start.4
  33.4 0.8 copy-done
  34.2 0.1 copy-done.1
  34.3 0.1 copy-done.2
  34.4 0.0 copy-done.3
  34.4 0.0 copy-done.4
  34.4 2.9 %spread.1 = (bf16[4,3,224,128]{3,2,1,0:T(8,128)(2,1)S(1)}, bf16[4,3,224,128]{3,2,1,0:T(8,128)(2,1)S(1)}, bf16[44,64,64]{2,1,0:T(8,128)(2,1)S(1)}, bf16[44,64,64]{2,1,0:T(8,128)(2,1)S(1)}, bf16[44,64,64]{2,1,0:T(8,128)(2,1)S(1)}) custom-call(s32[3,2,44]{2,1,0:T(2,128)S(1)} %bitcast.15, s32[3]{0:T(128)S(1)} %bitcast.17, ...), custom_call_target="tpu_custom_call" | custom-call | tf_op jit(solution)/shard_map/spread/pallas_call | solution.py:225
  37.3 10.1 %collective-permute-start = (bf16[4,3,224,128]{3,2,1,0:T(8,128)(2,1)S(1)}, bf16[4,3,224,128]{3,2,1,0:T(8,128)(2,1)S(1)}, u32[]{:S(2)}, u32[]{:S(2)}) collective-permute-start(bf16[4,3,224,128]{3,2,1,0:T(8,128)(2,1)S(1)} %get-tuple-element.24), channel_id=1, source_target_pairs={{0,16},{16,0},{32,48},{48,32},{64,80},{80,64},{96,112},{112,96},{1... | collective-permute-start | bytes 2064392 | tf_op jit(solution)/shard_map/ppermute | solution.py:236
  47.5 1.7 %collective-permute-done.other = bf16[4,3,224,128]{3,2,1,0:T(8,128)(2,1)S(1)} collective-permute-done((bf16[4,3,224,128]{3,2,1,0:T(8,128)(2,1)S(1)}, bf16[4,3,224,128]{3,2,1,0:T(8,128)(2,1)S(1)}, u32[]{:S(2)}, u32[]{:S(2)}) %collective-permute-start) | collective-permute-done | bytes 688160 | tf_op jit(solution)/shard_map/ppermute | solution.py:236
  49.2 0.2 pair_sum.1
  49.4 14.5 %all_to_all.15.terms = bf16[4,3,224,128]{3,2,1,0:T(8,128)(2,1)S(1)} all-to-all(bf16[4,3,224,128]{3,2,1,0:T(8,128)(2,1)S(1)} %pair_sum.1), channel_id=1, replica_groups={{0,32,64,96},{16,48,80,112},{1,33,65,97},{17,49,81,113},{2,34,66,98},{1..., dimensions={0} | all-to-all | bytes 1376256 | tf_op jit(solution)/shard_map/all_to_all | solution.py:238
  63.9 0.1 hidden.1
  64.0 11.8 %all_to_all.16.mine = bf16[4,3,224,128]{3,2,1,0:T(8,128)(2,1)S(1)} all-to-all(bf16[4,3,224,128]{3,2,1,0:T(8,128)(2,1)S(1)} %hidden.1), channel_id=1, replica_groups={{0,32,64,96},{16,48,80,112},{1,33,65,97},{17,49,81,113},{2,34,66,98},{1..., dimensions={0} | all-to-all | bytes 1376256 | tf_op jit(solution)/shard_map/all_to_all | solution.py:240
  75.9 4.6 %collective-permute-start.1 = (bf16[4,3,224,128]{3,2,1,0:T(8,128)(2,1)S(1)}, bf16[4,3,224,128]{3,2,1,0:T(8,128)(2,1)S(1)}, u32[]{:S(2)}, u32[]{:S(2)}) collective-permute-start(bf16[4,3,224,128]{3,2,1,0:T(8,128)(2,1)S(1)} %all_to_all.16.mine), channel_id=1, source_target_pairs={{0,16},{16,0},{32,48},{48,32},{64,80},{80,64},{96,112},{112,96},{1... | collective-permute-start | bytes 2064392 | tf_op jit(solution)/shard_map/ppermute | solution.py:241
  80.5 1.7 %collective-permute-done.1.theirs = bf16[4,3,224,128]{3,2,1,0:T(8,128)(2,1)S(1)} collective-permute-done((bf16[4,3,224,128]{3,2,1,0:T(8,128)(2,1)S(1)}, bf16[4,3,224,128]{3,2,1,0:T(8,128)(2,1)S(1)}, u32[]{:S(2)}, u32[]{:S(2)}) %collective-permute-start.1) | collective-permute-done | bytes 688160 | tf_op jit(solution)/shard_map/ppermute | solution.py:241
  82.3 3.8 %back.1 = (bf16[8,16,1024]{2,1,0:T(8,128)(2,1)S(1)}, bf16[8,16,1024]{2,1,0:T(8,128)(2,1)S(1)}, bf16[1200,128]{1,0:T(8,128)(2,1)S(1)}, bf16[1200,128]{1,0:T(8,128...) custom-call(s32[3,2,44]{2,1,0:T(2,128)S(1)} %bitcast.16, s32[3]{0:T(128)S(1)} %bitcast.18, ...), custom_call_target="tpu_custom_call" | custom-call | tf_op jit(solution)/shard_map/back/pallas_call | solution.py:246
  86.0 1.9 %collective-permute-start.2 = (bf16[8,16,1024]{2,1,0:T(8,128)(2,1)S(1)}, bf16[8,16,1024]{2,1,0:T(8,128)(2,1)S(1)}, u32[]{:S(2)}, u32[]{:S(2)}) collective-permute-start(bf16[8,16,1024]{2,1,0:T(8,128)(2,1)S(1)} %get-tuple-element.29), channel_id=1, source_target_pairs={{0,1},{1,0},{2,3},{3,2},{4,5},{5,4},{6,7},{7,6},{8,9},{9,8},{10,11... | collective-permute-start | bytes 786440 | tf_op jit(solution)/shard_map/ppermute | solution.py:259
  88.0 3.2 %collective-permute-start.3 = (bf16[1200,128]{1,0:T(8,128)(2,1)S(1)}, bf16[1200,128]{1,0:T(8,128)(2,1)S(1)}, u32[]{:S(2)}, u32[]{:S(2)}) collective-permute-start(bf16[1200,128]{1,0:T(8,128)(2,1)S(1)} %get-tuple-element.33), channel_id=1, source_target_pairs={{0,128},{128,256},{256,384},{384,0},{1,129},{129,257},{257,385},{3... | collective-permute-start | bytes 921608 | tf_op jit(solution)/shard_map/ppermute | solution.py:264
  91.2 4.5 %collective-permute-start.4 = (bf16[1200,128]{1,0:T(8,128)(2,1)S(1)}, bf16[1200,128]{1,0:T(8,128)(2,1)S(1)}, u32[]{:S(2)}, u32[]{:S(2)}) collective-permute-start(bf16[1200,128]{1,0:T(8,128)(2,1)S(1)} %get-tuple-element.34), channel_id=1, source_target_pairs={{0,256},{128,384},{256,0},{384,128},{1,257},{129,385},{257,1},{385... | collective-permute-start | bytes 921608 | tf_op jit(solution)/shard_map/ppermute | solution.py:263
  95.7 3.0 %collective-permute-start.5 = (bf16[1200,128]{1,0:T(8,128)(2,1)S(1)}, bf16[1200,128]{1,0:T(8,128)(2,1)S(1)}, u32[]{:S(2)}, u32[]{:S(2)}) collective-permute-start(bf16[1200,128]{1,0:T(8,128)(2,1)S(1)} %get-tuple-element.35), channel_id=1, source_target_pairs={{0,384},{128,0},{256,128},{384,256},{1,385},{129,1},{257,129},{385... | collective-permute-start | bytes 921608 | tf_op jit(solution)/shard_map/ppermute | solution.py:265
  98.7 0.0 collective-permute-done.2.other
  98.7 0.8 col_pair_sum.1
  99.5 7.0 %all-to-all-start.2 = ((bf16[8,16,1024]{2,1,0:T(8,128)(2,1)}), bf16[8,16,1024]{2,1,0:T(8,128)(2,1)S(1)}, u32[]{:S(2)}, u32[]{:S(2)}) async-start(bf16[8,16,1024]{2,1,0:T(8,128)(2,1)} %col_pair_sum.1), calls=%async_computation.2 | async-start | bytes 524288 | tf_op jit(solution)/shard_map/all_to_all | solution.py:262
  106.5 0.0 collective-permute-done.3.prev
  106.5 0.9 collective-permute-done.4.far
  107.4 1.1 collective-permute-done.5.next_
  108.5 0.2 dp_sum.1
  108.6 14.0 %all-gather.1 = bf16[4032,128]{1,0:T(8,128)(2,1)S(1)} all-gather(bf16[1008,128]{1,0:T(8,128)(2,1)S(1)} %get-tuple-element.36), channel_id=3, replica_groups=mesh['dp'=4,'row'=8,'col'=16] {'dp'}, dimensions={0}, use_global_device_ids=true | all-gather | bytes 1290240 | tf_op jit(solution)/shard_map/all_gather | solution.py:274
  122.7 1.5 %unpack.1 = (bf16[44,4096]{1,0:T(8,128)(2,1)}, bf16[44,4096]{1,0:T(8,128)(2,1)}, bf16[44,4096]{1,0:T(8,128)(2,1)}) custom-call(bf16[4,1008,128]{2,1,0:T(8,128)(2,1)S(1)} %bitcast.10, bf16[192,128]{1,0:T(8,128)(2,1)S(1)} %get-tuple-element.37.rest), custom_call_target="tpu_custom_call" | custom-call | tf_op jit(solution)/shard_map/unpack/pallas_call | solution.py:276
  124.2 0.0 all-to-all-done.2.terms
  124.2 0.7 row_sum.1
Async XLA Ops:
  33.2 1.0 copy-start
  33.2 1.1 copy-start.1
  33.2 1.2 copy-start.2
  33.4 1.0 copy-start.3
  33.4 1.0 copy-start.4
  37.3 11.9 %collective-permute-start = (bf16[4,3,224,128]{3,2,1,0:T(8,128)(2,1)S(1)}, bf16[4,3,224,128]{3,2,1,0:T(8,128)(2,1)S(1)}, u32[]{:S(2)}, u32[]{:S(2)}) collective-permute-start(bf16[4,3,224,128]{3,2,1,0:T(8,128)(2,1)S(1)} %get-tuple-element.24), channel_id=1, source_target_pairs={{0,16},{16,0},{32,48},{48,32},{64,80},{80,64},{96,112},{112,96},{1... | collective-permute-start | bytes 2064392 | tf_op jit(solution)/shard_map/ppermute | solution.py:236
  75.9 6.4 %collective-permute-start.1 = (bf16[4,3,224,128]{3,2,1,0:T(8,128)(2,1)S(1)}, bf16[4,3,224,128]{3,2,1,0:T(8,128)(2,1)S(1)}, u32[]{:S(2)}, u32[]{:S(2)}) collective-permute-start(bf16[4,3,224,128]{3,2,1,0:T(8,128)(2,1)S(1)} %all_to_all.16.mine), channel_id=1, source_target_pairs={{0,16},{16,0},{32,48},{48,32},{64,80},{80,64},{96,112},{112,96},{1... | collective-permute-start | bytes 2064392 | tf_op jit(solution)/shard_map/ppermute | solution.py:241
  86.0 12.7 %collective-permute-start.2 = (bf16[8,16,1024]{2,1,0:T(8,128)(2,1)S(1)}, bf16[8,16,1024]{2,1,0:T(8,128)(2,1)S(1)}, u32[]{:S(2)}, u32[]{:S(2)}) collective-permute-start(bf16[8,16,1024]{2,1,0:T(8,128)(2,1)S(1)} %get-tuple-element.29), channel_id=1, source_target_pairs={{0,1},{1,0},{2,3},{3,2},{4,5},{5,4},{6,7},{7,6},{8,9},{9,8},{10,11... | collective-permute-start | bytes 786440 | tf_op jit(solution)/shard_map/ppermute | solution.py:259
  88.0 18.5 %collective-permute-start.3 = (bf16[1200,128]{1,0:T(8,128)(2,1)S(1)}, bf16[1200,128]{1,0:T(8,128)(2,1)S(1)}, u32[]{:S(2)}, u32[]{:S(2)}) collective-permute-start(bf16[1200,128]{1,0:T(8,128)(2,1)S(1)} %get-tuple-element.33), channel_id=1, source_target_pairs={{0,128},{128,256},{256,384},{384,0},{1,129},{129,257},{257,385},{3... | collective-permute-start | bytes 921608 | tf_op jit(solution)/shard_map/ppermute | solution.py:264
  91.2 16.2 %collective-permute-start.4 = (bf16[1200,128]{1,0:T(8,128)(2,1)S(1)}, bf16[1200,128]{1,0:T(8,128)(2,1)S(1)}, u32[]{:S(2)}, u32[]{:S(2)}) collective-permute-start(bf16[1200,128]{1,0:T(8,128)(2,1)S(1)} %get-tuple-element.34), channel_id=1, source_target_pairs={{0,256},{128,384},{256,0},{384,128},{1,257},{129,385},{257,1},{385... | collective-permute-start | bytes 921608 | tf_op jit(solution)/shard_map/ppermute | solution.py:263
  95.7 12.8 %collective-permute-start.5 = (bf16[1200,128]{1,0:T(8,128)(2,1)S(1)}, bf16[1200,128]{1,0:T(8,128)(2,1)S(1)}, u32[]{:S(2)}, u32[]{:S(2)}) collective-permute-start(bf16[1200,128]{1,0:T(8,128)(2,1)S(1)} %get-tuple-element.35), channel_id=1, source_target_pairs={{0,384},{128,0},{256,128},{384,256},{1,385},{129,1},{257,129},{385... | collective-permute-start | bytes 921608 | tf_op jit(solution)/shard_map/ppermute | solution.py:265
  99.5 24.7 %all-to-all-start.2 = ((bf16[8,16,1024]{2,1,0:T(8,128)(2,1)}), bf16[8,16,1024]{2,1,0:T(8,128)(2,1)S(1)}, u32[]{:S(2)}, u32[]{:S(2)}) async-start(bf16[8,16,1024]{2,1,0:T(8,128)(2,1)} %col_pair_sum.1), calls=%async_computation.2 | async-start | bytes 524288 | tf_op jit(solution)/shard_map/all_to_all | solution.py:262
